TPU v7x, 128 devices: a whole 4x4x4 slice. The times are simulated.
128 devices in a mesh: row: 16 (over y, x_lo, core), col: 8 (over z, x_hi).
Axes of the slice: x: 4 (x_hi: 2, x_lo: 2; x = x_hi * 2 + x_lo), y: 4, z: 4, core: 2. Of those that a mesh axis runs over, the one named last changes fastest.
Arguments:
- grad: float32 [4096, 6144], P('row', 'col'), may hold values from -6 to 6
- weight: float32 [4096, 6144], P('row', 'col'), may hold values from -6 to 6
- exp_avg: float32 [4096, 6144], P('row', 'col'), may hold values from -2 to 2
- exp_avg_sq: float32 [4096, 6144], P('row', 'col'), may hold values from 0.05 to 3
- left_basis: bfloat16 [4096, 4096], P('row', 'col'), may hold values from -0.125 to 0.125
- right_basis: bfloat16 [6144, 6144], P('col', 'row'), may hold values from -0.109375 to 0.109375
Outputs:
- new_weight: float32 [4096, 6144], P('row', 'col')
- new_avg: float32 [4096, 6144], P('row', 'col')
- new_avg_sq: float32 [4096, 6144], P('row', 'col')
All inputs are finite; a program needn't handle non-finite values.
Results may differ from a plain program's by a relative error of at most 0.014.
Values may be sent and summed in bfloat16 or wider, within the bound.
No kernel may reach another device: no remote copies, remote signals or barrier semaphores. Data moves between devices by JAX's collectives and lax.ppermute only.
A program may use at most 64 MiB of HBM per device.

v0:
```python
import jax
import jax.numpy as jnp
from jax import lax
from jax.sharding import PartitionSpec as P

first_beta = 0.9
second_beta = 0.95
first_bias = 1.0 - 0.9**20
second_bias = 1.0 - 0.95**20
epsilon = 1e-08
learn_rate = 0.2
weight_decay = 0.1


def inner_rows(left, right):
    return lax.dot_general(
        left, right, (((0,), (0,)), ((), ())), preferred_element_type=jnp.float32
    )


def inner_cols(left, right):
    return lax.dot_general(
        left, right, (((1,), (1,)), ((), ())), preferred_element_type=jnp.float32
    )


def on_device(grad, weight, exp_avg, exp_avg_sq, left_basis, right_basis):
    grad_low = grad.astype(jnp.bfloat16)
    left_term = inner_rows(lax.all_gather(left_basis, "col", axis=1, tiled=True), grad_low)
    rotated_left = lax.psum_scatter(
        left_term.astype(jnp.bfloat16), "row", scatter_dimension=0, tiled=True
    )
    right_term = jnp.dot(
        rotated_left,
        lax.all_gather(right_basis, "row", axis=1, tiled=True),
        preferred_element_type=jnp.float32,
    )
    rotated = lax.psum_scatter(
        right_term.astype(jnp.bfloat16), "col", scatter_dimension=1, tiled=True
    ).astype(jnp.float32)
    new_avg = first_beta * exp_avg + (1.0 - first_beta) * rotated
    new_avg_sq = second_beta * exp_avg_sq + (1.0 - second_beta) * rotated * rotated
    step_low = (new_avg / first_bias / (jnp.sqrt(new_avg_sq / second_bias) + epsilon)).astype(
        jnp.bfloat16
    )
    step_rows = lax.all_gather(step_low, "col", axis=1, tiled=True)
    back = inner_cols(step_rows, lax.all_gather(right_basis, "row", axis=1, tiled=True))
    back_low = back.astype(jnp.bfloat16)
    back_cols = lax.all_gather(back_low, "row", axis=0, tiled=True)
    update = jnp.dot(
        lax.all_gather(left_basis, "col", axis=1, tiled=True),
        back_cols,
        preferred_element_type=jnp.float32,
    )
    new_weight = weight - learn_rate * (update + weight_decay * weight)
    return (new_weight, new_avg, new_avg_sq)


def solution(mesh):
    placed = (
        P("row", "col"),
        P("row", "col"),
        P("row", "col"),
        P("row", "col"),
        P("row", "col"),
        P("col", "row"),
    )
    return jax.shard_map(
        on_device,
        mesh=mesh,
        in_specs=placed,
        out_specs=(P("row", "col"), P("row", "col"), P("row", "col")),
        check_vma=False,
    )
```

profile of v0, /device:TPU:1, one launch (start us, length us, event | category | flops | bytes accessed | tf_op | source)
XLA Modules:
  0.0 421.7 jit_solution(8093565179017711877)
XLA Ops:
  7.2 0.0 all-gather.5.cloned.1.call-start
  7.2 0.7 all-gather.5.cloned.1.call-update
  7.9 0.0 reduce-scatter.3.cloned.1.call-start
  7.9 59.7 %all-gather.5.cloned.1.call-done = bf16[256,4096]{1,0:T(8,128)(2,1)} async-done(((bf16[256,512]{1,0:T(8,128)(2,1)}), bf16[256,4096]{1,0:T(8,128)(2,1)}) %all-gather.5.cloned.1.call-update) | async-done | bytes 2097168 | tf_op jit(solution)/shard_map/all_gather | solution.py:51
  67.6 6.3 %convolution_convert_fusion.1 = bf16[4096,768]{1,0:T(8,128)(2,1)} fusion(bf16[256,4096]{1,0:T(8,128)(2,1)} %all-gather.5.cloned.1.call-done, f32[256,768]{1,0:T(8,128)} %param.6), kind=kOutput, calls=%fused_computation.1 | convolution fusion | flops 1613955072 | bytes 9175040 | tf_op jit(solution)/shard_map/dot_general | solution.py:16
  73.9 0.0 reduce-scatter.3.cloned.1.call-update
  74.0 0.0 all-gather.7.cloned.1.call-start
  74.0 0.7 all-gather.7.cloned.1.call-update
  74.7 0.0 copy-start.1
  74.7 0.0 copy-start.2
  74.7 0.0 reduce-scatter.5.cloned.1.call-start
  74.8 73.1 %reduce-scatter.3.cloned.1.call-done = bf16[256,768]{1,0:T(8,128)(2,1)} async-done(((bf16[4096,768]{1,0:T(8,128)(2,1)}), bf16[256,768]{1,0:T(8,128)(2,1)}) %reduce-scatter.3.cloned.1.call-update) | async-done | bytes 393232 | tf_op jit(solution)/shard_map/reduce_scatter | solution.py:30
  147.8 60.6 %all-gather.7.cloned.1.call-done = bf16[768,6144]{1,0:T(8,128)(2,1)} async-done(((bf16[768,384]{1,0:T(8,128)(2,1)}), bf16[768,6144]{1,0:T(8,128)(2,1)}) %all-gather.7.cloned.1.call-update) | async-done | bytes 9437200 | tf_op jit(solution)/shard_map/all_gather | solution.py:35
  208.4 8.1 %convolution_convert_fusion = bf16[256,6144]{1,0:T(8,128)(2,1)} fusion(bf16[256,768]{1,0:T(8,128)(2,1)} %reduce-scatter.3.cloned.1.call-done, bf16[768,6144]{1,0:T(8,128)(2,1)} %all-gather.7.cloned.1.call-done), kind=kOutput, calls=%fused_computation | convolution fusion | flops 2417491968 | bytes 12976128 | tf_op jit(solution)/shard_map/dot_general | solution.py:33
  216.5 0.0 reduce-scatter.5.cloned.1.call-update
  216.5 0.0 all-gather.9.cloned.1.call-start
  216.6 79.0 %reduce-scatter.5.cloned.1.call-done = bf16[256,768]{1,0:T(8,128)(2,1)} async-done(((bf16[256,6144]{1,0:T(8,128)(2,1)}), bf16[256,768]{1,0:T(8,128)(2,1)}) %reduce-scatter.5.cloned.1.call-update) | async-done | bytes 393232 | tf_op jit(solution)/shard_map/reduce_scatter | solution.py:38
  295.6 0.0 copy-done.1
  295.6 0.0 copy-done.2
  295.6 2.6 divide_convert_fusion
  298.1 0.0 all-gather.9.cloned.1.call-update
  298.2 0.0 copy-start
  298.2 0.0 copy-start.3
  298.2 0.0 all-gather.11.cloned.1.call-start
  298.2 62.1 %all-gather.9.cloned.1.call-done = bf16[256,6144]{1,0:T(8,128)(2,1)} async-done(((bf16[256,768]{1,0:T(8,128)(2,1)}), bf16[256,6144]{1,0:T(8,128)(2,1)}) %all-gather.9.cloned.1.call-update) | async-done | bytes 3145744 | tf_op jit(solution)/shard_map/all_gather | solution.py:46
  360.4 8.0 %convolution_convert_fusion.2 = bf16[256,768]{1,0:T(8,128)(2,1)} fusion(bf16[256,6144]{1,0:T(8,128)(2,1)} %all-gather.9.cloned.1.call-done, bf16[768,6144]{1,0:T(8,128)(2,1)} %all-gather.7.cloned.1.call-done), kind=kOutput, calls=%fused_computation.6 | convolution fusion | flops 2416115712 | bytes 12976128 | tf_op jit(solution)/shard_map/dot_general | solution.py:22
  368.4 0.0 all-gather.11.cloned.1.call-update
  368.4 41.0 %all-gather.11.cloned.1.call-done = bf16[4096,768]{1,0:T(8,128)(2,1)} async-done(((bf16[256,768]{1,0:T(8,128)(2,1)}), bf16[4096,768]{1,0:T(8,128)(2,1)}) %all-gather.11.cloned.1.call-update) | async-done | bytes 6291472 | tf_op jit(solution)/shard_map/all_gather | solution.py:49
  409.4 0.0 copy-done
  409.4 0.0 copy-done.3
  409.4 5.5 %fusion.2 = f32[256,768]{1,0:T(8,128)} fusion(f32[256,768]{1,0:T(8,128)S(1)} %copy-done.3, bf16[256,4096]{1,0:T(8,128)(2,1)S(1)} %copy-done, bf16[4096,768]{1,0:T(8,128)(2,1)} %all-gather.11.cloned.1.call-done), kind=kOutput, calls=%fused_computation.5 | convolution fusion | flops 1611399168 | bytes 9961472 | tf_op jit(solution)/shard_map/dot_general | solution.py:50
Async XLA Ops:
  7.2 60.4 %all-gather.5.cloned.1.call-start = ((), (), s32[]{:S(2)}) async-start(), calls=%async_computation.2 | async-start | bytes 2359296 | tf_op jit(solution)/shard_map/all_gather | solution.py:51
  7.9 139.9 %reduce-scatter.3.cloned.1.call-start = ((), (), s32[]{:S(2)}) async-start(), calls=%async_computation.3 | async-start | bytes 6684672 | tf_op jit(solution)/shard_map/reduce_scatter | solution.py:30
  74.0 134.5 %all-gather.7.cloned.1.call-start = ((), (), s32[]{:S(2)}) async-start(), calls=%async_computation.4 | async-start | bytes 10027008 | tf_op jit(solution)/shard_map/all_gather | solution.py:35
  74.7 220.9 %copy-start.1 = (f32[256,768]{1,0:T(8,128)S(1)}, f32[256,768]{1,0:T(8,128)}, u32[]{:S(2)}) copy-start(f32[256,768]{1,0:T(8,128)} %param.8) | copy-start | bytes 2359300
  74.7 220.9 %copy-start.2 = (f32[256,768]{1,0:T(8,128)S(1)}, f32[256,768]{1,0:T(8,128)}, u32[]{:S(2)}) copy-start(f32[256,768]{1,0:T(8,128)} %param.9) | copy-start | bytes 2359300
  74.7 220.8 %reduce-scatter.5.cloned.1.call-start = ((), (), s32[]{:S(2)}) async-start(), calls=%async_computation.5 | async-start | bytes 3538944 | tf_op jit(solution)/shard_map/reduce_scatter | solution.py:38
  216.5 143.8 %all-gather.9.cloned.1.call-start = ((), (), s32[]{:S(2)}) async-start(), calls=%async_computation.6 | async-start | bytes 3538944 | tf_op jit(solution)/shard_map/all_gather | solution.py:46
  298.2 111.2 %copy-start = (bf16[256,4096]{1,0:T(8,128)(2,1)S(1)}, bf16[256,4096]{1,0:T(8,128)(2,1)}, u32[]{:S(2)}) copy-start(bf16[256,4096]{1,0:T(8,128)(2,1)} %all-gather.5.cloned.1.call-done) | copy-start | bytes 6291460
  298.2 111.2 %copy-start.3 = (f32[256,768]{1,0:T(8,128)S(1)}, f32[256,768]{1,0:T(8,128)}, u32[]{:S(2)}) copy-start(f32[256,768]{1,0:T(8,128)} %param.7) | copy-start | bytes 2359300
  298.2 111.2 %all-gather.11.cloned.1.call-start = ((), (), s32[]{:S(2)}) async-start(), calls=%async_computation.7 | async-start | bytes 6684672 | tf_op jit(solution)/shard_map/all_gather | solution.py:49
Sparse Core Ops, SparseCore 0:
  10.2 57.3 all-gather.4
  74.1 73.6 reduce-scatter.2
  149.5 58.8 all-gather.6
  216.7 78.8 reduce-scatter.4
  298.3 62.0 all-gather.8
  368.5 40.8 all-gather.10
where the time goes:
time: 422 us
  waiting for transfers between devices  377 us (89%)
  matrix products  27.9 us (7%)
  between operations  14.1 us (3%)
    reduce_scatter x1, waiting for transfers between devices, on_device(): lax.psum_scatter(right_term.astype(jnp.bfloat16), 'col', scatter_dimensio...  79 us
    reduce_scatter x1, waiting for transfers between devices, on_device(): lax.psum_scatter(left_term.astype(jnp.bfloat16), 'row', scatter_dimension...  73.1 us
    all_gather x1, waiting for transfers between devices, on_device(): step_rows = lax.all_gather(step_low, 'col', axis=1, tiled=True)  62.1 us
    all_gather x1, waiting for transfers between devices, on_device(): lax.all_gather(right_basis, 'row', axis=1, tiled=True)  60.6 us
    all_gather x1, waiting for transfers between devices, on_device(): lax.all_gather(left_basis, 'col', axis=1, tiled=True)  59.7 us
    all_gather x1, waiting for transfers between devices, on_device(): back_cols = lax.all_gather(back_low, 'row', axis=0, tiled=True)  41 us
  transfers between devices with their start and end apart: 6, of which 6 were waited for; matrix products, arithmetic and copies ran while one was open for 0% of the time, Pallas kernels for 0%

commit v1 on v0

v1 whole, which is shorter than its diff:
```python
import jax
import jax.numpy as jnp
import numpy as np
from jax import lax
from jax.sharding import Mesh, PartitionSpec as P

first_beta = 0.9
second_beta = 0.95
first_bias = 1.0 - 0.9**20
second_bias = 1.0 - 0.95**20
epsilon = 1e-08
learn_rate = 0.2
weight_decay = 0.1

AXES = ("y", "xl", "c", "z", "xh")
SIZES = (4, 2, 2, 4, 2)
RING = {"x": (("xl", "xh"), (0, 2, 1, 3)), "y": ("y", range(4)), "z": ("z", range(4))}
HALVES = 1
ROWS = 128 // HALVES
low = jnp.bfloat16
wide = jnp.float32


def dot(left, right, left_dim, right_dim):
    return lax.dot_general(
        left, right, (((left_dim,), (right_dim,)), ((), ())), preferred_element_type=jnp.float32
    )


def shift(value, axis, by):
    names, place = RING[axis]
    return lax.ppermute(value, names, [(place[i], place[(i + by) % 4]) for i in range(4)])


def swap(value, axis):
    return lax.ppermute(value, axis, [(0, 1), (1, 0)])


def move(value, target):
    pairs = []
    for source in range(128):
        place = target(*np.unravel_index(source, SIZES))
        pairs.append((source, int(np.ravel_multi_index(place, SIZES))))
    return lax.ppermute(value, AXES, pairs)


def gather(value, axis):
    two = shift(value, axis, 2)
    one, three = shift(value, axis, -1), shift(value, axis, 1)
    return [value, one, two, three]


def reduce(parts, axis):
    two = shift(parts[2], axis, 2)
    one, three = shift(parts[1], axis, 1), shift(parts[3], axis, -1)
    return (parts[0].astype(wide) + two.astype(wide)) + (one.astype(wide) + three.astype(wide))


def pick(test, first, second):
    return lax.select(jnp.broadcast_to(test, first.shape), first, second)


def rotate(blocks, by):
    odd, two = by % 2 == 1, by // 2 == 1
    blocks = [pick(odd, blocks[(d + 1) % 4], blocks[d]) for d in range(4)]
    return [pick(two, blocks[(d + 2) % 4], blocks[d]) for d in range(4)]


def on_device(grad, weight, exp_avg, exp_avg_sq, left_basis, right_basis):
    y, xl, c, z, xh = (lax.axis_index(name) for name in AXES)
    lo, hi = xl == 0, xh == 0

    grad_low = grad.astype(low)
    chunks = gather(grad_low, "x")
    near = pick(lo, chunks[1], chunks[3])
    far = pick(lo, chunks[3], chunks[1])
    own_cols = jnp.concatenate([chunks[0], near], axis=0)
    other_cols = jnp.concatenate([chunks[2], far], axis=0)
    grad_own = jnp.concatenate(
        [pick(hi, own_cols, other_cols), pick(hi, other_cols, own_cols)], axis=1
    )
    grad_all = jnp.concatenate([grad_own, swap(grad_own, "c")], axis=0)

    blocks = left_basis.reshape(256, 2, 2, 128)
    sub0, sub1 = blocks[:, :, 0].reshape(256, 256), blocks[:, :, 1].reshape(256, 256)
    same = move(
        pick(lo, sub0, sub1), lambda y, xl, c, z, xh: (y, xh, c, z, xl)
    )
    cross = move(
        pick(lo, sub1, sub0), lambda y, xl, c, z, xh: (y, xh, c, z, 1 - xl)
    )
    level = xl == xh
    left_part = jnp.concatenate([pick(level, same, cross), pick(level, cross, same)], axis=0)
    left_parts = rotate(gather(left_part, "z"), (y - z + 4) % 4)
    cores = [[p[:, :128] for p in left_parts], [p[:, 128:] for p in left_parts]]

    def columns(parts):
        return jnp.concatenate(
            [p[:, h * ROWS : (h + 1) * ROWS] for h in range(HALVES) for p in parts], axis=1
        )

    first, second = columns(cores[0]), columns(cores[1])
    left_own = pick(c == 0, first, second)
    left_other = pick(c == 0, second, first)
    left_tall = jnp.concatenate([left_own, swap(left_other, "c")], axis=0)

    right_part = move(right_basis, lambda y, xl, c, z, xh: (y, c, xh, z, xl))
    right_parts = rotate(gather(right_part, "y"), (z - y + 4) % 4)
    right_own = jnp.concatenate(right_parts, axis=1)
    right_other = swap(right_own, "c")
    right = jnp.concatenate(
        [pick(c == 0, right_own, right_other), pick(c == 0, right_other, right_own)], axis=0
    )

    def columns_of(array, block):
        return pick(block == 0, array[:, :384], array[:, 384:])

    def spread(array):
        own = columns_of(array, xl)
        other = swap(columns_of(array, 1 - xl), "xl")
        in_order = lo == hi
        return [
            pick(hi, own[:128], own[128:]),
            pick(in_order, other[:128], other[128:]),
            pick(hi, own[128:], own[:128]),
            pick(in_order, other[128:], other[:128]),
        ]

    avg_blocks, sq_blocks = spread(exp_avg), spread(exp_avg_sq)

    def moments(avg, avg_sq, rotated):
        new_avg = first_beta * avg + (1.0 - first_beta) * rotated
        new_avg_sq = second_beta * avg_sq + (1.0 - second_beta) * rotated * rotated
        return new_avg, new_avg_sq

    rotated_blocks = [[] for _ in range(4)]
    update = None
    for h in range(HALVES):
        span = slice(h * ROWS, (h + 1) * ROWS)
        wide_span = slice(h * 4 * ROWS, (h + 1) * 4 * ROWS)
        part = dot(left_tall[:, wide_span], grad_all, 0, 0).astype(low)
        left_low = reduce([part[d * ROWS : (d + 1) * ROWS] for d in range(4)], "y").astype(low)
        left_rows = jnp.concatenate(gather(left_low, "x"), axis=0)
        part = dot(left_rows, right, 1, 0).astype(low)
        rotated = reduce([part[:, d * 384 : (d + 1) * 384] for d in range(4)], "z")
        for d in range(4):
            rotated_blocks[d].append(rotated[d * ROWS : (d + 1) * ROWS])
        new_avg, new_avg_sq = moments(
            jnp.concatenate([b[span] for b in avg_blocks], axis=0),
            jnp.concatenate([b[span] for b in sq_blocks], axis=0),
            rotated,
        )
        step = (new_avg / first_bias / (jnp.sqrt(new_avg_sq / second_bias) + epsilon)).astype(low)
        step_rows = jnp.concatenate(gather(step, "z"), axis=1)
        part = dot(step_rows, right, 1, 1).astype(low)
        back = reduce([part[d * ROWS : (d + 1) * ROWS] for d in range(4)], "x").astype(low)
        back_own = jnp.concatenate(gather(back, "y"), axis=0)
        term = dot(left_own[:, wide_span], back_own, 1, 0)
        term = term + dot(left_other[:, wide_span], swap(back_own, "c"), 1, 0)
        update = term if update is None else update + term

    update_low = update.astype(low)

    def block(rows, test):
        strip = update_low[rows * 256 : (rows + 1) * 256]
        return pick(test, strip[:, :768], strip[:, 768:])

    straight = lo == hi
    total = reduce(
        [block(0, hi), block(1, straight), block(0, ~hi), block(1, ~straight)], "x"
    )
    new_weight = weight - learn_rate * (total + weight_decay * weight)

    rows = [jnp.concatenate(b, axis=0).astype(low) for b in rotated_blocks]
    kept = jnp.concatenate([pick(hi, rows[0], rows[2]), pick(hi, rows[2], rows[0])], axis=0)
    sent = jnp.concatenate(
        [pick(straight, rows[1], rows[3]), pick(straight, rows[3], rows[1])], axis=0
    )
    came = swap(sent, "xl")
    rotated = jnp.concatenate([pick(lo, kept, came), pick(lo, came, kept)], axis=1).astype(wide)
    new_avg, new_avg_sq = moments(exp_avg, exp_avg_sq, rotated)
    return (new_weight, new_avg, new_avg_sq)


def solution(mesh):
    grid = Mesh(np.asarray(mesh.devices).reshape(SIZES), AXES)
    row, col = ("y", "xl", "c"), ("z", "xh")
    placed = (P(row, col),) * 5 + (P(col, row),)
    return jax.shard_map(
        on_device,
        mesh=grid,
        in_specs=placed,
        out_specs=(P(row, col),) * 3,
        check_vma=False,
    )
```

time: 422 us -> 244 us (0.58)
  waiting for transfers between devices: 377 us -> 145 us
  starting transfers between devices: 0.24 us -> 69 us
  matrix products: 27.9 us -> 12.3 us
  between operations: 14.1 us -> 1.03 us
  other arithmetic: 2.57 us -> 13.7 us
    all_gather x4 -> x0, waiting for transfers between devices: 223 us -> none  [the longest x1 62.1 us: on_device(): step_rows = lax.all_gather(step_low, 'col', axis=1, tiled=True)]
    reduce_scatter x2 -> x0, waiting for transfers between devices: 152 us -> none  [the longest x1 79 us: on_device(): lax.psum_scatter(right_term.astype(jnp.bfloat16), 'col', scatter_dimensio...]
    ppermute x0 -> x40, waiting for transfers between devices: none -> 145 us  [the longest x30 136 us: shift(): lax.ppermute(value, names, [(place[i], place[(i + by) % 4]) for i in rang...]
    ppermute x0 -> x40, starting transfers between devices: none -> 69 us  [the longest x30 45 us: shift(): lax.ppermute(value, names, [(place[i], place[(i + by) % 4]) for i in rang...]
    dot_general x4 -> x5, matrix products: 27.9 us -> 12.3 us  [dot(): lax.dot_general(left, right, (((left_dim,), (right_dim,)), ((), ())), pre...]
    select_n x0 -> x15, other arithmetic: none -> 6.55 us  [pick(): return lax.select(jnp.broadcast_to(test, first.shape), first, second)]
  transfers between devices with their start and end apart: 6 -> 40, of which waited for: 6 -> 28; matrix products, arithmetic and copies ran while one was open for 0% -> 9% of each run, Pallas kernels for 0% -> 0%
where the time goes in v1:
time: 244 us; the launch traced here: 242 us
  waiting for transfers between devices  145 us (59%)
  starting transfers between devices  69 us (28%)
  other arithmetic  13.7 us (6%)
  matrix products  12.3 us (5%)
    ppermute x30, waiting for transfers between devices, shift(): lax.ppermute(value, names, [(place[i], place[(i + by) % 4]) for i in rang...  136 us
    ppermute x30, starting transfers between devices, shift(): lax.ppermute(value, names, [(place[i], place[(i + by) % 4]) for i in rang...  45 us
    ppermute x3, starting transfers between devices, move(): return lax.ppermute(value, AXES, pairs)  12.5 us
    dot_general x5, matrix products, dot(): lax.dot_general(left, right, (((left_dim,), (right_dim,)), ((), ())), pre...  12.3 us
    ppermute x7, starting transfers between devices, swap(): return lax.ppermute(value, axis, [(0, 1), (1, 0)])  11.5 us
    select_n x15, other arithmetic, pick(): return lax.select(jnp.broadcast_to(test, first.shape), first, second)  6.55 us
    ppermute x3, waiting for transfers between devices, move(): return lax.ppermute(value, AXES, pairs)  5.84 us
  transfers between devices with their start and end apart: 40, of which 28 were waited for; matrix products, arithmetic and copies ran while one was open for 9% of the time, Pallas kernels for 0%

profile of v1, /device:TPU:1, one launch (start us, length us, event | category | flops | bytes accessed | tf_op | source)
XLA Modules:
  0.0 242.5 jit_solution(546229383253535807)
XLA Ops:
  2.6 5.1 %collective-permute-start.1 = (bf16[256,256]{0,1:T(8,128)(2,1)S(1)}, bf16[256,256]{0,1:T(8,128)(2,1)S(1)}, u32[]{:S(2)}, u32[]{:S(2)}) collective-permute-start(bf16[256,256]{0,1:T(8,128)(2,1)S(1)} %bitcast.7), channel_id=1, source_target_pairs={{0,1},{1,17},{2,3},{3,19},{4,5},{5,21},{6,7},{7,23},{8,9},{9,25},{... | collective-permute-start | bytes 393224 | tf_op jit(solution)/shard_map/ppermute | solution.py:44
  11.8 3.3 %collective-permute-start.3 = (bf16[512,256]{0,1:T(8,128)(2,1)S(1)}, bf16[512,256]{0,1:T(8,128)(2,1)S(1)}, u32[]{:S(2)}, u32[]{:S(2)}) collective-permute-start(bf16[512,256]{0,1:T(8,128)(2,1)S(1)} %pad_maximum_fusion.15), channel_id=1, source_target_pairs={{0,4},{2,6},{4,0},{6,2},{1,5},{3,7},{5,1},{7,3},{8,12},{10,14},{12... | collective-permute-start | bytes 786440 | tf_op jit(solution)/shard_map/ppermute | solution.py:32
  20.8 4.7 %collective-permute-done.3 = bf16[512,256]{0,1:T(8,128)(2,1)S(1)} collective-permute-done((bf16[512,256]{0,1:T(8,128)(2,1)S(1)}, bf16[512,256]{0,1:T(8,128)(2,1)S(1)}, u32[]{:S(2)}, u32[]{:S(2)}) %collective-permute-start.3) | collective-permute-done | bytes 262176 | tf_op jit(solution)/shard_map/ppermute | solution.py:32
  25.5 6.7 %collective-permute-start.17 = (bf16[768,384]{1,0:T(8,128)(2,1)S(1)}, bf16[768,384]{1,0:T(8,128)(2,1)S(1)}, u32[]{:S(2)}, u32[]{:S(2)}) collective-permute-start(bf16[768,384]{1,0:T(8,128)(2,1)S(1)} %copy-done.7), channel_id=1, source_target_pairs={{0,0},{1,8},{2,2},{3,10},{4,4},{5,12},{6,6},{7,14},{8,16},{9,24},{... | collective-permute-start | bytes 1769480 | tf_op jit(solution)/shard_map/ppermute | solution.py:44
  35.4 5.7 %collective-permute-start.10 = (bf16[512,1536]{1,0:T(8,128)(2,1)}, bf16[512,1536]{1,0:T(8,128)(2,1)}, u32[]{:S(2)}, u32[]{:S(2)}) collective-permute-start(bf16[512,1536]{1,0:T(8,128)(2,1)} %pad_maximum_fusion.8), channel_id=1, source_target_pairs={{0,8},{8,0},{1,9},{9,1},{2,10},{10,2},{3,11},{11,3},{4,12},{12,4},... | collective-permute-start | bytes 4718600 | tf_op jit(solution)/shard_map/ppermute | solution.py:36
  41.1 3.5 %collective-permute-done.17 = bf16[768,384]{1,0:T(8,128)(2,1)S(1)} collective-permute-done((bf16[768,384]{1,0:T(8,128)(2,1)S(1)}, bf16[768,384]{1,0:T(8,128)(2,1)S(1)}, u32[]{:S(2)}, u32[]{:S(2)}) %collective-permute-start.17) | collective-permute-done | bytes 589856 | tf_op jit(solution)/shard_map/ppermute | solution.py:44
  45.9 2.6 %collective-permute-start.19 = (bf16[768,384]{1,0:T(8,128)(2,1)S(1)}, bf16[768,384]{1,0:T(8,128)(2,1)S(1)}, u32[]{:S(2)}, u32[]{:S(2)}) collective-permute-start(bf16[768,384]{1,0:T(8,128)(2,1)S(1)} %collective-permute-done.17), channel_id=1, source_target_pairs={{0,64},{32,96},{64,0},{96,32},{1,65},{33,97},{65,1},{97,33},{2,66}... | collective-permute-start | bytes 1769480 | tf_op jit(solution)/shard_map/ppermute | solution.py:32
  50.9 9.1 %collective-permute-done.18 = bf16[768,384]{1,0:T(8,128)(2,1)S(1)} collective-permute-done((bf16[768,384]{1,0:T(8,128)(2,1)S(1)}, bf16[768,384]{1,0:T(8,128)(2,1)S(1)}, u32[]{:S(2)}, u32[]{:S(2)}) %collective-permute-start.18) | collective-permute-done | bytes 589856 | tf_op jit(solution)/shard_map/ppermute | solution.py:32
  60.0 11.7 %collective-permute-done.19 = bf16[768,384]{1,0:T(8,128)(2,1)S(1)} collective-permute-done((bf16[768,384]{1,0:T(8,128)(2,1)S(1)}, bf16[768,384]{1,0:T(8,128)(2,1)S(1)}, u32[]{:S(2)}, u32[]{:S(2)}) %collective-permute-start.19) | collective-permute-done | bytes 589856 | tf_op jit(solution)/shard_map/ppermute | solution.py:32
  74.5 3.3 %collective-permute-start.25 = (f32[256,384]{1,0:T(8,128)}, f32[256,384]{1,0:T(8,128)}, u32[]{:S(2)}, u32[]{:S(2)}) collective-permute-start(f32[256,384]{1,0:T(8,128)} %get-tuple-element.36), channel_id=1, source_target_pairs={{0,16},{16,0},{1,17},{17,1},{2,18},{18,2},{3,19},{19,3},{4,20},{20... | collective-permute-start | bytes 1179656 | tf_op jit(solution)/shard_map/ppermute | solution.py:36
  77.8 4.0 %fusion.8 = bf16[512,1536]{1,0:T(8,128)(2,1)S(1)} fusion(bf16[512,1536]{1,0:T(8,128)(2,1)} %collective-permute-done.10, bf16[512,768]{1,0:T(8,128)(2,1)} %copy-done.3, bf16[512,768]{1,0:T(8,128)(2,1)} %copy-done.2, bf16[512,512]{0,1:T(8,128)(2,1)} %collective-permute-done.6, bf16[512,512]{0,1:T(8,128)(2,1)} %get-tuple-element.25), kind=kOutput, calls=%fused_computation.10 | convolution fusion | flops 1622933504 | bytes 5767168 | tf_op jit(solution)/shard_map/dot_general | solution.py:25
  85.9 6.5 %collective-permute-done.13 = bf16[128,1536]{1,0:T(8,128)(2,1)S(1)} collective-permute-done((bf16[128,1536]{1,0:T(8,128)(2,1)S(1)}, bf16[128,1536]{1,0:T(8,128)(2,1)S(1)}, u32[]{:S(2)}, u32[]{:S(2)}) %collective-permute-start.13) | collective-permute-done | bytes 393248 | tf_op jit(solution)/shard_map/ppermute | solution.py:32
  92.7 3.0 %collective-permute-done.12 = bf16[128,1536]{1,0:T(8,128)(2,1)S(1)} collective-permute-done((bf16[128,1536]{1,0:T(8,128)(2,1)S(1)}, bf16[128,1536]{1,0:T(8,128)(2,1)S(1)}, u32[]{:S(2)}, u32[]{:S(2)}) %collective-permute-start.12) | collective-permute-done | bytes 393248 | tf_op jit(solution)/shard_map/ppermute | solution.py:32
  95.8 7.1 %collective-permute-done.11 = bf16[128,1536]{1,0:T(8,128)(2,1)S(1)} collective-permute-done((bf16[128,1536]{1,0:T(8,128)(2,1)S(1)}, bf16[128,1536]{1,0:T(8,128)(2,1)S(1)}, u32[]{:S(2)}, u32[]{:S(2)}) %collective-permute-start.11) | collective-permute-done | bytes 393248 | tf_op jit(solution)/shard_map/ppermute | solution.py:32
  108.6 4.3 %collective-permute-done.16 = bf16[128,1536]{1,0:T(8,128)(2,1)S(1)} collective-permute-done((bf16[128,1536]{1,0:T(8,128)(2,1)S(1)}, bf16[128,1536]{1,0:T(8,128)(2,1)S(1)}, u32[]{:S(2)}, u32[]{:S(2)}) %collective-permute-start.16) | collective-permute-done | bytes 393248 | tf_op jit(solution)/shard_map/ppermute | solution.py:32
  112.9 10.5 %collective-permute-done.15 = bf16[128,1536]{1,0:T(8,128)(2,1)S(1)} collective-permute-done((bf16[128,1536]{1,0:T(8,128)(2,1)S(1)}, bf16[128,1536]{1,0:T(8,128)(2,1)S(1)}, u32[]{:S(2)}, u32[]{:S(2)}) %collective-permute-start.15) | collective-permute-done | bytes 393248 | tf_op jit(solution)/shard_map/ppermute | solution.py:32
  130.7 4.3 %collective-permute-done.24 = bf16[512,384]{1,0:T(8,128)(2,1)S(1)} collective-permute-done((bf16[512,384]{1,0:T(8,128)(2,1)S(1)}, bf16[512,384]{1,0:T(8,128)(2,1)S(1)}, u32[]{:S(2)}, u32[]{:S(2)}) %collective-permute-start.24) | collective-permute-done | bytes 393248 | tf_op jit(solution)/shard_map/ppermute | solution.py:32
  136.7 7.1 %collective-permute-done.22 = bf16[512,384]{1,0:T(8,128)(2,1)S(1)} collective-permute-done((bf16[512,384]{1,0:T(8,128)(2,1)S(1)}, bf16[512,384]{1,0:T(8,128)(2,1)S(1)}, u32[]{:S(2)}, u32[]{:S(2)}) %collective-permute-start.22) | collective-permute-done | bytes 393248 | tf_op jit(solution)/shard_map/ppermute | solution.py:32
  144.6 3.2 %collective-permute-start.27 = (bf16[512,384]{1,0:T(8,128)(2,1)S(1)}, bf16[512,384]{1,0:T(8,128)(2,1)S(1)}, u32[]{:S(2)}, u32[]{:S(2)}) collective-permute-start(bf16[512,384]{1,0:T(8,128)(2,1)S(1)} %get-tuple-element.6), channel_id=1, source_target_pairs={{0,4},{2,6},{4,0},{6,2},{1,5},{3,7},{5,1},{7,3},{8,12},{10,14},{12... | collective-permute-start | bytes 1179656 | tf_op jit(solution)/shard_map/ppermute | solution.py:32
  149.0 3.4 %collective-permute-done.28 = bf16[512,384]{1,0:T(8,128)(2,1)S(1)} collective-permute-done((bf16[512,384]{1,0:T(8,128)(2,1)S(1)}, bf16[512,384]{1,0:T(8,128)(2,1)S(1)}, u32[]{:S(2)}, u32[]{:S(2)}) %collective-permute-start.28) | collective-permute-done | bytes 393248 | tf_op jit(solution)/shard_map/ppermute | solution.py:32
  152.4 9.4 %collective-permute-done.27 = bf16[512,384]{1,0:T(8,128)(2,1)S(1)} collective-permute-done((bf16[512,384]{1,0:T(8,128)(2,1)S(1)}, bf16[512,384]{1,0:T(8,128)(2,1)S(1)}, u32[]{:S(2)}, u32[]{:S(2)}) %collective-permute-start.27) | collective-permute-done | bytes 393248 | tf_op jit(solution)/shard_map/ppermute | solution.py:32
  162.9 2.6 %fusion.12 = bf16[512,1536]{1,0:T(8,128)(2,1)S(1)} fusion(bf16[768,1536]{1,0:T(8,128)(2,1)S(1)} %get-tuple-element.4, bf16[768,1536]{1,0:T(8,128)(2,1)S(1)} %get-tuple-element.3, bf16[512,384]{1,0:T(8,128)(2,1)S(1)} %collective-permute-done.28, bf16[512,384]{1,0:T(8,128)(2,1)S(1)} %collective-permute-done.27, ...), kind=kOutput, calls=%fused_computation.12 | convolution fusion | flops 2432434176 | bytes 7864320 | tf_op jit(solution)/shard_map/dot_general | solution.py:25
  165.7 5.6 %collective-permute-start.31 = (bf16[128,1536]{1,0:T(8,128)(2,1)S(1)}, bf16[128,1536]{1,0:T(8,128)(2,1)S(1)}, u32[]{:S(2)}, u32[]{:S(2)}) collective-permute-start(bf16[128,1536]{1,0:T(8,128)(2,1)S(1)} %get-tuple-element.15), channel_id=1, source_target_pairs={{0,17},{16,0},{1,16},{17,1},{2,19},{18,2},{3,18},{19,3},{4,21},{20... | collective-permute-start | bytes 1179656 | tf_op jit(solution)/shard_map/ppermute | solution.py:32
  172.5 6.1 %collective-permute-done.31 = bf16[128,1536]{1,0:T(8,128)(2,1)S(1)} collective-permute-done((bf16[128,1536]{1,0:T(8,128)(2,1)S(1)}, bf16[128,1536]{1,0:T(8,128)(2,1)S(1)}, u32[]{:S(2)}, u32[]{:S(2)}) %collective-permute-start.31) | collective-permute-done | bytes 393248 | tf_op jit(solution)/shard_map/ppermute | solution.py:32
  178.7 3.7 %collective-permute-done.30 = bf16[128,1536]{1,0:T(8,128)(2,1)S(1)} collective-permute-done((bf16[128,1536]{1,0:T(8,128)(2,1)S(1)}, bf16[128,1536]{1,0:T(8,128)(2,1)S(1)}, u32[]{:S(2)}, u32[]{:S(2)}) %collective-permute-start.30) | collective-permute-done | bytes 393248 | tf_op jit(solution)/shard_map/ppermute | solution.py:32
  182.4 6.2 %collective-permute-done.29 = bf16[128,1536]{1,0:T(8,128)(2,1)S(1)} collective-permute-done((bf16[128,1536]{1,0:T(8,128)(2,1)S(1)}, bf16[128,1536]{1,0:T(8,128)(2,1)S(1)}, u32[]{:S(2)}, u32[]{:S(2)}) %collective-permute-start.29) | collective-permute-done | bytes 393248 | tf_op jit(solution)/shard_map/ppermute | solution.py:32
  190.5 5.7 %collective-permute-start.33 = (bf16[128,1536]{1,0:T(8,128)(2,1)S(1)}, bf16[128,1536]{1,0:T(8,128)(2,1)S(1)}, u32[]{:S(2)}, u32[]{:S(2)}) collective-permute-start(bf16[128,1536]{1,0:T(8,128)(2,1)S(1)} %add_convert_fusion), channel_id=1, source_target_pairs={{0,64},{32,96},{64,0},{96,32},{1,65},{33,97},{65,1},{97,33},{2,66}... | collective-permute-start | bytes 1179656 | tf_op jit(solution)/shard_map/ppermute | solution.py:32
  196.1 5.5 %collective-permute-done.34 = bf16[128,1536]{1,0:T(8,128)(2,1)S(1)} collective-permute-done((bf16[128,1536]{1,0:T(8,128)(2,1)S(1)}, bf16[128,1536]{1,0:T(8,128)(2,1)S(1)}, u32[]{:S(2)}, u32[]{:S(2)}) %collective-permute-start.34) | collective-permute-done | bytes 393248 | tf_op jit(solution)/shard_map/ppermute | solution.py:32
  201.6 9.3 %collective-permute-done.33 = bf16[128,1536]{1,0:T(8,128)(2,1)S(1)} collective-permute-done((bf16[128,1536]{1,0:T(8,128)(2,1)S(1)}, bf16[128,1536]{1,0:T(8,128)(2,1)S(1)}, u32[]{:S(2)}, u32[]{:S(2)}) %collective-permute-start.33) | collective-permute-done | bytes 393248 | tf_op jit(solution)/shard_map/ppermute | solution.py:32
  215.0 2.9 %collective-permute-done.35 = bf16[512,1536]{1,0:T(8,128)(2,1)S(1)} collective-permute-done((bf16[512,1536]{1,0:T(8,128)(2,1)S(1)}, bf16[512,1536]{1,0:T(8,128)(2,1)S(1)}, u32[]{:S(2)}, u32[]{:S(2)}) %collective-permute-start.35) | collective-permute-done | bytes 1572896 | tf_op jit(solution)/shard_map/ppermute | solution.py:36
  224.1 7.4 %collective-permute-done.38 = bf16[256,768]{1,0:T(8,128)(2,1)S(1)} collective-permute-done((bf16[256,768]{1,0:T(8,128)(2,1)S(1)}, bf16[256,768]{1,0:T(8,128)(2,1)S(1)}, u32[]{:S(2)}, u32[]{:S(2)}) %collective-permute-start.38) | collective-permute-done | bytes 393248 | tf_op jit(solution)/shard_map/ppermute | solution.py:32
  231.5 9.7 %collective-permute-done.37 = bf16[256,768]{1,0:T(8,128)(2,1)S(1)} collective-permute-done((bf16[256,768]{1,0:T(8,128)(2,1)S(1)}, bf16[256,768]{1,0:T(8,128)(2,1)S(1)}, u32[]{:S(2)}, u32[]{:S(2)}) %collective-permute-start.37) | collective-permute-done | bytes 393248 | tf_op jit(solution)/shard_map/ppermute | solution.py:32
  (102 shorter events, 58.1 us)
Async XLA Ops:
  11.8 13.7 %collective-permute-start.3 = (bf16[512,256]{0,1:T(8,128)(2,1)S(1)}, bf16[512,256]{0,1:T(8,128)(2,1)S(1)}, u32[]{:S(2)}, u32[]{:S(2)}) collective-permute-start(bf16[512,256]{0,1:T(8,128)(2,1)S(1)} %pad_maximum_fusion.15), channel_id=1, source_target_pairs={{0,4},{2,6},{4,0},{6,2},{1,5},{3,7},{5,1},{7,3},{8,12},{10,14},{12... | collective-permute-start | bytes 786440 | tf_op jit(solution)/shard_map/ppermute | solution.py:32
  15.1 17.1 %collective-permute-start.4 = (bf16[512,256]{0,1:T(8,128)(2,1)S(1)}, bf16[512,256]{0,1:T(8,128)(2,1)S(1)}, u32[]{:S(2)}, u32[]{:S(2)}) collective-permute-start(bf16[512,256]{0,1:T(8,128)(2,1)S(1)} %pad_maximum_fusion.15), channel_id=1, source_target_pairs={{0,6},{2,0},{4,2},{6,4},{1,7},{3,1},{5,3},{7,5},{8,14},{10,8},{12,... | collective-permute-start | bytes 786440 | tf_op jit(solution)/shard_map/ppermute | solution.py:32
  15.9 16.6 %collective-permute-start.7 = (bf16[256,768]{1,0:T(8,128)(2,1)S(1)}, bf16[256,768]{1,0:T(8,128)(2,1)S(1)}, u32[]{:S(2)}, u32[]{:S(2)}) collective-permute-start(bf16[256,768]{1,0:T(8,128)(2,1)S(1)} %convert_element_type.79), channel_id=1, source_target_pairs={{0,17},{16,0},{1,16},{17,1},{2,19},{18,2},{3,18},{19,3},{4,21},{20... | collective-permute-start | bytes 1179656 | tf_op jit(solution)/shard_map/ppermute | solution.py:32
  17.4 15.1 %collective-permute-start.8 = (bf16[256,768]{1,0:T(8,128)(2,1)S(1)}, bf16[256,768]{1,0:T(8,128)(2,1)S(1)}, u32[]{:S(2)}, u32[]{:S(2)}) collective-permute-start(bf16[256,768]{1,0:T(8,128)(2,1)S(1)} %convert_element_type.79), channel_id=1, source_target_pairs={{0,16},{16,1},{1,17},{17,0},{2,18},{18,3},{3,19},{19,2},{4,20},{20... | collective-permute-start | bytes 1179656 | tf_op jit(solution)/shard_map/ppermute | solution.py:32
  19.0 14.7 %collective-permute-start.9 = (bf16[256,768]{1,0:T(8,128)(2,1)S(1)}, bf16[256,768]{1,0:T(8,128)(2,1)S(1)}, u32[]{:S(2)}, u32[]{:S(2)}) collective-permute-start(bf16[256,768]{1,0:T(8,128)(2,1)S(1)} %convert_element_type.79), channel_id=1, source_target_pairs={{0,1},{16,17},{1,0},{17,16},{2,3},{18,19},{3,2},{19,18},{4,5},{20,... | collective-permute-start | bytes 1179656 | tf_op jit(solution)/shard_map/ppermute | solution.py:32
  25.5 19.1 %collective-permute-start.17 = (bf16[768,384]{1,0:T(8,128)(2,1)S(1)}, bf16[768,384]{1,0:T(8,128)(2,1)S(1)}, u32[]{:S(2)}, u32[]{:S(2)}) collective-permute-start(bf16[768,384]{1,0:T(8,128)(2,1)S(1)} %copy-done.7), channel_id=1, source_target_pairs={{0,0},{1,8},{2,2},{3,10},{4,4},{5,12},{6,6},{7,14},{8,16},{9,24},{... | collective-permute-start | bytes 1769480 | tf_op jit(solution)/shard_map/ppermute | solution.py:44
  35.4 42.4 %collective-permute-start.10 = (bf16[512,1536]{1,0:T(8,128)(2,1)}, bf16[512,1536]{1,0:T(8,128)(2,1)}, u32[]{:S(2)}, u32[]{:S(2)}) collective-permute-start(bf16[512,1536]{1,0:T(8,128)(2,1)} %pad_maximum_fusion.8), channel_id=1, source_target_pairs={{0,8},{8,0},{1,9},{9,1},{2,10},{10,2},{3,11},{11,3},{4,12},{12,4},... | collective-permute-start | bytes 4718600 | tf_op jit(solution)/shard_map/ppermute | solution.py:36
  44.6 15.4 %collective-permute-start.18 = (bf16[768,384]{1,0:T(8,128)(2,1)S(1)}, bf16[768,384]{1,0:T(8,128)(2,1)S(1)}, u32[]{:S(2)}, u32[]{:S(2)}) collective-permute-start(bf16[768,384]{1,0:T(8,128)(2,1)S(1)} %collective-permute-done.17), channel_id=1, source_target_pairs={{0,32},{32,64},{64,96},{96,0},{1,33},{33,65},{65,97},{97,1},{2,34}... | collective-permute-start | bytes 1769480 | tf_op jit(solution)/shard_map/ppermute | solution.py:32
  45.9 25.8 %collective-permute-start.19 = (bf16[768,384]{1,0:T(8,128)(2,1)S(1)}, bf16[768,384]{1,0:T(8,128)(2,1)S(1)}, u32[]{:S(2)}, u32[]{:S(2)}) collective-permute-start(bf16[768,384]{1,0:T(8,128)(2,1)S(1)} %collective-permute-done.17), channel_id=1, source_target_pairs={{0,64},{32,96},{64,0},{96,32},{1,65},{33,97},{65,1},{97,33},{2,66}... | collective-permute-start | bytes 1769480 | tf_op jit(solution)/shard_map/ppermute | solution.py:32
  48.5 23.2 %collective-permute-start.20 = (bf16[768,384]{1,0:T(8,128)(2,1)S(1)}, bf16[768,384]{1,0:T(8,128)(2,1)S(1)}, u32[]{:S(2)}, u32[]{:S(2)}) collective-permute-start(bf16[768,384]{1,0:T(8,128)(2,1)S(1)} %collective-permute-done.17), channel_id=1, source_target_pairs={{0,96},{32,0},{64,32},{96,64},{1,97},{33,1},{65,33},{97,65},{2,98}... | collective-permute-start | bytes 1769480 | tf_op jit(solution)/shard_map/ppermute | solution.py:32
  50.9 26.9 %collective-permute-start.6 = (bf16[512,512]{0,1:T(8,128)(2,1)}, bf16[512,512]{0,1:T(8,128)(2,1)}, u32[]{:S(2)}, u32[]{:S(2)}) collective-permute-start(bf16[512,512]{0,1:T(8,128)(2,1)} %get-tuple-element.26), channel_id=1, source_target_pairs={{0,8},{8,0},{1,9},{9,1},{2,10},{10,2},{3,11},{11,3},{4,12},{12,4},... | collective-permute-start | bytes 1572872 | tf_op jit(solution)/shard_map/ppermute | solution.py:36
  73.7 31.6 %collective-permute-start.21 = (bf16[768,1536]{1,0:T(8,128)(2,1)}, bf16[768,1536]{1,0:T(8,128)(2,1)}, u32[]{:S(2)}, u32[]{:S(2)}) collective-permute-start(bf16[768,1536]{1,0:T(8,128)(2,1)} %pad_maximum_fusion.7), channel_id=1, source_target_pairs={{0,8},{8,0},{1,9},{9,1},{2,10},{10,2},{3,11},{11,3},{4,12},{12,4},... | collective-permute-start | bytes 7077896 | tf_op jit(solution)/shard_map/ppermute | solution.py:36
  74.5 55.1 %collective-permute-start.25 = (f32[256,384]{1,0:T(8,128)}, f32[256,384]{1,0:T(8,128)}, u32[]{:S(2)}, u32[]{:S(2)}) collective-permute-start(f32[256,384]{1,0:T(8,128)} %get-tuple-element.36), channel_id=1, source_target_pairs={{0,16},{16,0},{1,17},{17,1},{2,18},{18,2},{3,19},{19,3},{4,20},{20... | collective-permute-start | bytes 1179656 | tf_op jit(solution)/shard_map/ppermute | solution.py:36
  81.9 10.5 %collective-permute-start.13 = (bf16[128,1536]{1,0:T(8,128)(2,1)S(1)}, bf16[128,1536]{1,0:T(8,128)(2,1)S(1)}, u32[]{:S(2)}, u32[]{:S(2)}) collective-permute-start(bf16[128,1536]{1,0:T(8,128)(2,1)S(1)} %get-tuple-element.21), channel_id=1, source_target_pairs={{0,96},{32,0},{64,32},{96,64},{1,97},{33,1},{65,33},{97,65},{2,98}... | collective-permute-start | bytes 1179656 | tf_op jit(solution)/shard_map/ppermute | solution.py:32
  83.8 12.0 %collective-permute-start.12 = (bf16[128,1536]{1,0:T(8,128)(2,1)S(1)}, bf16[128,1536]{1,0:T(8,128)(2,1)S(1)}, u32[]{:S(2)}, u32[]{:S(2)}) collective-permute-start(bf16[128,1536]{1,0:T(8,128)(2,1)S(1)} %get-tuple-element.22), channel_id=1, source_target_pairs={{0,32},{32,64},{64,96},{96,0},{1,33},{33,65},{65,97},{97,1},{2,34}... | collective-permute-start | bytes 1179656 | tf_op jit(solution)/shard_map/ppermute | solution.py:32
  83.8 19.1 %collective-permute-start.11 = (bf16[128,1536]{1,0:T(8,128)(2,1)S(1)}, bf16[128,1536]{1,0:T(8,128)(2,1)S(1)}, u32[]{:S(2)}, u32[]{:S(2)}) collective-permute-start(bf16[128,1536]{1,0:T(8,128)(2,1)S(1)} %get-tuple-element.20), channel_id=1, source_target_pairs={{0,64},{32,96},{64,0},{96,32},{1,65},{33,97},{65,1},{97,33},{2,66}... | collective-permute-start | bytes 1179656 | tf_op jit(solution)/shard_map/ppermute | solution.py:32
  92.4 38.2 %collective-permute-start.5 = (f32[256,384]{1,0:T(8,128)S(1)}, f32[256,384]{1,0:T(8,128)S(1)}, u32[]{:S(2)}, u32[]{:S(2)}) collective-permute-start(f32[256,384]{1,0:T(8,128)S(1)} %get-tuple-element.34), channel_id=1, source_target_pairs={{0,16},{16,0},{1,17},{17,1},{2,18},{18,2},{3,19},{19,3},{4,20},{20... | collective-permute-start | bytes 1179656 | tf_op jit(solution)/shard_map/ppermute | solution.py:36
  103.1 9.8 %collective-permute-start.16 = (bf16[128,1536]{1,0:T(8,128)(2,1)S(1)}, bf16[128,1536]{1,0:T(8,128)(2,1)S(1)}, u32[]{:S(2)}, u32[]{:S(2)}) collective-permute-start(bf16[128,1536]{1,0:T(8,128)(2,1)S(1)} %add_convert_fusion.1), channel_id=1, source_target_pairs={{0,16},{16,1},{1,17},{17,0},{2,18},{18,3},{3,19},{19,2},{4,20},{20... | collective-permute-start | bytes 1179656 | tf_op jit(solution)/shard_map/ppermute | solution.py:32
  103.5 19.9 %collective-permute-start.15 = (bf16[128,1536]{1,0:T(8,128)(2,1)S(1)}, bf16[128,1536]{1,0:T(8,128)(2,1)S(1)}, u32[]{:S(2)}, u32[]{:S(2)}) collective-permute-start(bf16[128,1536]{1,0:T(8,128)(2,1)S(1)} %add_convert_fusion.1), channel_id=1, source_target_pairs={{0,1},{16,17},{1,0},{17,16},{2,3},{18,19},{3,2},{19,18},{4,5},{20,... | collective-permute-start | bytes 1179656 | tf_op jit(solution)/shard_map/ppermute | solution.py:32
  105.3 18.9 %collective-permute-start.14 = (bf16[128,1536]{1,0:T(8,128)(2,1)S(1)}, bf16[128,1536]{1,0:T(8,128)(2,1)S(1)}, u32[]{:S(2)}, u32[]{:S(2)}) collective-permute-start(bf16[128,1536]{1,0:T(8,128)(2,1)S(1)} %add_convert_fusion.1), channel_id=1, source_target_pairs={{0,17},{16,0},{1,16},{17,1},{2,19},{18,2},{3,18},{19,3},{4,21},{20... | collective-permute-start | bytes 1179656 | tf_op jit(solution)/shard_map/ppermute | solution.py:32
  128.5 15.3 %collective-permute-start.22 = (bf16[512,384]{1,0:T(8,128)(2,1)S(1)}, bf16[512,384]{1,0:T(8,128)(2,1)S(1)}, u32[]{:S(2)}, u32[]{:S(2)}) collective-permute-start(bf16[512,384]{1,0:T(8,128)(2,1)S(1)} %get-tuple-element.17), channel_id=1, source_target_pairs={{0,4},{2,6},{4,0},{6,2},{1,5},{3,7},{5,1},{7,3},{8,12},{10,14},{12... | collective-permute-start | bytes 1179656 | tf_op jit(solution)/shard_map/ppermute | solution.py:32
  144.6 17.2 %collective-permute-start.27 = (bf16[512,384]{1,0:T(8,128)(2,1)S(1)}, bf16[512,384]{1,0:T(8,128)(2,1)S(1)}, u32[]{:S(2)}, u32[]{:S(2)}) collective-permute-start(bf16[512,384]{1,0:T(8,128)(2,1)S(1)} %get-tuple-element.6), channel_id=1, source_target_pairs={{0,4},{2,6},{4,0},{6,2},{1,5},{3,7},{5,1},{7,3},{8,12},{10,14},{12... | collective-permute-start | bytes 1179656 | tf_op jit(solution)/shard_map/ppermute | solution.py:32
  147.8 15.1 %collective-permute-start.26 = (bf16[512,384]{1,0:T(8,128)(2,1)S(1)}, bf16[512,384]{1,0:T(8,128)(2,1)S(1)}, u32[]{:S(2)}, u32[]{:S(2)}) collective-permute-start(bf16[512,384]{1,0:T(8,128)(2,1)S(1)} %get-tuple-element.6), channel_id=1, source_target_pairs={{0,6},{2,0},{4,2},{6,4},{1,7},{3,1},{5,3},{7,5},{8,14},{10,8},{12,... | collective-permute-start | bytes 1179656 | tf_op jit(solution)/shard_map/ppermute | solution.py:32
  165.7 13.0 %collective-permute-start.31 = (bf16[128,1536]{1,0:T(8,128)(2,1)S(1)}, bf16[128,1536]{1,0:T(8,128)(2,1)S(1)}, u32[]{:S(2)}, u32[]{:S(2)}) collective-permute-start(bf16[128,1536]{1,0:T(8,128)(2,1)S(1)} %get-tuple-element.15), channel_id=1, source_target_pairs={{0,17},{16,0},{1,16},{17,1},{2,19},{18,2},{3,18},{19,3},{4,21},{20... | collective-permute-start | bytes 1179656 | tf_op jit(solution)/shard_map/ppermute | solution.py:32
  171.3 11.1 %collective-permute-start.30 = (bf16[128,1536]{1,0:T(8,128)(2,1)S(1)}, bf16[128,1536]{1,0:T(8,128)(2,1)S(1)}, u32[]{:S(2)}, u32[]{:S(2)}) collective-permute-start(bf16[128,1536]{1,0:T(8,128)(2,1)S(1)} %get-tuple-element.16), channel_id=1, source_target_pairs={{0,16},{16,1},{1,17},{17,0},{2,18},{18,3},{3,19},{19,2},{4,20},{20... | collective-permute-start | bytes 1179656 | tf_op jit(solution)/shard_map/ppermute | solution.py:32
  171.3 17.3 %collective-permute-start.29 = (bf16[128,1536]{1,0:T(8,128)(2,1)S(1)}, bf16[128,1536]{1,0:T(8,128)(2,1)S(1)}, u32[]{:S(2)}, u32[]{:S(2)}) collective-permute-start(bf16[128,1536]{1,0:T(8,128)(2,1)S(1)} %get-tuple-element.14), channel_id=1, source_target_pairs={{0,1},{16,17},{1,0},{17,16},{2,3},{18,19},{3,2},{19,18},{4,5},{20,... | collective-permute-start | bytes 1179656 | tf_op jit(solution)/shard_map/ppermute | solution.py:32
  188.8 12.8 %collective-permute-start.34 = (bf16[128,1536]{1,0:T(8,128)(2,1)S(1)}, bf16[128,1536]{1,0:T(8,128)(2,1)S(1)}, u32[]{:S(2)}, u32[]{:S(2)}) collective-permute-start(bf16[128,1536]{1,0:T(8,128)(2,1)S(1)} %add_convert_fusion), channel_id=1, source_target_pairs={{0,32},{32,64},{64,96},{96,0},{1,33},{33,65},{65,97},{97,1},{2,34}... | collective-permute-start | bytes 1179656 | tf_op jit(solution)/shard_map/ppermute | solution.py:32
  190.5 20.5 %collective-permute-start.33 = (bf16[128,1536]{1,0:T(8,128)(2,1)S(1)}, bf16[128,1536]{1,0:T(8,128)(2,1)S(1)}, u32[]{:S(2)}, u32[]{:S(2)}) collective-permute-start(bf16[128,1536]{1,0:T(8,128)(2,1)S(1)} %add_convert_fusion), channel_id=1, source_target_pairs={{0,64},{32,96},{64,0},{96,32},{1,65},{33,97},{65,1},{97,33},{2,66}... | collective-permute-start | bytes 1179656 | tf_op jit(solution)/shard_map/ppermute | solution.py:32
  196.1 16.5 %collective-permute-start.32 = (bf16[128,1536]{1,0:T(8,128)(2,1)S(1)}, bf16[128,1536]{1,0:T(8,128)(2,1)S(1)}, u32[]{:S(2)}, u32[]{:S(2)}) collective-permute-start(bf16[128,1536]{1,0:T(8,128)(2,1)S(1)} %add_convert_fusion), channel_id=1, source_target_pairs={{0,96},{32,0},{64,32},{96,64},{1,97},{33,1},{65,33},{97,65},{2,98}... | collective-permute-start | bytes 1179656 | tf_op jit(solution)/shard_map/ppermute | solution.py:32
  221.1 10.4 %collective-permute-start.38 = (bf16[256,768]{1,0:T(8,128)(2,1)S(1)}, bf16[256,768]{1,0:T(8,128)(2,1)S(1)}, u32[]{:S(2)}, u32[]{:S(2)}) collective-permute-start(bf16[256,768]{1,0:T(8,128)(2,1)S(1)} %get-tuple-element.13), channel_id=1, source_target_pairs={{0,17},{16,0},{1,16},{17,1},{2,19},{18,2},{3,18},{19,3},{4,21},{20... | collective-permute-start | bytes 1179656 | tf_op jit(solution)/shard_map/ppermute | solution.py:32
  221.2 20.0 %collective-permute-start.37 = (bf16[256,768]{1,0:T(8,128)(2,1)S(1)}, bf16[256,768]{1,0:T(8,128)(2,1)S(1)}, u32[]{:S(2)}, u32[]{:S(2)}) collective-permute-start(bf16[256,768]{1,0:T(8,128)(2,1)S(1)} %get-tuple-element.12), channel_id=1, source_target_pairs={{0,16},{16,1},{1,17},{17,0},{2,18},{18,3},{3,19},{19,2},{4,20},{20... | collective-permute-start | bytes 1179656 | tf_op jit(solution)/shard_map/ppermute | solution.py:32
  222.6 18.6 %collective-permute-start.36 = (bf16[256,768]{1,0:T(8,128)(2,1)S(1)}, bf16[256,768]{1,0:T(8,128)(2,1)S(1)}, u32[]{:S(2)}, u32[]{:S(2)}) collective-permute-start(bf16[256,768]{1,0:T(8,128)(2,1)S(1)} %get-tuple-element.11), channel_id=1, source_target_pairs={{0,1},{16,17},{1,0},{17,16},{2,3},{18,19},{3,2},{19,18},{4,5},{20,... | collective-permute-start | bytes 1179656 | tf_op jit(solution)/shard_map/ppermute | solution.py:32
  (16 other events, 162.8 us)

commit v2 on v1

v2 whole, which is shorter than its diff:
```python
import jax
import jax.numpy as jnp
import numpy as np
from jax import lax
from jax.sharding import Mesh, PartitionSpec as P

first_beta = 0.9
second_beta = 0.95
first_bias = 1.0 - 0.9**20
second_bias = 1.0 - 0.95**20
epsilon = 1e-08
learn_rate = 0.2
weight_decay = 0.1

AXES = ("y", "xl", "c", "z", "xh")
SIZES = (4, 2, 2, 4, 2)
RING = {"x": (("xl", "xh"), (0, 2, 1, 3)), "y": ("y", range(4)), "z": ("z", range(4))}
HALVES = 2
ROWS = 128 // HALVES
low = jnp.bfloat16
wide = jnp.float32


def dot(left, right, left_dim, right_dim):
    return lax.dot_general(
        left, right, (((left_dim,), (right_dim,)), ((), ())), preferred_element_type=jnp.float32
    )


def shift(value, axis, by):
    names, place = RING[axis]
    return lax.ppermute(value, names, [(place[i], place[(i + by) % 4]) for i in range(4)])


def swap(value, axis):
    return lax.ppermute(value, axis, [(0, 1), (1, 0)])


def move(value, target):
    pairs = []
    for source in range(128):
        place = target(*np.unravel_index(source, SIZES))
        pairs.append((source, int(np.ravel_multi_index(place, SIZES))))
    return lax.ppermute(value, AXES, pairs)


def after(value, token):
    return lax.optimization_barrier((value, token))[0]


def near(value, axis):
    with jax.named_scope("gather_" + axis):
        return shift(value, axis, -1), shift(value, axis, 1)


def far(value, axis):
    with jax.named_scope("gather_" + axis):
        return shift(value, axis, 2)


def gather(value, axis):
    one, three = near(value, axis)
    return [value, one, far(value, axis), three]


def reduce(parts, axis):
    with jax.named_scope("reduce_" + axis):
        two = shift(parts[2], axis, 2)
        one, three = shift(parts[1], axis, 1), shift(parts[3], axis, -1)
    return (parts[0].astype(wide) + two.astype(wide)) + (one.astype(wide) + three.astype(wide))


def pick(test, first, second):
    return lax.select(jnp.broadcast_to(test, first.shape), first, second)


def turned(array):
    half = array.shape[1] // 2
    return jnp.concatenate([array[:, half:], array[:, :half]], axis=1)


def rotate(blocks, by):
    odd, two = by % 2 == 1, by // 2 == 1
    blocks = [pick(odd, blocks[(d + 1) % 4], blocks[d]) for d in range(4)]
    return [pick(two, blocks[(d + 2) % 4], blocks[d]) for d in range(4)]


def on_device(grad, weight, exp_avg, exp_avg_sq, left_basis, right_basis):
    y, xl, c, z, xh = (lax.axis_index(name) for name in AXES)
    x = 2 * xh + xl
    lo = xl == 0

    def columns_of(array, block):
        return pick(block == 0, array[:, :384], array[:, 384:])

    blocks = left_basis.reshape(256, 2, 2, 128)
    sub0, sub1 = blocks[:, :, 0].reshape(256, 256), blocks[:, :, 1].reshape(256, 256)
    left_came = swap(pick(lo, sub1, sub0), "xl")
    left_part = jnp.concatenate([pick(lo, sub0, sub1), left_came], axis=0)

    right_part = move(right_basis, lambda y, xl, c, z, xh: (y, c, xh, z, xl))

    grad_low = grad.astype(low)
    grad_near, left_near = near(grad_low, "x"), near(left_part, "z")
    grad_low, grad_near, left_part, left_near, right_part = lax.optimization_barrier(
        (grad_low, grad_near, left_part, left_near, right_part)
    )
    grad_far, left_far = far(grad_low, "x"), far(left_part, "z")
    right_near = near(right_part, "y")
    pair = jnp.concatenate([exp_avg, exp_avg_sq], axis=0)
    grad_far, left_far, right_part, right_near, pair = lax.optimization_barrier(
        (grad_far, left_far, right_part, right_near, pair)
    )
    right_far = far(right_part, "y")
    entering = swap(columns_of(pair, 1 - xl), "xl")

    beside = pick(lo, grad_near[0], grad_near[1])
    across = pick(lo, grad_near[1], grad_near[0])
    own_cols = jnp.concatenate([grad_low, beside], axis=0)
    other_cols = jnp.concatenate([grad_far, across], axis=0)
    ahead = xh == c
    grad_own = jnp.concatenate(
        [pick(ahead, own_cols, other_cols), pick(ahead, other_cols, own_cols)], axis=1
    )
    grad_other = turned(swap(grad_own, "c"))

    left_parts = rotate([left_part, left_near[0], left_far, left_near[1]], (y - z + 4) % 4)
    cores = [[p[:, :128] for p in left_parts], [p[:, 128:] for p in left_parts]]

    def columns(parts):
        return jnp.concatenate(
            [p[:, h * ROWS : (h + 1) * ROWS] for h in range(HALVES) for p in parts], axis=1
        )

    first, second = columns(cores[0]), columns(cores[1])
    left_own = pick(c == 0, first, second)
    left_other = pick(c == 0, second, first)
    left_swapped = swap(left_other, "c")

    def right_halves():
        right_chunks = [right_part, right_near[0], right_far, right_near[1]]
        right_own = jnp.concatenate(rotate(right_chunks, (z - y + 4) % 4), axis=1)
        return right_own, swap(right_own, "c")

    staying = columns_of(pair, xl)

    def spread(start):
        rows = [
            array[start + 128 * half : start + 128 * (half + 1)]
            for array in (staying, entering)
            for half in range(2)
        ]
        return rotate(rows, (4 - x) % 4)

    def moments(avg, avg_sq, rotated):
        new_avg = first_beta * avg + (1.0 - first_beta) * rotated
        new_avg_sq = second_beta * avg_sq + (1.0 - second_beta) * rotated * rotated
        return new_avg, new_avg_sq

    rotated_blocks = [[] for _ in range(4)]
    update = None
    left_lows = []
    for h in range(HALVES):
        now = slice(h * 4 * ROWS, (h + 1) * 4 * ROWS)
        part = dot(left_own[:, now], grad_own, 0, 0) + dot(left_swapped[:, now], grad_other, 0, 0)
        part = part.astype(low)
        parts = [part[d * ROWS : (d + 1) * ROWS] for d in range(4)]
        left_lows.append(reduce(parts, "y").astype(low))
    right_far, entering = after((right_far, entering), left_lows[0])
    right_own, right_other = right_halves()
    avg_blocks, sq_blocks = spread(0), spread(256)

    for h in range(HALVES):
        span = slice(h * ROWS, (h + 1) * ROWS)
        wide_span = slice(h * 4 * ROWS, (h + 1) * 4 * ROWS)
        left_low = left_lows[h]
        left_rows = jnp.concatenate(gather(left_low, "x"), axis=0)
        part = dot(left_rows[:, :768], right_own, 1, 0) + dot(left_rows[:, 768:], right_other, 1, 0)
        part = part.astype(low)
        rotated = reduce([part[:, d * 384 : (d + 1) * 384] for d in range(4)], "z")
        for d in range(4):
            rotated_blocks[d].append(rotated[d * ROWS : (d + 1) * ROWS])
        new_avg, new_avg_sq = moments(
            jnp.concatenate([b[span] for b in avg_blocks], axis=0),
            jnp.concatenate([b[span] for b in sq_blocks], axis=0),
            rotated,
        )
        step = (new_avg / first_bias / (jnp.sqrt(new_avg_sq / second_bias) + epsilon)).astype(low)
        step_rows = jnp.concatenate(gather(step, "z"), axis=1)
        part = [dot(step_rows, right, 1, 1).astype(low) for right in (right_own, right_other)]
        part = jnp.concatenate(part, axis=1)
        back = reduce([part[d * ROWS : (d + 1) * ROWS] for d in range(4)], "x").astype(low)
        back_own = jnp.concatenate(gather(back, "y"), axis=0)
        term = dot(left_own[:, wide_span], back_own, 1, 0)
        term = term + dot(left_other[:, wide_span], turned(swap(back_own, "c")), 1, 0)
        update = term if update is None else update + term

    update_low = update.astype(low)

    def block(rows, test):
        strip = update_low[rows * 256 : (rows + 1) * 256]
        return pick(test, strip[:, :768], strip[:, 768:])

    straight = lo == ahead
    total = reduce(
        [block(0, ahead), block(1, straight), block(0, ~ahead), block(1, ~straight)], "x"
    )
    new_weight = weight - learn_rate * (total + weight_decay * weight)

    rows = [jnp.concatenate(b, axis=0).astype(low) for b in rotated_blocks]
    rows = rotate(rows, x)
    kept = jnp.concatenate(rows[:2], axis=0)
    came = swap(jnp.concatenate(rows[2:], axis=0), "xl")
    rotated = jnp.concatenate([pick(lo, kept, came), pick(lo, came, kept)], axis=1).astype(wide)
    new_avg, new_avg_sq = moments(exp_avg, exp_avg_sq, rotated)
    return (new_weight, new_avg, new_avg_sq)


def solution(mesh):
    grid = Mesh(np.asarray(mesh.devices).reshape(SIZES), AXES)
    row, col = ("y", "xl", "c"), ("z", "xh")
    placed = (P(row, col),) * 5 + (P(col, row),)
    return jax.shard_map(
        on_device,
        mesh=grid,
        in_specs=placed,
        out_specs=(P(row, col),) * 3,
        check_vma=False,
    )
```

time: 244 us -> 198 us (0.81)
  waiting for transfers between devices: 145 us -> 91.1 us
  starting transfers between devices: 69 us -> 84.8 us
  other arithmetic: 13.7 us -> 7.36 us
    ppermute x30 -> x48, waiting for transfers between devices: 136 us -> 78.3 us  [shift(): lax.ppermute(value, names, [(place[i], place[(i + by) % 4]) for i in rang...]
    ppermute x30 -> x48, starting transfers between devices: 45 us -> 65.9 us  [shift(): lax.ppermute(value, names, [(place[i], place[(i + by) % 4]) for i in rang...]
    ppermute x7 -> x8, waiting for transfers between devices: 2.87 us -> 12.8 us  [swap(): return lax.ppermute(value, axis, [(0, 1), (1, 0)])]
    ppermute x3 -> x1, starting transfers between devices: 12.5 us -> 4.64 us  [move(): return lax.ppermute(value, AXES, pairs)]
    ppermute x3 -> x1, waiting for transfers between devices: 5.84 us -> 0.01 us  [move(): return lax.ppermute(value, AXES, pairs)]
    select_n x15 -> x12, other arithmetic: 6.55 us -> 2.65 us  [pick(): return lax.select(jnp.broadcast_to(test, first.shape), first, second)]
    ppermute x7 -> x8, starting transfers between devices: 11.5 us -> 14.2 us  [swap(): return lax.ppermute(value, axis, [(0, 1), (1, 0)])]
    dot_general x5 -> x16, matrix products: 12.3 us -> 11.2 us  [dot(): lax.dot_general(left, right, (((left_dim,), (right_dim,)), ((), ())), pre...]
  transfers between devices with their start and end apart: 40 -> 57, of which waited for: 28 -> 25; matrix products, arithmetic and copies ran while one was open for 9% -> 9% of each run, Pallas kernels for 0% -> 0%
where the time goes in v2:
time: 198 us
  waiting for transfers between devices  91.1 us (46%)
  starting transfers between devices  84.8 us (43%)
  matrix products  11.2 us (6%)
  other arithmetic  7.36 us (4%)
  local copies, waits for them, and re-layouts  2.53 us (1%)
    ppermute x48, waiting for transfers between devices, shift(): lax.ppermute(value, names, [(place[i], place[(i + by) % 4]) for i in rang...  78.3 us
    ppermute x48, starting transfers between devices, shift(): lax.ppermute(value, names, [(place[i], place[(i + by) % 4]) for i in rang...  65.9 us
    ppermute x8, starting transfers between devices, swap(): return lax.ppermute(value, axis, [(0, 1), (1, 0)])  14.2 us
    ppermute x8, waiting for transfers between devices, swap(): return lax.ppermute(value, axis, [(0, 1), (1, 0)])  12.8 us
    dot_general x16, matrix products, dot(): lax.dot_general(left, right, (((left_dim,), (right_dim,)), ((), ())), pre...  11.2 us
    ppermute x1, starting transfers between devices, move(): return lax.ppermute(value, AXES, pairs)  4.64 us
  transfers between devices with their start and end apart: 57, of which 25 were waited for; matrix products, arithmetic and copies ran while one was open for 9% of the time, Pallas kernels for 0%

profile of v2, /device:TPU:1, one launch (start us, length us, event | category | flops | bytes accessed | tf_op | source)
XLA Modules:
  0.0 198.3 jit_solution(15993828459754641274)
XLA Ops:
  0.7 4.6 %collective-permute-start.5 = (bf16[768,384]{1,0:T(8,128)(2,1)}, bf16[768,384]{1,0:T(8,128)(2,1)S(1)}, u32[]{:S(2)}, u32[]{:S(2)}) collective-permute-start(bf16[768,384]{1,0:T(8,128)(2,1)} %param.11), channel_id=1, source_target_pairs={{0,0},{1,8},{2,2},{3,10},{4,4},{5,12},{6,6},{7,14},{8,16},{9,24},{... | collective-permute-start | bytes 1769480 | tf_op jit(solution)/shard_map/ppermute | solution.py:44
  6.4 1.9 collective-permute-start.2
  8.5 2.7 %collective-permute-start = (bf16[256,768]{1,0:T(8,128)(2,1)S(1)}, bf16[256,768]{1,0:T(8,128)(2,1)S(1)}, u32[]{:S(2)}, u32[]{:S(2)}) collective-permute-start(bf16[256,768]{1,0:T(8,128)(2,1)S(1)} %convert_element_type.139), channel_id=1, source_target_pairs={{0,17},{16,0},{1,16},{17,1},{2,19},{18,2},{3,18},{19,3},{4,21},{20... | collective-permute-start | bytes 1179656 | tf_op jit(solution)/shard_map/gather_x/ppermute | solution.py:32
  11.2 10.8 %collective-permute-done.2 = bf16[256,256]{0,1:T(8,128)(2,1)S(1)} collective-permute-done((bf16[256,256]{0,1:T(8,128)(2,1)S(1)}, bf16[256,256]{0,1:T(8,128)(2,1)S(1)}, u32[]{:S(2)}, u32[]{:S(2)}) %collective-permute-start.2) | collective-permute-done | bytes 131104 | tf_op jit(solution)/shard_map/ppermute | solution.py:36
  23.7 2.2 %collective-permute-start.3 = (bf16[512,256]{0,1:T(8,128)(2,1)S(1)}, bf16[512,256]{0,1:T(8,128)(2,1)S(1)}, u32[]{:S(2)}, u32[]{:S(2)}) collective-permute-start(bf16[512,256]{0,1:T(8,128)(2,1)S(1)} %pad_maximum_fusion.15), channel_id=1, source_target_pairs={{0,6},{2,0},{4,2},{6,4},{1,7},{3,1},{5,3},{7,5},{8,14},{10,8},{12,... | collective-permute-start | bytes 786440 | tf_op jit(solution)/shard_map/gather_z/ppermute | solution.py:32
  25.9 3.7 %collective-permute-done.4 = bf16[512,256]{0,1:T(8,128)(2,1)S(1)} collective-permute-done((bf16[512,256]{0,1:T(8,128)(2,1)S(1)}, bf16[512,256]{0,1:T(8,128)(2,1)S(1)}, u32[]{:S(2)}, u32[]{:S(2)}) %collective-permute-start.4) | collective-permute-done | bytes 262176 | tf_op jit(solution)/shard_map/gather_z/ppermute | solution.py:32
  33.2 2.7 %collective-permute-start.7 = (bf16[512,256]{0,1:T(8,128)(2,1)S(1)}, bf16[512,256]{0,1:T(8,128)(2,1)S(1)}, u32[]{:S(2)}, u32[]{:S(2)}) collective-permute-start(bf16[512,256]{0,1:T(8,128)(2,1)S(1)} %pad_maximum_fusion.15), channel_id=1, source_target_pairs={{0,4},{2,6},{4,0},{6,2},{1,5},{3,7},{5,1},{7,3},{8,12},{10,14},{12... | collective-permute-start | bytes 786440 | tf_op jit(solution)/shard_map/gather_z/ppermute | solution.py:32
  36.1 4.3 %collective-permute-done.7 = bf16[512,256]{0,1:T(8,128)(2,1)S(1)} collective-permute-done((bf16[512,256]{0,1:T(8,128)(2,1)S(1)}, bf16[512,256]{0,1:T(8,128)(2,1)S(1)}, u32[]{:S(2)}, u32[]{:S(2)}) %collective-permute-start.7) | collective-permute-done | bytes 262176 | tf_op jit(solution)/shard_map/gather_z/ppermute | solution.py:32
  40.3 5.3 %collective-permute-done.6 = bf16[256,768]{1,0:T(8,128)(2,1)S(1)} collective-permute-done((bf16[256,768]{1,0:T(8,128)(2,1)S(1)}, bf16[256,768]{1,0:T(8,128)(2,1)S(1)}, u32[]{:S(2)}, u32[]{:S(2)}) %collective-permute-start.6) | collective-permute-done | bytes 393248 | tf_op jit(solution)/shard_map/gather_x/ppermute | solution.py:32
  56.7 9.1 %collective-permute-done.14 = bf16[64,1536]{1,0:T(8,128)(2,1)S(1)} collective-permute-done((bf16[64,1536]{1,0:T(8,128)(2,1)S(1)}, bf16[64,1536]{1,0:T(8,128)(2,1)S(1)}, u32[]{:S(2)}, u32[]{:S(2)}) %collective-permute-start.14) | collective-permute-done | bytes 196640 | tf_op jit(solution)/shard_map/reduce_y/ppermute | solution.py:32
  69.1 3.9 %collective-permute-start.36 = (bf16[64,1536]{1,0:T(8,128)(2,1)S(1)}, bf16[64,1536]{1,0:T(8,128)(2,1)S(1)}, u32[]{:S(2)}, u32[]{:S(2)}) collective-permute-start(bf16[64,1536]{1,0:T(8,128)(2,1)S(1)} %get-tuple-element.81), channel_id=1, source_target_pairs={{0,96},{32,0},{64,32},{96,64},{1,97},{33,1},{65,33},{97,65},{2,98}... | collective-permute-start | bytes 589832 | tf_op jit(solution)/shard_map/reduce_y/ppermute | solution.py:32
  80.5 3.2 %collective-permute-done.19 = bf16[64,1536]{1,0:T(8,128)(2,1)S(1)} collective-permute-done((bf16[64,1536]{1,0:T(8,128)(2,1)S(1)}, bf16[64,1536]{1,0:T(8,128)(2,1)S(1)}, u32[]{:S(2)}, u32[]{:S(2)}) %collective-permute-start.19) | collective-permute-done | bytes 196640 | tf_op jit(solution)/shard_map/gather_x/ppermute | solution.py:32
  84.8 5.9 %collective-permute-done.39 = bf16[64,1536]{1,0:T(8,128)(2,1)S(1)} collective-permute-done((bf16[64,1536]{1,0:T(8,128)(2,1)S(1)}, bf16[64,1536]{1,0:T(8,128)(2,1)S(1)}, u32[]{:S(2)}, u32[]{:S(2)}) %collective-permute-start.39) | collective-permute-done | bytes 196640 | tf_op jit(solution)/shard_map/gather_x/ppermute | solution.py:32
  90.7 2.2 %collective-permute-done.37 = bf16[64,1536]{1,0:T(8,128)(2,1)S(1)} collective-permute-done((bf16[64,1536]{1,0:T(8,128)(2,1)S(1)}, bf16[64,1536]{1,0:T(8,128)(2,1)S(1)}, u32[]{:S(2)}, u32[]{:S(2)}) %collective-permute-start.37) | collective-permute-done | bytes 196640 | tf_op jit(solution)/shard_map/gather_x/ppermute | solution.py:32
  94.7 2.8 %collective-permute-start.40 = (bf16[256,384]{1,0:T(8,128)(2,1)S(1)}, bf16[256,384]{1,0:T(8,128)(2,1)S(1)}, u32[]{:S(2)}, u32[]{:S(2)}) collective-permute-start(bf16[256,384]{1,0:T(8,128)(2,1)S(1)} %get-tuple-element.77), channel_id=1, source_target_pairs={{0,4},{2,6},{4,0},{6,2},{1,5},{3,7},{5,1},{7,3},{8,12},{10,14},{12... | collective-permute-start | bytes 589832 | tf_op jit(solution)/shard_map/reduce_z/ppermute | solution.py:32
  101.7 2.1 %collective-permute-start.23 = (bf16[256,384]{1,0:T(8,128)(2,1)S(1)}, bf16[256,384]{1,0:T(8,128)(2,1)S(1)}, u32[]{:S(2)}, u32[]{:S(2)}) collective-permute-start(bf16[256,384]{1,0:T(8,128)(2,1)S(1)} %get-tuple-element.70), channel_id=1, source_target_pairs={{0,6},{2,0},{4,2},{6,4},{1,7},{3,1},{5,3},{7,5},{8,14},{10,8},{12,... | collective-permute-start | bytes 589832 | tf_op jit(solution)/shard_map/reduce_z/ppermute | solution.py:32
  103.7 3.1 %collective-permute-done.42 = bf16[256,384]{1,0:T(8,128)(2,1)S(1)} collective-permute-done((bf16[256,384]{1,0:T(8,128)(2,1)S(1)}, bf16[256,384]{1,0:T(8,128)(2,1)S(1)}, u32[]{:S(2)}, u32[]{:S(2)}) %collective-permute-start.42) | collective-permute-done | bytes 196640 | tf_op jit(solution)/shard_map/reduce_z/ppermute | solution.py:32
  109.6 2.8 %collective-permute-start.44 = (bf16[256,384]{1,0:T(8,128)(2,1)S(1)}, bf16[256,384]{1,0:T(8,128)(2,1)S(1)}, u32[]{:S(2)}, u32[]{:S(2)}) collective-permute-start(bf16[256,384]{1,0:T(8,128)(2,1)S(1)} %get-tuple-element.57), channel_id=1, source_target_pairs={{0,4},{2,6},{4,0},{6,2},{1,5},{3,7},{5,1},{7,3},{8,12},{10,14},{12... | collective-permute-start | bytes 589832 | tf_op jit(solution)/shard_map/gather_z/ppermute | solution.py:32
  112.4 2.9 %collective-permute-done.23 = bf16[256,384]{1,0:T(8,128)(2,1)S(1)} collective-permute-done((bf16[256,384]{1,0:T(8,128)(2,1)S(1)}, bf16[256,384]{1,0:T(8,128)(2,1)S(1)}, u32[]{:S(2)}, u32[]{:S(2)}) %collective-permute-start.23) | collective-permute-done | bytes 196640 | tf_op jit(solution)/shard_map/reduce_z/ppermute | solution.py:32
  117.5 3.3 %collective-permute-start.25 = (bf16[256,384]{1,0:T(8,128)(2,1)S(1)}, bf16[256,384]{1,0:T(8,128)(2,1)S(1)}, u32[]{:S(2)}, u32[]{:S(2)}) collective-permute-start(bf16[256,384]{1,0:T(8,128)(2,1)S(1)} %get-tuple-element.55), channel_id=1, source_target_pairs={{0,4},{2,6},{4,0},{6,2},{1,5},{3,7},{5,1},{7,3},{8,12},{10,14},{12... | collective-permute-start | bytes 589832 | tf_op jit(solution)/shard_map/gather_z/ppermute | solution.py:32
  120.9 8.6 %collective-permute-done.26 = bf16[256,384]{1,0:T(8,128)(2,1)S(1)} collective-permute-done((bf16[256,384]{1,0:T(8,128)(2,1)S(1)}, bf16[256,384]{1,0:T(8,128)(2,1)S(1)}, u32[]{:S(2)}, u32[]{:S(2)}) %collective-permute-start.26) | collective-permute-done | bytes 196640 | tf_op jit(solution)/shard_map/gather_z/ppermute | solution.py:32
  132.6 5.1 %collective-permute-start.29 = (bf16[64,1536]{1,0:T(8,128)(2,1)S(1)}, bf16[64,1536]{1,0:T(8,128)(2,1)S(1)}, u32[]{:S(2)}, u32[]{:S(2)}) collective-permute-start(bf16[64,1536]{1,0:T(8,128)(2,1)S(1)} %get-tuple-element.67), channel_id=1, source_target_pairs={{0,17},{16,0},{1,16},{17,1},{2,19},{18,2},{3,18},{19,3},{4,21},{20... | collective-permute-start | bytes 589832 | tf_op jit(solution)/shard_map/reduce_x/ppermute | solution.py:32
  140.7 2.6 %collective-permute-start.48 = (bf16[64,1536]{1,0:T(8,128)(2,1)S(1)}, bf16[64,1536]{1,0:T(8,128)(2,1)S(1)}, u32[]{:S(2)}, u32[]{:S(2)}) collective-permute-start(bf16[64,1536]{1,0:T(8,128)(2,1)S(1)} %get-tuple-element.75), channel_id=1, source_target_pairs={{0,17},{16,0},{1,16},{17,1},{2,19},{18,2},{3,18},{19,3},{4,21},{20... | collective-permute-start | bytes 589832 | tf_op jit(solution)/shard_map/reduce_x/ppermute | solution.py:32
  143.3 3.7 %collective-permute-done.29 = bf16[64,1536]{1,0:T(8,128)(2,1)S(1)} collective-permute-done((bf16[64,1536]{1,0:T(8,128)(2,1)S(1)}, bf16[64,1536]{1,0:T(8,128)(2,1)S(1)}, u32[]{:S(2)}, u32[]{:S(2)}) %collective-permute-start.29) | collective-permute-done | bytes 196640 | tf_op jit(solution)/shard_map/reduce_x/ppermute | solution.py:32
  148.5 2.4 %collective-permute-start.31 = (bf16[64,1536]{1,0:T(8,128)(2,1)S(1)}, bf16[64,1536]{1,0:T(8,128)(2,1)S(1)}, u32[]{:S(2)}, u32[]{:S(2)}) collective-permute-start(bf16[64,1536]{1,0:T(8,128)(2,1)S(1)} %add_convert_fusion.2), channel_id=1, source_target_pairs={{0,64},{32,96},{64,0},{96,32},{1,65},{33,97},{65,1},{97,33},{2,66}... | collective-permute-start | bytes 589832 | tf_op jit(solution)/shard_map/gather_y/ppermute | solution.py:32
  155.0 4.4 %collective-permute-start.50 = (bf16[64,1536]{1,0:T(8,128)(2,1)S(1)}, bf16[64,1536]{1,0:T(8,128)(2,1)S(1)}, u32[]{:S(2)}, u32[]{:S(2)}) collective-permute-start(bf16[64,1536]{1,0:T(8,128)(2,1)S(1)} %add_convert_fusion), channel_id=1, source_target_pairs={{0,64},{32,96},{64,0},{96,32},{1,65},{33,97},{65,1},{97,33},{2,66}... | collective-permute-start | bytes 589832 | tf_op jit(solution)/shard_map/gather_y/ppermute | solution.py:32
  159.5 6.7 %collective-permute-start.33 = (bf16[256,1536]{1,0:T(8,128)(2,1)S(1)}, bf16[256,1536]{1,0:T(8,128)(2,1)S(1)}, u32[]{:S(2)}, u32[]{:S(2)}) collective-permute-start(bf16[256,1536]{1,0:T(8,128)(2,1)S(1)} %pad_maximum_fusion.10), channel_id=1, source_target_pairs={{0,8},{8,0},{1,9},{9,1},{2,10},{10,2},{3,11},{11,3},{4,12},{12,4},... | collective-permute-start | bytes 2359304 | tf_op jit(solution)/shard_map/ppermute | solution.py:36
  166.3 3.0 %collective-permute-done.51 = bf16[64,1536]{1,0:T(8,128)(2,1)S(1)} collective-permute-done((bf16[64,1536]{1,0:T(8,128)(2,1)S(1)}, bf16[64,1536]{1,0:T(8,128)(2,1)S(1)}, u32[]{:S(2)}, u32[]{:S(2)}) %collective-permute-start.51) | collective-permute-done | bytes 196640 | tf_op jit(solution)/shard_map/gather_y/ppermute | solution.py:32
  175.0 2.7 %collective-permute-start.53 = (bf16[256,768]{1,0:T(8,128)(2,1)S(1)}, bf16[256,768]{1,0:T(8,128)(2,1)S(1)}, u32[]{:S(2)}, u32[]{:S(2)}) collective-permute-start(bf16[256,768]{1,0:T(8,128)(2,1)S(1)} %get-tuple-element.37), channel_id=1, source_target_pairs={{0,1},{16,17},{1,0},{17,16},{2,3},{18,19},{3,2},{19,18},{4,5},{20,... | collective-permute-start | bytes 1179656 | tf_op jit(solution)/shard_map/reduce_x/ppermute | solution.py:32
  178.1 2.2 %collective-permute-start.55 = (bf16[256,768]{1,0:T(8,128)(2,1)S(1)}, bf16[256,768]{1,0:T(8,128)(2,1)S(1)}, u32[]{:S(2)}, u32[]{:S(2)}) collective-permute-start(bf16[256,768]{1,0:T(8,128)(2,1)S(1)} %get-tuple-element.39), channel_id=1, source_target_pairs={{0,17},{16,0},{1,16},{17,1},{2,19},{18,2},{3,18},{19,3},{4,21},{20... | collective-permute-start | bytes 1179656 | tf_op jit(solution)/shard_map/reduce_x/ppermute | solution.py:32
  181.9 6.5 %collective-permute-done.53 = bf16[256,768]{1,0:T(8,128)(2,1)S(1)} collective-permute-done((bf16[256,768]{1,0:T(8,128)(2,1)S(1)}, bf16[256,768]{1,0:T(8,128)(2,1)S(1)}, u32[]{:S(2)}, u32[]{:S(2)}) %collective-permute-start.53) | collective-permute-done | bytes 393248 | tf_op jit(solution)/shard_map/reduce_x/ppermute | solution.py:32
  188.3 8.7 %collective-permute-done.54 = bf16[256,768]{1,0:T(8,128)(2,1)S(1)} collective-permute-done((bf16[256,768]{1,0:T(8,128)(2,1)S(1)}, bf16[256,768]{1,0:T(8,128)(2,1)S(1)}, u32[]{:S(2)}, u32[]{:S(2)}) %collective-permute-start.54) | collective-permute-done | bytes 393248 | tf_op jit(solution)/shard_map/reduce_x/ppermute | solution.py:32
  (169 shorter events, 60.9 us)
Async XLA Ops:
  0.7 28.9 %collective-permute-start.5 = (bf16[768,384]{1,0:T(8,128)(2,1)}, bf16[768,384]{1,0:T(8,128)(2,1)S(1)}, u32[]{:S(2)}, u32[]{:S(2)}) collective-permute-start(bf16[768,384]{1,0:T(8,128)(2,1)} %param.11), channel_id=1, source_target_pairs={{0,0},{1,8},{2,2},{3,10},{4,4},{5,12},{6,6},{7,14},{8,16},{9,24},{... | collective-permute-start | bytes 1769480 | tf_op jit(solution)/shard_map/ppermute | solution.py:44
  6.4 15.5 %collective-permute-start.2 = (bf16[256,256]{0,1:T(8,128)(2,1)S(1)}, bf16[256,256]{0,1:T(8,128)(2,1)S(1)}, u32[]{:S(2)}, u32[]{:S(2)}) collective-permute-start(bf16[256,256]{0,1:T(8,128)(2,1)S(1)} %bitcast.13), channel_id=1, source_target_pairs={{0,16},{16,0},{1,17},{17,1},{2,18},{18,2},{3,19},{19,3},{4,20},{20... | collective-permute-start | bytes 393224 | tf_op jit(solution)/shard_map/ppermute | solution.py:36
  8.4 21.1 %collective-permute-start.1 = (bf16[256,768]{1,0:T(8,128)(2,1)S(1)}, bf16[256,768]{1,0:T(8,128)(2,1)S(1)}, u32[]{:S(2)}, u32[]{:S(2)}) collective-permute-start(bf16[256,768]{1,0:T(8,128)(2,1)S(1)} %convert_element_type.139), channel_id=1, source_target_pairs={{0,16},{16,1},{1,17},{17,0},{2,18},{18,3},{3,19},{19,2},{4,20},{20... | collective-permute-start | bytes 1179656 | tf_op jit(solution)/shard_map/gather_x/ppermute | solution.py:32
  8.5 21.0 %collective-permute-start = (bf16[256,768]{1,0:T(8,128)(2,1)S(1)}, bf16[256,768]{1,0:T(8,128)(2,1)S(1)}, u32[]{:S(2)}, u32[]{:S(2)}) collective-permute-start(bf16[256,768]{1,0:T(8,128)(2,1)S(1)} %convert_element_type.139), channel_id=1, source_target_pairs={{0,17},{16,0},{1,16},{17,1},{2,19},{18,2},{3,18},{19,3},{4,21},{20... | collective-permute-start | bytes 1179656 | tf_op jit(solution)/shard_map/gather_x/ppermute | solution.py:32
  30.3 15.3 %collective-permute-start.9 = (bf16[768,384]{1,0:T(8,128)(2,1)S(1)}, bf16[768,384]{1,0:T(8,128)(2,1)}, u32[]{:S(2)}, u32[]{:S(2)}) collective-permute-start(bf16[768,384]{1,0:T(8,128)(2,1)S(1)} %collective-permute-done.5), channel_id=1, source_target_pairs={{0,32},{32,64},{64,96},{96,0},{1,33},{33,65},{65,97},{97,1},{2,34}... | collective-permute-start | bytes 1769480 | tf_op jit(solution)/shard_map/gather_y/ppermute | solution.py:32
  31.6 14.0 %collective-permute-start.8 = (bf16[768,384]{1,0:T(8,128)(2,1)S(1)}, bf16[768,384]{1,0:T(8,128)(2,1)}, u32[]{:S(2)}, u32[]{:S(2)}) collective-permute-start(bf16[768,384]{1,0:T(8,128)(2,1)S(1)} %collective-permute-done.5), channel_id=1, source_target_pairs={{0,96},{32,0},{64,32},{96,64},{1,97},{33,1},{65,33},{97,65},{2,98}... | collective-permute-start | bytes 1769480 | tf_op jit(solution)/shard_map/gather_y/ppermute | solution.py:32
  33.1 12.5 %collective-permute-start.6 = (bf16[256,768]{1,0:T(8,128)(2,1)S(1)}, bf16[256,768]{1,0:T(8,128)(2,1)S(1)}, u32[]{:S(2)}, u32[]{:S(2)}) collective-permute-start(bf16[256,768]{1,0:T(8,128)(2,1)S(1)} %convert_element_type.139), channel_id=1, source_target_pairs={{0,1},{16,17},{1,0},{17,16},{2,3},{18,19},{3,2},{19,18},{4,5},{20,... | collective-permute-start | bytes 1179656 | tf_op jit(solution)/shard_map/gather_x/ppermute | solution.py:32
  45.6 27.5 %collective-permute-start.10 = (bf16[768,384]{1,0:T(8,128)(2,1)S(1)}, bf16[768,384]{1,0:T(8,128)(2,1)S(1)}, u32[]{:S(2)}, u32[]{:S(2)}) collective-permute-start(bf16[768,384]{1,0:T(8,128)(2,1)S(1)} %collective-permute-done.5), channel_id=1, source_target_pairs={{0,64},{32,96},{64,0},{96,32},{1,65},{33,97},{65,1},{97,33},{2,66}... | collective-permute-start | bytes 1769480 | tf_op jit(solution)/shard_map/gather_y/ppermute | solution.py:32
  49.1 24.1 %collective-permute-start.11 = (f32[512,384]{1,0:T(8,128)S(1)}, f32[512,384]{1,0:T(8,128)S(1)}, u32[]{:S(2)}, u32[]{:S(2)}) collective-permute-start(f32[512,384]{1,0:T(8,128)S(1)} %get-tuple-element.49), channel_id=1, source_target_pairs={{0,16},{16,0},{1,17},{17,1},{2,18},{18,2},{3,19},{19,3},{4,20},{20... | collective-permute-start | bytes 2359304 | tf_op jit(solution)/shard_map/ppermute | solution.py:36
  53.1 12.7 %collective-permute-start.14 = (bf16[64,1536]{1,0:T(8,128)(2,1)S(1)}, bf16[64,1536]{1,0:T(8,128)(2,1)S(1)}, u32[]{:S(2)}, u32[]{:S(2)}) collective-permute-start(bf16[64,1536]{1,0:T(8,128)(2,1)S(1)} %get-tuple-element.83), channel_id=1, source_target_pairs={{0,64},{32,96},{64,0},{96,32},{1,65},{33,97},{65,1},{97,33},{2,66}... | collective-permute-start | bytes 589832 | tf_op jit(solution)/shard_map/reduce_y/ppermute | solution.py:32
  54.6 14.6 %collective-permute-start.16 = (bf16[64,1536]{1,0:T(8,128)(2,1)S(1)}, bf16[64,1536]{1,0:T(8,128)(2,1)S(1)}, u32[]{:S(2)}, u32[]{:S(2)}) collective-permute-start(bf16[64,1536]{1,0:T(8,128)(2,1)S(1)} %get-tuple-element.84), channel_id=1, source_target_pairs={{0,96},{32,0},{64,32},{96,64},{1,97},{33,1},{65,33},{97,65},{2,98}... | collective-permute-start | bytes 589832 | tf_op jit(solution)/shard_map/reduce_y/ppermute | solution.py:32
  56.0 17.0 %collective-permute-start.15 = (bf16[64,1536]{1,0:T(8,128)(2,1)S(1)}, bf16[64,1536]{1,0:T(8,128)(2,1)S(1)}, u32[]{:S(2)}, u32[]{:S(2)}) collective-permute-start(bf16[64,1536]{1,0:T(8,128)(2,1)S(1)} %get-tuple-element.85), channel_id=1, source_target_pairs={{0,32},{32,64},{64,96},{96,0},{1,33},{33,65},{65,97},{97,1},{2,34}... | collective-permute-start | bytes 589832 | tf_op jit(solution)/shard_map/reduce_y/ppermute | solution.py:32
  77.7 15.3 %collective-permute-start.20 = (bf16[768,1536]{1,0:T(8,128)(2,1)S(1)}, bf16[768,1536]{1,0:T(8,128)(2,1)S(1)}, u32[]{:S(2)}, u32[]{:S(2)}) collective-permute-start(bf16[768,1536]{1,0:T(8,128)(2,1)S(1)} %pad_maximum_fusion), channel_id=1, source_target_pairs={{0,8},{8,0},{1,9},{9,1},{2,10},{10,2},{3,11},{11,3},{4,12},{12,4},... | collective-permute-start | bytes 7077896 | tf_op jit(solution)/shard_map/ppermute | solution.py:36
  100.6 11.8 %collective-permute-start.21 = (bf16[256,384]{1,0:T(8,128)(2,1)S(1)}, bf16[256,384]{1,0:T(8,128)(2,1)S(1)}, u32[]{:S(2)}, u32[]{:S(2)}) collective-permute-start(bf16[256,384]{1,0:T(8,128)(2,1)S(1)} %get-tuple-element.69), channel_id=1, source_target_pairs={{0,4},{2,6},{4,0},{6,2},{1,5},{3,7},{5,1},{7,3},{8,12},{10,14},{12... | collective-permute-start | bytes 589832 | tf_op jit(solution)/shard_map/reduce_z/ppermute | solution.py:32
  101.7 13.6 %collective-permute-start.23 = (bf16[256,384]{1,0:T(8,128)(2,1)S(1)}, bf16[256,384]{1,0:T(8,128)(2,1)S(1)}, u32[]{:S(2)}, u32[]{:S(2)}) collective-permute-start(bf16[256,384]{1,0:T(8,128)(2,1)S(1)} %get-tuple-element.70), channel_id=1, source_target_pairs={{0,6},{2,0},{4,2},{6,4},{1,7},{3,1},{5,3},{7,5},{8,14},{10,8},{12,... | collective-permute-start | bytes 589832 | tf_op jit(solution)/shard_map/reduce_z/ppermute | solution.py:32
  103.7 11.5 %collective-permute-start.22 = (bf16[256,384]{1,0:T(8,128)(2,1)S(1)}, bf16[256,384]{1,0:T(8,128)(2,1)S(1)}, u32[]{:S(2)}, u32[]{:S(2)}) collective-permute-start(bf16[256,384]{1,0:T(8,128)(2,1)S(1)} %get-tuple-element.71), channel_id=1, source_target_pairs={{0,2},{2,4},{4,6},{6,0},{1,3},{3,5},{5,7},{7,1},{8,10},{10,12},{12... | collective-permute-start | bytes 589832 | tf_op jit(solution)/shard_map/reduce_z/ppermute | solution.py:32
  108.5 29.2 %collective-permute-start.45 = (bf16[256,384]{1,0:T(8,128)(2,1)S(1)}, bf16[256,384]{1,0:T(8,128)(2,1)S(1)}, u32[]{:S(2)}, u32[]{:S(2)}) collective-permute-start(bf16[256,384]{1,0:T(8,128)(2,1)S(1)} %get-tuple-element.57), channel_id=1, source_target_pairs={{0,2},{2,4},{4,6},{6,0},{1,3},{3,5},{5,7},{7,1},{8,10},{10,12},{12... | collective-permute-start | bytes 589832 | tf_op jit(solution)/shard_map/gather_z/ppermute | solution.py:32
  109.6 28.1 %collective-permute-start.44 = (bf16[256,384]{1,0:T(8,128)(2,1)S(1)}, bf16[256,384]{1,0:T(8,128)(2,1)S(1)}, u32[]{:S(2)}, u32[]{:S(2)}) collective-permute-start(bf16[256,384]{1,0:T(8,128)(2,1)S(1)} %get-tuple-element.57), channel_id=1, source_target_pairs={{0,4},{2,6},{4,0},{6,2},{1,5},{3,7},{5,1},{7,3},{8,12},{10,14},{12... | collective-permute-start | bytes 589832 | tf_op jit(solution)/shard_map/gather_z/ppermute | solution.py:32
  115.7 13.8 %collective-permute-start.26 = (bf16[256,384]{1,0:T(8,128)(2,1)S(1)}, bf16[256,384]{1,0:T(8,128)(2,1)S(1)}, u32[]{:S(2)}, u32[]{:S(2)}) collective-permute-start(bf16[256,384]{1,0:T(8,128)(2,1)S(1)} %get-tuple-element.55), channel_id=1, source_target_pairs={{0,2},{2,4},{4,6},{6,0},{1,3},{3,5},{5,7},{7,1},{8,10},{10,12},{12... | collective-permute-start | bytes 589832 | tf_op jit(solution)/shard_map/gather_z/ppermute | solution.py:32
  117.5 12.7 %collective-permute-start.25 = (bf16[256,384]{1,0:T(8,128)(2,1)S(1)}, bf16[256,384]{1,0:T(8,128)(2,1)S(1)}, u32[]{:S(2)}, u32[]{:S(2)}) collective-permute-start(bf16[256,384]{1,0:T(8,128)(2,1)S(1)} %get-tuple-element.55), channel_id=1, source_target_pairs={{0,4},{2,6},{4,0},{6,2},{1,5},{3,7},{5,1},{7,3},{8,12},{10,14},{12... | collective-permute-start | bytes 589832 | tf_op jit(solution)/shard_map/gather_z/ppermute | solution.py:32
  132.0 11.3 %collective-permute-start.27 = (bf16[64,1536]{1,0:T(8,128)(2,1)S(1)}, bf16[64,1536]{1,0:T(8,128)(2,1)S(1)}, u32[]{:S(2)}, u32[]{:S(2)}) collective-permute-start(bf16[64,1536]{1,0:T(8,128)(2,1)S(1)} %get-tuple-element.66), channel_id=1, source_target_pairs={{0,1},{16,17},{1,0},{17,16},{2,3},{18,19},{3,2},{19,18},{4,5},{20,... | collective-permute-start | bytes 589832 | tf_op jit(solution)/shard_map/reduce_x/ppermute | solution.py:32
  132.6 14.3 %collective-permute-start.29 = (bf16[64,1536]{1,0:T(8,128)(2,1)S(1)}, bf16[64,1536]{1,0:T(8,128)(2,1)S(1)}, u32[]{:S(2)}, u32[]{:S(2)}) collective-permute-start(bf16[64,1536]{1,0:T(8,128)(2,1)S(1)} %get-tuple-element.67), channel_id=1, source_target_pairs={{0,17},{16,0},{1,16},{17,1},{2,19},{18,2},{3,18},{19,3},{4,21},{20... | collective-permute-start | bytes 589832 | tf_op jit(solution)/shard_map/reduce_x/ppermute | solution.py:32
  139.4 11.6 %collective-permute-start.46 = (bf16[64,1536]{1,0:T(8,128)(2,1)S(1)}, bf16[64,1536]{1,0:T(8,128)(2,1)S(1)}, u32[]{:S(2)}, u32[]{:S(2)}) collective-permute-start(bf16[64,1536]{1,0:T(8,128)(2,1)S(1)} %get-tuple-element.74), channel_id=1, source_target_pairs={{0,1},{16,17},{1,0},{17,16},{2,3},{18,19},{3,2},{19,18},{4,5},{20,... | collective-permute-start | bytes 589832 | tf_op jit(solution)/shard_map/reduce_x/ppermute | solution.py:32
  140.7 13.0 %collective-permute-start.48 = (bf16[64,1536]{1,0:T(8,128)(2,1)S(1)}, bf16[64,1536]{1,0:T(8,128)(2,1)S(1)}, u32[]{:S(2)}, u32[]{:S(2)}) collective-permute-start(bf16[64,1536]{1,0:T(8,128)(2,1)S(1)} %get-tuple-element.75), channel_id=1, source_target_pairs={{0,17},{16,0},{1,16},{17,1},{2,19},{18,2},{3,18},{19,3},{4,21},{20... | collective-permute-start | bytes 589832 | tf_op jit(solution)/shard_map/reduce_x/ppermute | solution.py:32
  143.2 11.5 %collective-permute-start.47 = (bf16[64,1536]{1,0:T(8,128)(2,1)S(1)}, bf16[64,1536]{1,0:T(8,128)(2,1)S(1)}, u32[]{:S(2)}, u32[]{:S(2)}) collective-permute-start(bf16[64,1536]{1,0:T(8,128)(2,1)S(1)} %get-tuple-element.76), channel_id=1, source_target_pairs={{0,16},{16,1},{1,17},{17,0},{2,18},{18,3},{3,19},{19,2},{4,20},{20... | collective-permute-start | bytes 589832 | tf_op jit(solution)/shard_map/reduce_x/ppermute | solution.py:32
  148.5 10.9 %collective-permute-start.32 = (bf16[64,1536]{1,0:T(8,128)(2,1)S(1)}, bf16[64,1536]{1,0:T(8,128)(2,1)S(1)}, u32[]{:S(2)}, u32[]{:S(2)}) collective-permute-start(bf16[64,1536]{1,0:T(8,128)(2,1)S(1)} %add_convert_fusion.2), channel_id=1, source_target_pairs={{0,32},{32,64},{64,96},{96,0},{1,33},{33,65},{65,97},{97,1},{2,34}... | collective-permute-start | bytes 589832 | tf_op jit(solution)/shard_map/gather_y/ppermute | solution.py:32
  154.8 14.5 %collective-permute-start.51 = (bf16[64,1536]{1,0:T(8,128)(2,1)S(1)}, bf16[64,1536]{1,0:T(8,128)(2,1)S(1)}, u32[]{:S(2)}, u32[]{:S(2)}) collective-permute-start(bf16[64,1536]{1,0:T(8,128)(2,1)S(1)} %add_convert_fusion), channel_id=1, source_target_pairs={{0,32},{32,64},{64,96},{96,0},{1,33},{33,65},{65,97},{97,1},{2,34}... | collective-permute-start | bytes 589832 | tf_op jit(solution)/shard_map/gather_y/ppermute | solution.py:32
  155.0 14.3 %collective-permute-start.50 = (bf16[64,1536]{1,0:T(8,128)(2,1)S(1)}, bf16[64,1536]{1,0:T(8,128)(2,1)S(1)}, u32[]{:S(2)}, u32[]{:S(2)}) collective-permute-start(bf16[64,1536]{1,0:T(8,128)(2,1)S(1)} %add_convert_fusion), channel_id=1, source_target_pairs={{0,64},{32,96},{64,0},{96,32},{1,65},{33,97},{65,1},{97,33},{2,66}... | collective-permute-start | bytes 589832 | tf_op jit(solution)/shard_map/gather_y/ppermute | solution.py:32
  159.5 12.8 %collective-permute-start.33 = (bf16[256,1536]{1,0:T(8,128)(2,1)S(1)}, bf16[256,1536]{1,0:T(8,128)(2,1)S(1)}, u32[]{:S(2)}, u32[]{:S(2)}) collective-permute-start(bf16[256,1536]{1,0:T(8,128)(2,1)S(1)} %pad_maximum_fusion.10), channel_id=1, source_target_pairs={{0,8},{8,0},{1,9},{9,1},{2,10},{10,2},{3,11},{11,3},{4,12},{12,4},... | collective-permute-start | bytes 2359304 | tf_op jit(solution)/shard_map/ppermute | solution.py:36
  175.0 13.3 %collective-permute-start.53 = (bf16[256,768]{1,0:T(8,128)(2,1)S(1)}, bf16[256,768]{1,0:T(8,128)(2,1)S(1)}, u32[]{:S(2)}, u32[]{:S(2)}) collective-permute-start(bf16[256,768]{1,0:T(8,128)(2,1)S(1)} %get-tuple-element.37), channel_id=1, source_target_pairs={{0,1},{16,17},{1,0},{17,16},{2,3},{18,19},{3,2},{19,18},{4,5},{20,... | collective-permute-start | bytes 1179656 | tf_op jit(solution)/shard_map/reduce_x/ppermute | solution.py:32
  177.7 19.3 %collective-permute-start.54 = (bf16[256,768]{1,0:T(8,128)(2,1)S(1)}, bf16[256,768]{1,0:T(8,128)(2,1)S(1)}, u32[]{:S(2)}, u32[]{:S(2)}) collective-permute-start(bf16[256,768]{1,0:T(8,128)(2,1)S(1)} %get-tuple-element.38), channel_id=1, source_target_pairs={{0,16},{16,1},{1,17},{17,0},{2,18},{18,3},{3,19},{19,2},{4,20},{20... | collective-permute-start | bytes 1179656 | tf_op jit(solution)/shard_map/reduce_x/ppermute | solution.py:32
  178.1 18.9 %collective-permute-start.55 = (bf16[256,768]{1,0:T(8,128)(2,1)S(1)}, bf16[256,768]{1,0:T(8,128)(2,1)S(1)}, u32[]{:S(2)}, u32[]{:S(2)}) collective-permute-start(bf16[256,768]{1,0:T(8,128)(2,1)S(1)} %get-tuple-element.39), channel_id=1, source_target_pairs={{0,17},{16,0},{1,16},{17,1},{2,19},{18,2},{3,18},{19,3},{4,21},{20... | collective-permute-start | bytes 1179656 | tf_op jit(solution)/shard_map/reduce_x/ppermute | solution.py:32
  (33 other events, 318.3 us)

commit v3 on v2

--- a/solution.py
+++ b/solution.py
@@ -48,6 +48,10 @@
     return lax.optimization_barrier((value, token))[0]
 
 
+def in_turn(values, token):
+    return values if token is None else after(values, token)
+
+
 def near(value, axis):
     with jax.named_scope("gather_" + axis):
         return shift(value, axis, -1), shift(value, axis, 1)
@@ -58,14 +62,23 @@
         return shift(value, axis, 2)
 
 
-def gather(value, axis):
+def passed_on(values, axis):
+    one, three = values
+    half = one.shape[0] // 2
+    with jax.named_scope("gather_" + axis):
+        halves = [shift(one[:half], axis, -1), shift(three[half:], axis, 1)]
+    return jnp.concatenate(halves, axis=0)
+
+
+def gather(value, axis, token=None):
     one, three = near(value, axis)
-    return [value, one, far(value, axis), three]
-
-
-def reduce(parts, axis):
+    return [value, one, far(value if token is None else after(value, token), axis), three]
+
+
+def reduce(parts, axis, token=None):
     with jax.named_scope("reduce_" + axis):
-        two = shift(parts[2], axis, 2)
+        last = parts[2] if token is None else after(parts[2], token)
+        two = shift(last, axis, 2)
         one, three = shift(parts[1], axis, 1), shift(parts[3], axis, -1)
     return (parts[0].astype(wide) + two.astype(wide)) + (one.astype(wide) + three.astype(wide))
 
@@ -100,19 +113,18 @@
 
     right_part = move(right_basis, lambda y, xl, c, z, xh: (y, c, xh, z, xl))
 
-    grad_low = grad.astype(low)
+    grad_low, left_part, right_part = lax.optimization_barrier(
+        (grad.astype(low), left_part, right_part)
+    )
     grad_near, left_near = near(grad_low, "x"), near(left_part, "z")
-    grad_low, grad_near, left_part, left_near, right_part = lax.optimization_barrier(
-        (grad_low, grad_near, left_part, left_near, right_part)
+    right_near = near(right_part, "y")
+    grad_low, grad_near, left_part, left_near = lax.optimization_barrier(
+        (grad_low, grad_near, left_part, left_near)
     )
     grad_far, left_far = far(grad_low, "x"), far(left_part, "z")
-    right_near = near(right_part, "y")
+    right_far = far(after(right_part, right_near), "y")
     pair = jnp.concatenate([exp_avg, exp_avg_sq], axis=0)
-    grad_far, left_far, right_part, right_near, pair = lax.optimization_barrier(
-        (grad_far, left_far, right_part, right_near, pair)
-    )
-    right_far = far(right_part, "y")
-    entering = swap(columns_of(pair, 1 - xl), "xl")
+    entering = swap(after(columns_of(pair, 1 - xl), grad_far), "xl")
 
     beside = pick(lo, grad_near[0], grad_near[1])
     across = pick(lo, grad_near[1], grad_near[0])
@@ -157,8 +169,7 @@
         new_avg_sq = second_beta * avg_sq + (1.0 - second_beta) * rotated * rotated
         return new_avg, new_avg_sq
 
-    rotated_blocks = [[] for _ in range(4)]
-    update = None
+    rotated_blocks = [[None] * HALVES for _ in range(4)]
     left_lows = []
     for h in range(HALVES):
         now = slice(h * 4 * ROWS, (h + 1) * 4 * ROWS)
@@ -170,27 +181,35 @@
     right_own, right_other = right_halves()
     avg_blocks, sq_blocks = spread(0), spread(256)
 
+    moved, turned_back, update = None, None, None
+    tokens = {"z": None, "x": None}
+    steps, backs = [None] * HALVES, [None] * HALVES
     for h in range(HALVES):
         span = slice(h * ROWS, (h + 1) * ROWS)
-        wide_span = slice(h * 4 * ROWS, (h + 1) * 4 * ROWS)
-        left_low = left_lows[h]
-        left_rows = jnp.concatenate(gather(left_low, "x"), axis=0)
+        left_rows = gather(left_lows[h], "x", moved)
+        left_rows = jnp.concatenate(left_rows, axis=0)
         part = dot(left_rows[:, :768], right_own, 1, 0) + dot(left_rows[:, 768:], right_other, 1, 0)
-        part = part.astype(low)
+        moved = part = part.astype(low)
         rotated = reduce([part[:, d * 384 : (d + 1) * 384] for d in range(4)], "z")
         for d in range(4):
-            rotated_blocks[d].append(rotated[d * ROWS : (d + 1) * ROWS])
+            rotated_blocks[d][h] = rotated[d * ROWS : (d + 1) * ROWS]
         new_avg, new_avg_sq = moments(
             jnp.concatenate([b[span] for b in avg_blocks], axis=0),
             jnp.concatenate([b[span] for b in sq_blocks], axis=0),
             rotated,
         )
-        step = (new_avg / first_bias / (jnp.sqrt(new_avg_sq / second_bias) + epsilon)).astype(low)
-        step_rows = jnp.concatenate(gather(step, "z"), axis=1)
+        step = new_avg / first_bias / (jnp.sqrt(new_avg_sq / second_bias) + epsilon)
+        steps[h] = step.astype(low)
+    for h in range(HALVES):
+        step_rows = gather(steps[h], "z", turned_back)
+        step_rows = jnp.concatenate(step_rows, axis=1)
         part = [dot(step_rows, right, 1, 1).astype(low) for right in (right_own, right_other)]
-        part = jnp.concatenate(part, axis=1)
-        back = reduce([part[d * ROWS : (d + 1) * ROWS] for d in range(4)], "x").astype(low)
-        back_own = jnp.concatenate(gather(back, "y"), axis=0)
+        turned_back = part = jnp.concatenate(part, axis=1)
+        backs[h] = reduce([part[d * ROWS : (d + 1) * ROWS] for d in range(4)], "x", tokens["x"]).astype(low)
+        tokens["x"] = backs[h]
+    for h in range(HALVES):
+        wide_span = slice(h * 4 * ROWS, (h + 1) * 4 * ROWS)
+        back_own = jnp.concatenate(gather(backs[h], "y"), axis=0)
         term = dot(left_own[:, wide_span], back_own, 1, 0)
         term = term + dot(left_other[:, wide_span], turned(swap(back_own, "c")), 1, 0)
         update = term if update is None else update + term

time: 198 us -> 191 us (0.965)
  waiting for transfers between devices: 91.1 us -> 63.7 us
  matrix products: 11.2 us -> 17.8 us
  other arithmetic: 7.36 us -> 13.6 us
  starting transfers between devices: 84.8 us -> 90.2 us
    ppermute x48, waiting for transfers between devices: 78.3 us -> 52.7 us  [shift(): lax.ppermute(value, names, [(place[i], place[(i + by) % 4]) for i in rang...]
    dot_general x16, matrix products: 11.2 us -> 17.8 us  [dot(): lax.dot_general(left, right, (((left_dim,), (right_dim,)), ((), ())), pre...]
    select_n x12, other arithmetic: 2.65 us -> 7.85 us  [pick(): return lax.select(jnp.broadcast_to(test, first.shape), first, second)]
    ppermute x48, starting transfers between devices: 65.9 us -> 70.8 us  [shift(): lax.ppermute(value, names, [(place[i], place[(i + by) % 4]) for i in rang...]
  transfers between devices with their start and end apart: 57 -> 57, of which waited for: 25 -> 26; matrix products, arithmetic and copies ran while one was open for 9% -> 17% of each run, Pallas kernels for 0% -> 0%
where the time goes in v3:
time: 191 us; the launch traced here: 190 us
  starting transfers between devices  90.2 us (47%)
  waiting for transfers between devices  63.7 us (33%)
  matrix products  17.8 us (9%)
  other arithmetic  13.6 us (7%)
  local copies, waits for them, and re-layouts  3.19 us (2%)
    ppermute x48, starting transfers between devices, shift(): lax.ppermute(value, names, [(place[i], place[(i + by) % 4]) for i in rang...  70.8 us
    ppermute x48, waiting for transfers between devices, shift(): lax.ppermute(value, names, [(place[i], place[(i + by) % 4]) for i in rang...  52.7 us
    dot_general x16, matrix products, dot(): lax.dot_general(left, right, (((left_dim,), (right_dim,)), ((), ())), pre...  17.8 us
    ppermute x8, starting transfers between devices, swap(): return lax.ppermute(value, axis, [(0, 1), (1, 0)])  14.8 us
    ppermute x8, waiting for transfers between devices, swap(): return lax.ppermute(value, axis, [(0, 1), (1, 0)])  11 us
    select_n x12, other arithmetic, pick(): return lax.select(jnp.broadcast_to(test, first.shape), first, second)  7.85 us
    ppermute x1, starting transfers between devices, move(): return lax.ppermute(value, AXES, pairs)  4.64 us
  transfers between devices with their start and end apart: 57, of which 26 were waited for; matrix products, arithmetic and copies ran while one was open for 17% of the time, Pallas kernels for 0%

profile of v3, /device:TPU:1, one launch (start us, length us, event | category | flops | bytes accessed | tf_op | source)
XLA Modules:
  0.0 189.9 jit_solution(16892032389037033967)
XLA Ops:
  0.7 4.6 %collective-permute-start.1 = (bf16[768,384]{1,0:T(8,128)(2,1)}, bf16[768,384]{1,0:T(8,128)(2,1)}, u32[]{:S(2)}, u32[]{:S(2)}) collective-permute-start(bf16[768,384]{1,0:T(8,128)(2,1)} %param.11), channel_id=1, source_target_pairs={{0,0},{1,8},{2,2},{3,10},{4,4},{5,12},{6,6},{7,14},{8,16},{9,24},{... | collective-permute-start | bytes 1769480 | tf_op jit(solution)/shard_map/ppermute | solution.py:44
  8.4 9.0 %collective-permute-done = bf16[256,256]{0,1:T(8,128)(2,1)S(1)} collective-permute-done((bf16[256,256]{0,1:T(8,128)(2,1)S(1)}, bf16[256,256]{0,1:T(8,128)(2,1)S(1)}, u32[]{:S(2)}, u32[]{:S(2)}) %collective-permute-start) | collective-permute-done | bytes 131104 | tf_op jit(solution)/shard_map/ppermute | solution.py:36
  19.3 2.7 %collective-permute-start.2 = (bf16[256,768]{1,0:T(8,128)(2,1)S(1)}, bf16[256,768]{1,0:T(8,128)(2,1)}, u32[]{:S(2)}, u32[]{:S(2)}) collective-permute-start(bf16[256,768]{1,0:T(8,128)(2,1)S(1)} %convert_element_type.139), channel_id=1, source_target_pairs={{0,17},{16,0},{1,16},{17,1},{2,19},{18,2},{3,18},{19,3},{4,21},{20... | collective-permute-start | bytes 1179656 | tf_op jit(solution)/shard_map/gather_x/ppermute | solution.py:32
  24.8 2.1 %collective-permute-done.5 = bf16[512,256]{0,1:T(8,128)(2,1)} collective-permute-done((bf16[512,256]{0,1:T(8,128)(2,1)S(1)}, bf16[512,256]{0,1:T(8,128)(2,1)}, u32[]{:S(2)}, u32[]{:S(2)}) %collective-permute-start.5) | collective-permute-done | bytes 262176 | tf_op jit(solution)/shard_map/gather_z/ppermute | solution.py:32
  29.7 5.2 %collective-permute-done.4 = bf16[512,256]{0,1:T(8,128)(2,1)S(1)} collective-permute-done((bf16[512,256]{0,1:T(8,128)(2,1)S(1)}, bf16[512,256]{0,1:T(8,128)(2,1)S(1)}, u32[]{:S(2)}, u32[]{:S(2)}) %collective-permute-start.4) | collective-permute-done | bytes 262176 | tf_op jit(solution)/shard_map/gather_z/ppermute | solution.py:32
  38.8 2.4 %collective-permute-start.9 = (bf16[768,384]{1,0:T(8,128)(2,1)}, bf16[768,384]{1,0:T(8,128)(2,1)S(1)}, u32[]{:S(2)}, u32[]{:S(2)}) collective-permute-start(bf16[768,384]{1,0:T(8,128)(2,1)} %collective-permute-done.1), channel_id=1, source_target_pairs={{0,64},{32,96},{64,0},{96,32},{1,65},{33,97},{65,1},{97,33},{2,66}... | collective-permute-start | bytes 1769480 | tf_op jit(solution)/shard_map/gather_y/ppermute | solution.py:32
  41.2 3.1 %collective-permute-done.6 = bf16[512,256]{0,1:T(8,128)(2,1)S(1)} collective-permute-done((bf16[512,256]{0,1:T(8,128)(2,1)S(1)}, bf16[512,256]{0,1:T(8,128)(2,1)S(1)}, u32[]{:S(2)}, u32[]{:S(2)}) %collective-permute-start.6) | collective-permute-done | bytes 262176 | tf_op jit(solution)/shard_map/gather_z/ppermute | solution.py:32
  45.5 2.4 %collective-permute-done.10 = bf16[256,768]{1,0:T(8,128)(2,1)S(1)} collective-permute-done((bf16[256,768]{1,0:T(8,128)(2,1)S(1)}, bf16[256,768]{1,0:T(8,128)(2,1)S(1)}, u32[]{:S(2)}, u32[]{:S(2)}) %collective-permute-start.10) | collective-permute-done | bytes 393248 | tf_op jit(solution)/shard_map/gather_x/ppermute | solution.py:32
  54.6 3.2 %collective-permute-start.14 = (bf16[64,1536]{1,0:T(8,128)(2,1)S(1)}, bf16[64,1536]{1,0:T(8,128)(2,1)S(1)}, u32[]{:S(2)}, u32[]{:S(2)}) collective-permute-start(bf16[64,1536]{1,0:T(8,128)(2,1)S(1)} %get-tuple-element.85), channel_id=1, source_target_pairs={{0,64},{32,96},{64,0},{96,32},{1,65},{33,97},{65,1},{97,33},{2,66}... | collective-permute-start | bytes 589832 | tf_op jit(solution)/shard_map/reduce_y/ppermute | solution.py:32
  62.6 2.9 %collective-permute-start.34 = (bf16[64,1536]{1,0:T(8,128)(2,1)}, bf16[64,1536]{1,0:T(8,128)(2,1)}, u32[]{:S(2)}, u32[]{:S(2)}) collective-permute-start(bf16[64,1536]{1,0:T(8,128)(2,1)} %get-tuple-element.82), channel_id=1, source_target_pairs={{0,64},{32,96},{64,0},{96,32},{1,65},{33,97},{65,1},{97,33},{2,66}... | collective-permute-start | bytes 589832 | tf_op jit(solution)/shard_map/reduce_y/ppermute | solution.py:32
  67.2 3.3 %collective-permute-start.36 = (bf16[64,1536]{1,0:T(8,128)(2,1)}, bf16[64,1536]{1,0:T(8,128)(2,1)}, u32[]{:S(2)}, u32[]{:S(2)}) collective-permute-start(bf16[64,1536]{1,0:T(8,128)(2,1)} %get-tuple-element.83), channel_id=1, source_target_pairs={{0,96},{32,0},{64,32},{96,64},{1,97},{33,1},{65,33},{97,65},{2,98}... | collective-permute-start | bytes 589832 | tf_op jit(solution)/shard_map/reduce_y/ppermute | solution.py:32
  81.5 3.4 %collective-permute-done.19 = bf16[64,1536]{1,0:T(8,128)(2,1)S(1)} collective-permute-done((bf16[64,1536]{1,0:T(8,128)(2,1)S(1)}, bf16[64,1536]{1,0:T(8,128)(2,1)S(1)}, u32[]{:S(2)}, u32[]{:S(2)}) %collective-permute-start.19) | collective-permute-done | bytes 196640 | tf_op jit(solution)/shard_map/gather_x/ppermute | solution.py:32
  85.7 2.4 %fusion.29 = f32[256,1536]{1,0:T(8,128)S(1)} fusion(bf16[768,1536]{1,0:T(8,128)(2,1)} %collective-permute-done.20, bf16[256,1536]{1,0:T(8,128)(2,1)S(1)} %pad_maximum_fusion.8), kind=kOutput, calls=%fused_computation.84 | convolution fusion | flops 603979776 | bytes 4325376 | tf_op jit(solution)/shard_map/dot_general | solution.py:25
  91.5 2.9 %collective-permute-start.23 = (bf16[256,384]{1,0:T(8,128)(2,1)S(1)}, bf16[256,384]{1,0:T(8,128)(2,1)S(1)}, u32[]{:S(2)}, u32[]{:S(2)}) collective-permute-start(bf16[256,384]{1,0:T(8,128)(2,1)S(1)} %get-tuple-element.74), channel_id=1, source_target_pairs={{0,6},{2,0},{4,2},{6,4},{1,7},{3,1},{5,3},{7,5},{8,14},{10,8},{12,... | collective-permute-start | bytes 589832 | tf_op jit(solution)/shard_map/reduce_z/ppermute | solution.py:32
  95.7 2.4 %fusion.26 = f32[256,1536]{1,0:T(8,128)S(1)} fusion(bf16[768,1536]{1,0:T(8,128)(2,1)} %collective-permute-done.20, bf16[256,1536]{1,0:T(8,128)(2,1)S(1)} %pad_maximum_fusion.11), kind=kOutput, calls=%fused_computation.81 | convolution fusion | flops 603979776 | bytes 4325376 | tf_op jit(solution)/shard_map/dot_general | solution.py:25
  100.2 3.3 %collective-permute-start.42 = (bf16[256,384]{1,0:T(8,128)(2,1)S(1)}, bf16[256,384]{1,0:T(8,128)(2,1)S(1)}, u32[]{:S(2)}, u32[]{:S(2)}) collective-permute-start(bf16[256,384]{1,0:T(8,128)(2,1)S(1)} %get-tuple-element.80), channel_id=1, source_target_pairs={{0,6},{2,0},{4,2},{6,4},{1,7},{3,1},{5,3},{7,5},{8,14},{10,8},{12,... | collective-permute-start | bytes 589832 | tf_op jit(solution)/shard_map/reduce_z/ppermute | solution.py:32
  104.0 3.8 %collective-permute-start.25 = (bf16[256,384]{1,0:T(8,128)(2,1)S(1)}, bf16[256,384]{1,0:T(8,128)(2,1)S(1)}, u32[]{:S(2)}, u32[]{:S(2)}) collective-permute-start(bf16[256,384]{1,0:T(8,128)(2,1)S(1)} %get-tuple-element.57), channel_id=1, source_target_pairs={{0,4},{2,6},{4,0},{6,2},{1,5},{3,7},{5,1},{7,3},{8,12},{10,14},{12... | collective-permute-start | bytes 589832 | tf_op jit(solution)/shard_map/gather_z/ppermute | solution.py:32
  111.6 2.7 %collective-permute-start.43 = (bf16[256,384]{1,0:T(8,128)(2,1)S(1)}, bf16[256,384]{1,0:T(8,128)(2,1)S(1)}, u32[]{:S(2)}, u32[]{:S(2)}) collective-permute-start(bf16[256,384]{1,0:T(8,128)(2,1)S(1)} %get-tuple-element.33), channel_id=1, source_target_pairs={{0,6},{2,0},{4,2},{6,4},{1,7},{3,1},{5,3},{7,5},{8,14},{10,8},{12,... | collective-permute-start | bytes 589832 | tf_op jit(solution)/shard_map/gather_z/ppermute | solution.py:32
  114.3 2.2 %collective-permute-done.26 = bf16[256,384]{1,0:T(8,128)(2,1)S(1)} collective-permute-done((bf16[256,384]{1,0:T(8,128)(2,1)S(1)}, bf16[256,384]{1,0:T(8,128)(2,1)S(1)}, u32[]{:S(2)}, u32[]{:S(2)}) %collective-permute-start.26) | collective-permute-done | bytes 196640 | tf_op jit(solution)/shard_map/gather_z/ppermute | solution.py:32
  118.1 2.5 %convolution_convert_fusion.2 = bf16[256,768]{1,0:T(8,128)(2,1)S(1)} fusion(bf16[768,1536]{1,0:T(8,128)(2,1)} %collective-permute-done.20, bf16[256,384]{1,0:T(8,128)(2,1)S(1)} %collective-permute-done.26, bf16[256,384]{1,0:T(8,128)(2,1)S(1)} %collective-permute-done.25, bf16[256,384]{1,0:T(8,128)(2,1)S(1)} %collective-permute-done.24, ...), kind=kOutput, calls=%fused_computation.17 | convolution fusion | flops 607322112 | bytes 3538944 | tf_op jit(solution)/shard_map/dot_general | solution.py:25
  122.8 3.5 %collective-permute-start.28 = (bf16[64,1536]{1,0:T(8,128)(2,1)S(1)}, bf16[64,1536]{1,0:T(8,128)(2,1)S(1)}, u32[]{:S(2)}, u32[]{:S(2)}) collective-permute-start(bf16[64,1536]{1,0:T(8,128)(2,1)S(1)} %get-tuple-element.71), channel_id=1, source_target_pairs={{0,16},{16,1},{1,17},{17,0},{2,18},{18,3},{3,19},{19,2},{4,20},{20... | collective-permute-start | bytes 589832 | tf_op jit(solution)/shard_map/reduce_x/ppermute | solution.py:32
  126.3 3.9 %collective-permute-start.29 = (bf16[64,1536]{1,0:T(8,128)(2,1)S(1)}, bf16[64,1536]{1,0:T(8,128)(2,1)S(1)}, u32[]{:S(2)}, u32[]{:S(2)}) collective-permute-start(bf16[64,1536]{1,0:T(8,128)(2,1)S(1)} %get-tuple-element.72), channel_id=1, source_target_pairs={{0,17},{16,0},{1,16},{17,1},{2,19},{18,2},{3,18},{19,3},{4,21},{20... | collective-permute-start | bytes 589832 | tf_op jit(solution)/shard_map/reduce_x/ppermute | solution.py:32
  130.2 2.5 %convolution_convert_fusion = bf16[256,768]{1,0:T(8,128)(2,1)S(1)} fusion(bf16[768,1536]{1,0:T(8,128)(2,1)} %collective-permute-done.20, bf16[256,384]{1,0:T(8,128)(2,1)S(1)} %collective-permute-done.45, bf16[256,384]{1,0:T(8,128)(2,1)S(1)} %collective-permute-done.44, bf16[256,384]{1,0:T(8,128)(2,1)S(1)} %collective-permute-done.43, ...), kind=kOutput, calls=%fused_computation.15 | convolution fusion | flops 607322112 | bytes 3538944 | tf_op jit(solution)/shard_map/dot_general | solution.py:25
  135.9 3.2 %collective-permute-start.48 = (bf16[64,1536]{1,0:T(8,128)(2,1)S(1)}, bf16[64,1536]{1,0:T(8,128)(2,1)S(1)}, u32[]{:S(2)}, u32[]{:S(2)}) collective-permute-start(bf16[64,1536]{1,0:T(8,128)(2,1)S(1)} %get-tuple-element.77), channel_id=1, source_target_pairs={{0,17},{16,0},{1,16},{17,1},{2,19},{18,2},{3,18},{19,3},{4,21},{20... | collective-permute-start | bytes 589832 | tf_op jit(solution)/shard_map/reduce_x/ppermute | solution.py:32
  140.0 3.7 %collective-permute-start.31 = (bf16[64,1536]{1,0:T(8,128)(2,1)S(1)}, bf16[64,1536]{1,0:T(8,128)(2,1)S(1)}, u32[]{:S(2)}, u32[]{:S(2)}) collective-permute-start(bf16[64,1536]{1,0:T(8,128)(2,1)S(1)} %add_convert_fusion.2), channel_id=1, source_target_pairs={{0,64},{32,96},{64,0},{96,32},{1,65},{33,97},{65,1},{97,33},{2,66}... | collective-permute-start | bytes 589832 | tf_op jit(solution)/shard_map/gather_y/ppermute | solution.py:32
  144.4 2.5 %collective-permute-done.48 = bf16[64,1536]{1,0:T(8,128)(2,1)S(1)} collective-permute-done((bf16[64,1536]{1,0:T(8,128)(2,1)S(1)}, bf16[64,1536]{1,0:T(8,128)(2,1)S(1)}, u32[]{:S(2)}, u32[]{:S(2)}) %collective-permute-start.48) | collective-permute-done | bytes 196640 | tf_op jit(solution)/shard_map/reduce_x/ppermute | solution.py:32
  148.0 3.6 %collective-permute-start.50 = (bf16[64,1536]{1,0:T(8,128)(2,1)S(1)}, bf16[64,1536]{1,0:T(8,128)(2,1)S(1)}, u32[]{:S(2)}, u32[]{:S(2)}) collective-permute-start(bf16[64,1536]{1,0:T(8,128)(2,1)S(1)} %add_convert_fusion), channel_id=1, source_target_pairs={{0,64},{32,96},{64,0},{96,32},{1,65},{33,97},{65,1},{97,33},{2,66}... | collective-permute-start | bytes 589832 | tf_op jit(solution)/shard_map/gather_y/ppermute | solution.py:32
  151.8 6.2 %collective-permute-start.33 = (bf16[256,1536]{1,0:T(8,128)(2,1)S(1)}, bf16[256,1536]{1,0:T(8,128)(2,1)S(1)}, u32[]{:S(2)}, u32[]{:S(2)}) collective-permute-start(bf16[256,1536]{1,0:T(8,128)(2,1)S(1)} %pad_maximum_fusion.10), channel_id=1, source_target_pairs={{0,8},{8,0},{1,9},{9,1},{2,10},{10,2},{3,11},{11,3},{4,12},{12,4},... | collective-permute-start | bytes 2359304 | tf_op jit(solution)/shard_map/ppermute | solution.py:36
  167.1 2.6 %collective-permute-start.53 = (bf16[256,768]{1,0:T(8,128)(2,1)S(1)}, bf16[256,768]{1,0:T(8,128)(2,1)S(1)}, u32[]{:S(2)}, u32[]{:S(2)}) collective-permute-start(bf16[256,768]{1,0:T(8,128)(2,1)S(1)} %get-tuple-element.39), channel_id=1, source_target_pairs={{0,1},{16,17},{1,0},{17,16},{2,3},{18,19},{3,2},{19,18},{4,5},{20,... | collective-permute-start | bytes 1179656 | tf_op jit(solution)/shard_map/reduce_x/ppermute | solution.py:32
  170.2 2.2 %collective-permute-start.55 = (bf16[256,768]{1,0:T(8,128)(2,1)S(1)}, bf16[256,768]{1,0:T(8,128)(2,1)S(1)}, u32[]{:S(2)}, u32[]{:S(2)}) collective-permute-start(bf16[256,768]{1,0:T(8,128)(2,1)S(1)} %get-tuple-element.41), channel_id=1, source_target_pairs={{0,17},{16,0},{1,16},{17,1},{2,19},{18,2},{3,18},{19,3},{4,21},{20... | collective-permute-start | bytes 1179656 | tf_op jit(solution)/shard_map/reduce_x/ppermute | solution.py:32
  173.9 6.0 %collective-permute-done.53 = bf16[256,768]{1,0:T(8,128)(2,1)S(1)} collective-permute-done((bf16[256,768]{1,0:T(8,128)(2,1)S(1)}, bf16[256,768]{1,0:T(8,128)(2,1)S(1)}, u32[]{:S(2)}, u32[]{:S(2)}) %collective-permute-start.53) | collective-permute-done | bytes 393248 | tf_op jit(solution)/shard_map/reduce_x/ppermute | solution.py:32
  180.0 8.7 %collective-permute-done.54 = bf16[256,768]{1,0:T(8,128)(2,1)S(1)} collective-permute-done((bf16[256,768]{1,0:T(8,128)(2,1)S(1)}, bf16[256,768]{1,0:T(8,128)(2,1)S(1)}, u32[]{:S(2)}, u32[]{:S(2)}) %collective-permute-start.54) | collective-permute-done | bytes 393248 | tf_op jit(solution)/shard_map/reduce_x/ppermute | solution.py:32
  (176 shorter events, 73.3 us)
Async XLA Ops:
  0.7 16.8 %collective-permute-start.1 = (bf16[768,384]{1,0:T(8,128)(2,1)}, bf16[768,384]{1,0:T(8,128)(2,1)}, u32[]{:S(2)}, u32[]{:S(2)}) collective-permute-start(bf16[768,384]{1,0:T(8,128)(2,1)} %param.11), channel_id=1, source_target_pairs={{0,0},{1,8},{2,2},{3,10},{4,4},{5,12},{6,6},{7,14},{8,16},{9,24},{... | collective-permute-start | bytes 1769480 | tf_op jit(solution)/shard_map/ppermute | solution.py:44
  6.4 11.0 %collective-permute-start = (bf16[256,256]{0,1:T(8,128)(2,1)S(1)}, bf16[256,256]{0,1:T(8,128)(2,1)S(1)}, u32[]{:S(2)}, u32[]{:S(2)}) collective-permute-start(bf16[256,256]{0,1:T(8,128)(2,1)S(1)} %bitcast.13), channel_id=1, source_target_pairs={{0,16},{16,0},{1,17},{17,1},{2,18},{18,2},{3,19},{19,3},{4,20},{20... | collective-permute-start | bytes 393224 | tf_op jit(solution)/shard_map/ppermute | solution.py:36
  19.2 15.7 %collective-permute-start.3 = (bf16[256,768]{1,0:T(8,128)(2,1)S(1)}, bf16[256,768]{1,0:T(8,128)(2,1)S(1)}, u32[]{:S(2)}, u32[]{:S(2)}) collective-permute-start(bf16[256,768]{1,0:T(8,128)(2,1)S(1)} %convert_element_type.139), channel_id=1, source_target_pairs={{0,16},{16,1},{1,17},{17,0},{2,18},{18,3},{3,19},{19,2},{4,20},{20... | collective-permute-start | bytes 1179656 | tf_op jit(solution)/shard_map/gather_x/ppermute | solution.py:32
  19.3 15.6 %collective-permute-start.2 = (bf16[256,768]{1,0:T(8,128)(2,1)S(1)}, bf16[256,768]{1,0:T(8,128)(2,1)}, u32[]{:S(2)}, u32[]{:S(2)}) collective-permute-start(bf16[256,768]{1,0:T(8,128)(2,1)S(1)} %convert_element_type.139), channel_id=1, source_target_pairs={{0,17},{16,0},{1,16},{17,1},{2,19},{18,2},{3,18},{19,3},{4,21},{20... | collective-permute-start | bytes 1179656 | tf_op jit(solution)/shard_map/gather_x/ppermute | solution.py:32
  22.0 16.9 %collective-permute-start.8 = (bf16[768,384]{1,0:T(8,128)(2,1)}, bf16[768,384]{1,0:T(8,128)(2,1)}, u32[]{:S(2)}, u32[]{:S(2)}) collective-permute-start(bf16[768,384]{1,0:T(8,128)(2,1)} %collective-permute-done.1), channel_id=1, source_target_pairs={{0,32},{32,64},{64,96},{96,0},{1,33},{33,65},{65,97},{97,1},{2,34}... | collective-permute-start | bytes 1769480 | tf_op jit(solution)/shard_map/gather_y/ppermute | solution.py:32
  23.2 15.6 %collective-permute-start.7 = (bf16[768,384]{1,0:T(8,128)(2,1)}, bf16[768,384]{1,0:T(8,128)(2,1)}, u32[]{:S(2)}, u32[]{:S(2)}) collective-permute-start(bf16[768,384]{1,0:T(8,128)(2,1)} %collective-permute-done.1), channel_id=1, source_target_pairs={{0,96},{32,0},{64,32},{96,64},{1,97},{33,1},{65,33},{97,65},{2,98}... | collective-permute-start | bytes 1769480 | tf_op jit(solution)/shard_map/gather_y/ppermute | solution.py:32
  36.6 11.2 %collective-permute-start.10 = (bf16[256,768]{1,0:T(8,128)(2,1)S(1)}, bf16[256,768]{1,0:T(8,128)(2,1)S(1)}, u32[]{:S(2)}, u32[]{:S(2)}) collective-permute-start(bf16[256,768]{1,0:T(8,128)(2,1)S(1)} %convert_element_type.139), channel_id=1, source_target_pairs={{0,1},{16,17},{1,0},{17,16},{2,3},{18,19},{3,2},{19,18},{4,5},{20,... | collective-permute-start | bytes 1179656 | tf_op jit(solution)/shard_map/gather_x/ppermute | solution.py:32
  38.8 31.8 %collective-permute-start.9 = (bf16[768,384]{1,0:T(8,128)(2,1)}, bf16[768,384]{1,0:T(8,128)(2,1)S(1)}, u32[]{:S(2)}, u32[]{:S(2)}) collective-permute-start(bf16[768,384]{1,0:T(8,128)(2,1)} %collective-permute-done.1), channel_id=1, source_target_pairs={{0,64},{32,96},{64,0},{96,32},{1,65},{33,97},{65,1},{97,33},{2,66}... | collective-permute-start | bytes 1769480 | tf_op jit(solution)/shard_map/gather_y/ppermute | solution.py:32
  50.5 20.2 %collective-permute-start.11 = (f32[512,384]{1,0:T(8,128)S(1)}, f32[512,384]{1,0:T(8,128)}, u32[]{:S(2)}, u32[]{:S(2)}) collective-permute-start(f32[512,384]{1,0:T(8,128)S(1)} %get-tuple-element.27), channel_id=1, source_target_pairs={{0,16},{16,0},{1,17},{17,1},{2,18},{18,2},{3,19},{19,3},{4,20},{20... | collective-permute-start | bytes 2359304 | tf_op jit(solution)/shard_map/ppermute | solution.py:36
  58.5 12.0 %collective-permute-start.15 = (bf16[64,1536]{1,0:T(8,128)(2,1)S(1)}, bf16[64,1536]{1,0:T(8,128)(2,1)S(1)}, u32[]{:S(2)}, u32[]{:S(2)}) collective-permute-start(bf16[64,1536]{1,0:T(8,128)(2,1)S(1)} %get-tuple-element.87), channel_id=1, source_target_pairs={{0,32},{32,64},{64,96},{96,0},{1,33},{33,65},{65,97},{97,1},{2,34}... | collective-permute-start | bytes 589832 | tf_op jit(solution)/shard_map/reduce_y/ppermute | solution.py:32
  62.6 11.0 %collective-permute-start.34 = (bf16[64,1536]{1,0:T(8,128)(2,1)}, bf16[64,1536]{1,0:T(8,128)(2,1)}, u32[]{:S(2)}, u32[]{:S(2)}) collective-permute-start(bf16[64,1536]{1,0:T(8,128)(2,1)} %get-tuple-element.82), channel_id=1, source_target_pairs={{0,64},{32,96},{64,0},{96,32},{1,65},{33,97},{65,1},{97,33},{2,66}... | collective-permute-start | bytes 589832 | tf_op jit(solution)/shard_map/reduce_y/ppermute | solution.py:32
  72.6 13.1 %collective-permute-start.20 = (bf16[768,1536]{1,0:T(8,128)(2,1)S(1)}, bf16[768,1536]{1,0:T(8,128)(2,1)}, u32[]{:S(2)}, u32[]{:S(2)}) collective-permute-start(bf16[768,1536]{1,0:T(8,128)(2,1)S(1)} %pad_maximum_fusion), channel_id=1, source_target_pairs={{0,8},{8,0},{1,9},{9,1},{2,10},{10,2},{3,11},{11,3},{4,12},{12,4},... | collective-permute-start | bytes 7077896 | tf_op jit(solution)/shard_map/ppermute | solution.py:36
  73.6 11.3 %collective-permute-start.19 = (bf16[64,1536]{1,0:T(8,128)(2,1)S(1)}, bf16[64,1536]{1,0:T(8,128)(2,1)S(1)}, u32[]{:S(2)}, u32[]{:S(2)}) collective-permute-start(bf16[64,1536]{1,0:T(8,128)(2,1)S(1)} %add_convert_fusion.3), channel_id=1, source_target_pairs={{0,16},{16,1},{1,17},{17,0},{2,18},{18,3},{3,19},{19,2},{4,20},{20... | collective-permute-start | bytes 589832 | tf_op jit(solution)/shard_map/gather_x/ppermute | solution.py:32
  73.6 11.3 %collective-permute-start.18 = (bf16[64,1536]{1,0:T(8,128)(2,1)S(1)}, bf16[64,1536]{1,0:T(8,128)(2,1)S(1)}, u32[]{:S(2)}, u32[]{:S(2)}) collective-permute-start(bf16[64,1536]{1,0:T(8,128)(2,1)S(1)} %add_convert_fusion.3), channel_id=1, source_target_pairs={{0,1},{16,17},{1,0},{17,16},{2,3},{18,19},{3,2},{19,18},{4,5},{20,... | collective-permute-start | bytes 589832 | tf_op jit(solution)/shard_map/gather_x/ppermute | solution.py:32
  78.7 15.8 %collective-permute-start.39 = (bf16[64,1536]{1,0:T(8,128)(2,1)S(1)}, bf16[64,1536]{1,0:T(8,128)(2,1)S(1)}, u32[]{:S(2)}, u32[]{:S(2)}) collective-permute-start(bf16[64,1536]{1,0:T(8,128)(2,1)S(1)} %add_convert_fusion.1), channel_id=1, source_target_pairs={{0,16},{16,1},{1,17},{17,0},{2,18},{18,3},{3,19},{19,2},{4,20},{20... | collective-permute-start | bytes 589832 | tf_op jit(solution)/shard_map/gather_x/ppermute | solution.py:32
  89.9 13.6 %collective-permute-start.21 = (bf16[256,384]{1,0:T(8,128)(2,1)S(1)}, bf16[256,384]{1,0:T(8,128)(2,1)S(1)}, u32[]{:S(2)}, u32[]{:S(2)}) collective-permute-start(bf16[256,384]{1,0:T(8,128)(2,1)S(1)} %get-tuple-element.73), channel_id=1, source_target_pairs={{0,4},{2,6},{4,0},{6,2},{1,5},{3,7},{5,1},{7,3},{8,12},{10,14},{12... | collective-permute-start | bytes 589832 | tf_op jit(solution)/shard_map/reduce_z/ppermute | solution.py:32
  91.5 11.9 %collective-permute-start.23 = (bf16[256,384]{1,0:T(8,128)(2,1)S(1)}, bf16[256,384]{1,0:T(8,128)(2,1)S(1)}, u32[]{:S(2)}, u32[]{:S(2)}) collective-permute-start(bf16[256,384]{1,0:T(8,128)(2,1)S(1)} %get-tuple-element.74), channel_id=1, source_target_pairs={{0,6},{2,0},{4,2},{6,4},{1,7},{3,1},{5,3},{7,5},{8,14},{10,8},{12,... | collective-permute-start | bytes 589832 | tf_op jit(solution)/shard_map/reduce_z/ppermute | solution.py:32
  103.9 12.6 %collective-permute-start.26 = (bf16[256,384]{1,0:T(8,128)(2,1)S(1)}, bf16[256,384]{1,0:T(8,128)(2,1)S(1)}, u32[]{:S(2)}, u32[]{:S(2)}) collective-permute-start(bf16[256,384]{1,0:T(8,128)(2,1)S(1)} %get-tuple-element.57), channel_id=1, source_target_pairs={{0,2},{2,4},{4,6},{6,0},{1,3},{3,5},{5,7},{7,1},{8,10},{10,12},{12... | collective-permute-start | bytes 589832 | tf_op jit(solution)/shard_map/gather_z/ppermute | solution.py:32
  104.0 14.2 %collective-permute-start.25 = (bf16[256,384]{1,0:T(8,128)(2,1)S(1)}, bf16[256,384]{1,0:T(8,128)(2,1)S(1)}, u32[]{:S(2)}, u32[]{:S(2)}) collective-permute-start(bf16[256,384]{1,0:T(8,128)(2,1)S(1)} %get-tuple-element.57), channel_id=1, source_target_pairs={{0,4},{2,6},{4,0},{6,2},{1,5},{3,7},{5,1},{7,3},{8,12},{10,14},{12... | collective-permute-start | bytes 589832 | tf_op jit(solution)/shard_map/gather_z/ppermute | solution.py:32
  111.5 18.7 %collective-permute-start.45 = (bf16[256,384]{1,0:T(8,128)(2,1)S(1)}, bf16[256,384]{1,0:T(8,128)(2,1)S(1)}, u32[]{:S(2)}, u32[]{:S(2)}) collective-permute-start(bf16[256,384]{1,0:T(8,128)(2,1)S(1)} %get-tuple-element.33), channel_id=1, source_target_pairs={{0,2},{2,4},{4,6},{6,0},{1,3},{3,5},{5,7},{7,1},{8,10},{10,12},{12... | collective-permute-start | bytes 589832 | tf_op jit(solution)/shard_map/gather_z/ppermute | solution.py:32
  111.6 18.6 %collective-permute-start.43 = (bf16[256,384]{1,0:T(8,128)(2,1)S(1)}, bf16[256,384]{1,0:T(8,128)(2,1)S(1)}, u32[]{:S(2)}, u32[]{:S(2)}) collective-permute-start(bf16[256,384]{1,0:T(8,128)(2,1)S(1)} %get-tuple-element.33), channel_id=1, source_target_pairs={{0,6},{2,0},{4,2},{6,4},{1,7},{3,1},{5,3},{7,5},{8,14},{10,8},{12,... | collective-permute-start | bytes 589832 | tf_op jit(solution)/shard_map/gather_z/ppermute | solution.py:32
  121.5 12.0 %collective-permute-start.27 = (bf16[64,1536]{1,0:T(8,128)(2,1)S(1)}, bf16[64,1536]{1,0:T(8,128)(2,1)S(1)}, u32[]{:S(2)}, u32[]{:S(2)}) collective-permute-start(bf16[64,1536]{1,0:T(8,128)(2,1)S(1)} %get-tuple-element.70), channel_id=1, source_target_pairs={{0,1},{16,17},{1,0},{17,16},{2,3},{18,19},{3,2},{19,18},{4,5},{20,... | collective-permute-start | bytes 589832 | tf_op jit(solution)/shard_map/reduce_x/ppermute | solution.py:32
  122.8 10.8 %collective-permute-start.28 = (bf16[64,1536]{1,0:T(8,128)(2,1)S(1)}, bf16[64,1536]{1,0:T(8,128)(2,1)S(1)}, u32[]{:S(2)}, u32[]{:S(2)}) collective-permute-start(bf16[64,1536]{1,0:T(8,128)(2,1)S(1)} %get-tuple-element.71), channel_id=1, source_target_pairs={{0,16},{16,1},{1,17},{17,0},{2,18},{18,3},{3,19},{19,2},{4,20},{20... | collective-permute-start | bytes 589832 | tf_op jit(solution)/shard_map/reduce_x/ppermute | solution.py:32
  135.9 11.1 %collective-permute-start.48 = (bf16[64,1536]{1,0:T(8,128)(2,1)S(1)}, bf16[64,1536]{1,0:T(8,128)(2,1)S(1)}, u32[]{:S(2)}, u32[]{:S(2)}) collective-permute-start(bf16[64,1536]{1,0:T(8,128)(2,1)S(1)} %get-tuple-element.77), channel_id=1, source_target_pairs={{0,17},{16,0},{1,16},{17,1},{2,19},{18,2},{3,18},{19,3},{4,21},{20... | collective-permute-start | bytes 589832 | tf_op jit(solution)/shard_map/reduce_x/ppermute | solution.py:32
  139.3 12.4 %collective-permute-start.32 = (bf16[64,1536]{1,0:T(8,128)(2,1)S(1)}, bf16[64,1536]{1,0:T(8,128)(2,1)S(1)}, u32[]{:S(2)}, u32[]{:S(2)}) collective-permute-start(bf16[64,1536]{1,0:T(8,128)(2,1)S(1)} %add_convert_fusion.2), channel_id=1, source_target_pairs={{0,32},{32,64},{64,96},{96,0},{1,33},{33,65},{65,97},{97,1},{2,34}... | collective-permute-start | bytes 589832 | tf_op jit(solution)/shard_map/gather_y/ppermute | solution.py:32
  140.0 11.7 %collective-permute-start.31 = (bf16[64,1536]{1,0:T(8,128)(2,1)S(1)}, bf16[64,1536]{1,0:T(8,128)(2,1)S(1)}, u32[]{:S(2)}, u32[]{:S(2)}) collective-permute-start(bf16[64,1536]{1,0:T(8,128)(2,1)S(1)} %add_convert_fusion.2), channel_id=1, source_target_pairs={{0,64},{32,96},{64,0},{96,32},{1,65},{33,97},{65,1},{97,33},{2,66}... | collective-permute-start | bytes 589832 | tf_op jit(solution)/shard_map/gather_y/ppermute | solution.py:32
  147.4 10.6 %collective-permute-start.51 = (bf16[64,1536]{1,0:T(8,128)(2,1)S(1)}, bf16[64,1536]{1,0:T(8,128)(2,1)S(1)}, u32[]{:S(2)}, u32[]{:S(2)}) collective-permute-start(bf16[64,1536]{1,0:T(8,128)(2,1)S(1)} %add_convert_fusion), channel_id=1, source_target_pairs={{0,32},{32,64},{64,96},{96,0},{1,33},{33,65},{65,97},{97,1},{2,34}... | collective-permute-start | bytes 589832 | tf_op jit(solution)/shard_map/gather_y/ppermute | solution.py:32
  148.0 11.2 %collective-permute-start.50 = (bf16[64,1536]{1,0:T(8,128)(2,1)S(1)}, bf16[64,1536]{1,0:T(8,128)(2,1)S(1)}, u32[]{:S(2)}, u32[]{:S(2)}) collective-permute-start(bf16[64,1536]{1,0:T(8,128)(2,1)S(1)} %add_convert_fusion), channel_id=1, source_target_pairs={{0,64},{32,96},{64,0},{96,32},{1,65},{33,97},{65,1},{97,33},{2,66}... | collective-permute-start | bytes 589832 | tf_op jit(solution)/shard_map/gather_y/ppermute | solution.py:32
  151.8 12.2 %collective-permute-start.33 = (bf16[256,1536]{1,0:T(8,128)(2,1)S(1)}, bf16[256,1536]{1,0:T(8,128)(2,1)S(1)}, u32[]{:S(2)}, u32[]{:S(2)}) collective-permute-start(bf16[256,1536]{1,0:T(8,128)(2,1)S(1)} %pad_maximum_fusion.10), channel_id=1, source_target_pairs={{0,8},{8,0},{1,9},{9,1},{2,10},{10,2},{3,11},{11,3},{4,12},{12,4},... | collective-permute-start | bytes 2359304 | tf_op jit(solution)/shard_map/ppermute | solution.py:36
  167.1 12.9 %collective-permute-start.53 = (bf16[256,768]{1,0:T(8,128)(2,1)S(1)}, bf16[256,768]{1,0:T(8,128)(2,1)S(1)}, u32[]{:S(2)}, u32[]{:S(2)}) collective-permute-start(bf16[256,768]{1,0:T(8,128)(2,1)S(1)} %get-tuple-element.39), channel_id=1, source_target_pairs={{0,1},{16,17},{1,0},{17,16},{2,3},{18,19},{3,2},{19,18},{4,5},{20,... | collective-permute-start | bytes 1179656 | tf_op jit(solution)/shard_map/reduce_x/ppermute | solution.py:32
  169.8 18.9 %collective-permute-start.54 = (bf16[256,768]{1,0:T(8,128)(2,1)S(1)}, bf16[256,768]{1,0:T(8,128)(2,1)S(1)}, u32[]{:S(2)}, u32[]{:S(2)}) collective-permute-start(bf16[256,768]{1,0:T(8,128)(2,1)S(1)} %get-tuple-element.40), channel_id=1, source_target_pairs={{0,16},{16,1},{1,17},{17,0},{2,18},{18,3},{3,19},{19,2},{4,20},{20... | collective-permute-start | bytes 1179656 | tf_op jit(solution)/shard_map/reduce_x/ppermute | solution.py:32
  170.2 18.5 %collective-permute-start.55 = (bf16[256,768]{1,0:T(8,128)(2,1)S(1)}, bf16[256,768]{1,0:T(8,128)(2,1)S(1)}, u32[]{:S(2)}, u32[]{:S(2)}) collective-permute-start(bf16[256,768]{1,0:T(8,128)(2,1)S(1)} %get-tuple-element.41), channel_id=1, source_target_pairs={{0,17},{16,0},{1,16},{17,1},{2,19},{18,2},{3,18},{19,3},{4,21},{20... | collective-permute-start | bytes 1179656 | tf_op jit(solution)/shard_map/reduce_x/ppermute | solution.py:32
  (36 other events, 296.0 us)

commit v4 on v3

--- a/solution.py
+++ b/solution.py
@@ -201,7 +201,7 @@
         step = new_avg / first_bias / (jnp.sqrt(new_avg_sq / second_bias) + epsilon)
         steps[h] = step.astype(low)
     for h in range(HALVES):
-        step_rows = gather(steps[h], "z", turned_back)
+        step_rows = gather(steps[h], "z", None)
         step_rows = jnp.concatenate(step_rows, axis=1)
         part = [dot(step_rows, right, 1, 1).astype(low) for right in (right_own, right_other)]
         turned_back = part = jnp.concatenate(part, axis=1)

time: 191 us -> 189 us (0.990)
  waiting for transfers between devices: 63.7 us -> 61.7 us
    ppermute x48, starting transfers between devices: 70.8 us -> 65.6 us  [shift(): lax.ppermute(value, names, [(place[i], place[(i + by) % 4]) for i in rang...]
    ppermute x8, starting transfers between devices: 14.8 us -> 19.9 us  [swap(): return lax.ppermute(value, axis, [(0, 1), (1, 0)])]
    ppermute x48, waiting for transfers between devices: 52.7 us -> 49.7 us  [shift(): lax.ppermute(value, names, [(place[i], place[(i + by) % 4]) for i in rang...]
  transfers between devices with their start and end apart: 57 -> 57, of which waited for: 26 -> 25; matrix products, arithmetic and copies ran while one was open for 17% -> 17% of each run, Pallas kernels for 0% -> 0%
where the time goes in v4:
time: 189 us; the launch traced here: 188 us
  starting transfers between devices  90.2 us (48%)
  waiting for transfers between devices  61.7 us (33%)
  matrix products  17.8 us (9%)
  other arithmetic  13.6 us (7%)
  local copies, waits for them, and re-layouts  3.19 us (2%)
    ppermute x48, starting transfers between devices, shift(): lax.ppermute(value, names, [(place[i], place[(i + by) % 4]) for i in rang...  65.6 us
    ppermute x48, waiting for transfers between devices, shift(): lax.ppermute(value, names, [(place[i], place[(i + by) % 4]) for i in rang...  49.7 us
    ppermute x8, starting transfers between devices, swap(): return lax.ppermute(value, axis, [(0, 1), (1, 0)])  19.9 us
    dot_general x16, matrix products, dot(): lax.dot_general(left, right, (((left_dim,), (right_dim,)), ((), ())), pre...  17.8 us
    ppermute x8, waiting for transfers between devices, swap(): return lax.ppermute(value, axis, [(0, 1), (1, 0)])  12 us
    select_n x12, other arithmetic, pick(): return lax.select(jnp.broadcast_to(test, first.shape), first, second)  7.85 us
    ppermute x1, starting transfers between devices, move(): return lax.ppermute(value, AXES, pairs)  4.64 us
  transfers between devices with their start and end apart: 57, of which 25 were waited for; matrix products, arithmetic and copies ran while one was open for 17% of the time, Pallas kernels for 0%

profile of v4, /device:TPU:1, one launch (start us, length us, event | category | flops | bytes accessed | tf_op | source)
XLA Modules:
  0.0 188.0 jit_solution(14333035780879246082)
XLA Ops:
  0.7 4.6 %collective-permute-start.1 = (bf16[768,384]{1,0:T(8,128)(2,1)}, bf16[768,384]{1,0:T(8,128)(2,1)}, u32[]{:S(2)}, u32[]{:S(2)}) collective-permute-start(bf16[768,384]{1,0:T(8,128)(2,1)} %param.11), channel_id=1, source_target_pairs={{0,0},{1,8},{2,2},{3,10},{4,4},{5,12},{6,6},{7,14},{8,16},{9,24},{... | collective-permute-start | bytes 1769480 | tf_op jit(solution)/shard_map/ppermute | solution.py:44
  6.4 1.9 %collective-permute-start = (bf16[256,256]{0,1:T(8,128)(2,1)S(1)}, bf16[256,256]{0,1:T(8,128)(2,1)S(1)}, u32[]{:S(2)}, u32[]{:S(2)}) collective-permute-start(bf16[256,256]{0,1:T(8,128)(2,1)S(1)} %bitcast.13), channel_id=1, source_target_pairs={{0,16},{16,0},{1,17},{17,1},{2,18},{18,2},{3,19},{19,3},{4,20},{20... | collective-permute-start | bytes 393224 | tf_op jit(solution)/shard_map/ppermute | solution.py:36
  8.4 9.0 %collective-permute-done = bf16[256,256]{0,1:T(8,128)(2,1)S(1)} collective-permute-done((bf16[256,256]{0,1:T(8,128)(2,1)S(1)}, bf16[256,256]{0,1:T(8,128)(2,1)S(1)}, u32[]{:S(2)}, u32[]{:S(2)}) %collective-permute-start) | collective-permute-done | bytes 131104 | tf_op jit(solution)/shard_map/ppermute | solution.py:36
  19.3 2.7 %collective-permute-start.2 = (bf16[256,768]{1,0:T(8,128)(2,1)S(1)}, bf16[256,768]{1,0:T(8,128)(2,1)}, u32[]{:S(2)}, u32[]{:S(2)}) collective-permute-start(bf16[256,768]{1,0:T(8,128)(2,1)S(1)} %convert_element_type.139), channel_id=1, source_target_pairs={{0,17},{16,0},{1,16},{17,1},{2,19},{18,2},{3,18},{19,3},{4,21},{20... | collective-permute-start | bytes 1179656 | tf_op jit(solution)/shard_map/gather_x/ppermute | solution.py:32
  24.8 2.1 %collective-permute-done.5 = bf16[512,256]{0,1:T(8,128)(2,1)} collective-permute-done((bf16[512,256]{0,1:T(8,128)(2,1)S(1)}, bf16[512,256]{0,1:T(8,128)(2,1)}, u32[]{:S(2)}, u32[]{:S(2)}) %collective-permute-start.5) | collective-permute-done | bytes 262176 | tf_op jit(solution)/shard_map/gather_z/ppermute | solution.py:32
  29.7 5.2 %collective-permute-done.4 = bf16[512,256]{0,1:T(8,128)(2,1)S(1)} collective-permute-done((bf16[512,256]{0,1:T(8,128)(2,1)S(1)}, bf16[512,256]{0,1:T(8,128)(2,1)S(1)}, u32[]{:S(2)}, u32[]{:S(2)}) %collective-permute-start.4) | collective-permute-done | bytes 262176 | tf_op jit(solution)/shard_map/gather_z/ppermute | solution.py:32
  38.8 2.4 %collective-permute-start.9 = (bf16[768,384]{1,0:T(8,128)(2,1)}, bf16[768,384]{1,0:T(8,128)(2,1)S(1)}, u32[]{:S(2)}, u32[]{:S(2)}) collective-permute-start(bf16[768,384]{1,0:T(8,128)(2,1)} %collective-permute-done.1), channel_id=1, source_target_pairs={{0,64},{32,96},{64,0},{96,32},{1,65},{33,97},{65,1},{97,33},{2,66}... | collective-permute-start | bytes 1769480 | tf_op jit(solution)/shard_map/gather_y/ppermute | solution.py:32
  41.2 3.1 %collective-permute-done.6 = bf16[512,256]{0,1:T(8,128)(2,1)S(1)} collective-permute-done((bf16[512,256]{0,1:T(8,128)(2,1)S(1)}, bf16[512,256]{0,1:T(8,128)(2,1)S(1)}, u32[]{:S(2)}, u32[]{:S(2)}) %collective-permute-start.6) | collective-permute-done | bytes 262176 | tf_op jit(solution)/shard_map/gather_z/ppermute | solution.py:32
  45.5 2.4 %collective-permute-done.10 = bf16[256,768]{1,0:T(8,128)(2,1)S(1)} collective-permute-done((bf16[256,768]{1,0:T(8,128)(2,1)S(1)}, bf16[256,768]{1,0:T(8,128)(2,1)S(1)}, u32[]{:S(2)}, u32[]{:S(2)}) %collective-permute-start.10) | collective-permute-done | bytes 393248 | tf_op jit(solution)/shard_map/gather_x/ppermute | solution.py:32
  54.6 3.2 %collective-permute-start.14 = (bf16[64,1536]{1,0:T(8,128)(2,1)S(1)}, bf16[64,1536]{1,0:T(8,128)(2,1)S(1)}, u32[]{:S(2)}, u32[]{:S(2)}) collective-permute-start(bf16[64,1536]{1,0:T(8,128)(2,1)S(1)} %get-tuple-element.83), channel_id=1, source_target_pairs={{0,64},{32,96},{64,0},{96,32},{1,65},{33,97},{65,1},{97,33},{2,66}... | collective-permute-start | bytes 589832 | tf_op jit(solution)/shard_map/reduce_y/ppermute | solution.py:32
  62.6 2.9 %collective-permute-start.34 = (bf16[64,1536]{1,0:T(8,128)(2,1)}, bf16[64,1536]{1,0:T(8,128)(2,1)}, u32[]{:S(2)}, u32[]{:S(2)}) collective-permute-start(bf16[64,1536]{1,0:T(8,128)(2,1)} %get-tuple-element.80), channel_id=1, source_target_pairs={{0,64},{32,96},{64,0},{96,32},{1,65},{33,97},{65,1},{97,33},{2,66}... | collective-permute-start | bytes 589832 | tf_op jit(solution)/shard_map/reduce_y/ppermute | solution.py:32
  67.2 3.3 %collective-permute-start.36 = (bf16[64,1536]{1,0:T(8,128)(2,1)}, bf16[64,1536]{1,0:T(8,128)(2,1)}, u32[]{:S(2)}, u32[]{:S(2)}) collective-permute-start(bf16[64,1536]{1,0:T(8,128)(2,1)} %get-tuple-element.81), channel_id=1, source_target_pairs={{0,96},{32,0},{64,32},{96,64},{1,97},{33,1},{65,33},{97,65},{2,98}... | collective-permute-start | bytes 589832 | tf_op jit(solution)/shard_map/reduce_y/ppermute | solution.py:32
  81.5 3.4 %collective-permute-done.19 = bf16[64,1536]{1,0:T(8,128)(2,1)S(1)} collective-permute-done((bf16[64,1536]{1,0:T(8,128)(2,1)S(1)}, bf16[64,1536]{1,0:T(8,128)(2,1)S(1)}, u32[]{:S(2)}, u32[]{:S(2)}) %collective-permute-start.19) | collective-permute-done | bytes 196640 | tf_op jit(solution)/shard_map/gather_x/ppermute | solution.py:32
  85.7 2.4 %fusion.29 = f32[256,1536]{1,0:T(8,128)S(1)} fusion(bf16[768,1536]{1,0:T(8,128)(2,1)} %collective-permute-done.20, bf16[256,1536]{1,0:T(8,128)(2,1)S(1)} %pad_maximum_fusion.7), kind=kOutput, calls=%fused_computation.81 | convolution fusion | flops 603979776 | bytes 4325376 | tf_op jit(solution)/shard_map/dot_general | solution.py:25
  91.5 2.9 %collective-permute-start.23 = (bf16[256,384]{1,0:T(8,128)(2,1)S(1)}, bf16[256,384]{1,0:T(8,128)(2,1)S(1)}, u32[]{:S(2)}, u32[]{:S(2)}) collective-permute-start(bf16[256,384]{1,0:T(8,128)(2,1)S(1)} %get-tuple-element.72), channel_id=1, source_target_pairs={{0,6},{2,0},{4,2},{6,4},{1,7},{3,1},{5,3},{7,5},{8,14},{10,8},{12,... | collective-permute-start | bytes 589832 | tf_op jit(solution)/shard_map/reduce_z/ppermute | solution.py:32
  95.7 2.4 %fusion.26 = f32[256,1536]{1,0:T(8,128)S(1)} fusion(bf16[768,1536]{1,0:T(8,128)(2,1)} %collective-permute-done.20, bf16[256,1536]{1,0:T(8,128)(2,1)S(1)} %pad_maximum_fusion.10), kind=kOutput, calls=%fused_computation.78 | convolution fusion | flops 603979776 | bytes 4325376 | tf_op jit(solution)/shard_map/dot_general | solution.py:25
  100.2 3.3 %collective-permute-start.42 = (bf16[256,384]{1,0:T(8,128)(2,1)S(1)}, bf16[256,384]{1,0:T(8,128)(2,1)S(1)}, u32[]{:S(2)}, u32[]{:S(2)}) collective-permute-start(bf16[256,384]{1,0:T(8,128)(2,1)S(1)} %get-tuple-element.78), channel_id=1, source_target_pairs={{0,6},{2,0},{4,2},{6,4},{1,7},{3,1},{5,3},{7,5},{8,14},{10,8},{12,... | collective-permute-start | bytes 589832 | tf_op jit(solution)/shard_map/reduce_z/ppermute | solution.py:32
  104.0 3.8 %collective-permute-start.25 = (bf16[256,384]{1,0:T(8,128)(2,1)S(1)}, bf16[256,384]{1,0:T(8,128)(2,1)S(1)}, u32[]{:S(2)}, u32[]{:S(2)}) collective-permute-start(bf16[256,384]{1,0:T(8,128)(2,1)S(1)} %get-tuple-element.55), channel_id=1, source_target_pairs={{0,4},{2,6},{4,0},{6,2},{1,5},{3,7},{5,1},{7,3},{8,12},{10,14},{12... | collective-permute-start | bytes 589832 | tf_op jit(solution)/shard_map/gather_z/ppermute | solution.py:32
  109.2 1.9 %collective-permute-done.41 = bf16[256,384]{1,0:T(8,128)(2,1)S(1)} collective-permute-done((bf16[256,384]{1,0:T(8,128)(2,1)S(1)}, bf16[256,384]{1,0:T(8,128)(2,1)S(1)}, u32[]{:S(2)}, u32[]{:S(2)}) %collective-permute-start.41) | collective-permute-done | bytes 196640 | tf_op jit(solution)/shard_map/reduce_z/ppermute | solution.py:32
  111.6 3.2 %collective-permute-start.44 = (bf16[256,384]{1,0:T(8,128)(2,1)S(1)}, bf16[256,384]{1,0:T(8,128)(2,1)S(1)}, u32[]{:S(2)}, u32[]{:S(2)}) collective-permute-start(bf16[256,384]{1,0:T(8,128)(2,1)S(1)} %get-tuple-element.57), channel_id=1, source_target_pairs={{0,4},{2,6},{4,0},{6,2},{1,5},{3,7},{5,1},{7,3},{8,12},{10,14},{12... | collective-permute-start | bytes 589832 | tf_op jit(solution)/shard_map/gather_z/ppermute | solution.py:32
  118.1 2.5 %convolution_convert_fusion.2 = bf16[256,768]{1,0:T(8,128)(2,1)S(1)} fusion(bf16[768,1536]{1,0:T(8,128)(2,1)} %collective-permute-done.20, bf16[256,384]{1,0:T(8,128)(2,1)S(1)} %collective-permute-done.26, bf16[256,384]{1,0:T(8,128)(2,1)S(1)} %collective-permute-done.25, bf16[256,384]{1,0:T(8,128)(2,1)S(1)} %collective-permute-done.24, ...), kind=kOutput, calls=%fused_computation.17 | convolution fusion | flops 607322112 | bytes 3538944 | tf_op jit(solution)/shard_map/dot_general | solution.py:25
  122.9 3.4 %collective-permute-start.29 = (bf16[64,1536]{1,0:T(8,128)(2,1)S(1)}, bf16[64,1536]{1,0:T(8,128)(2,1)S(1)}, u32[]{:S(2)}, u32[]{:S(2)}) collective-permute-start(bf16[64,1536]{1,0:T(8,128)(2,1)S(1)} %get-tuple-element.69), channel_id=1, source_target_pairs={{0,17},{16,0},{1,16},{17,1},{2,19},{18,2},{3,18},{19,3},{4,21},{20... | collective-permute-start | bytes 589832 | tf_op jit(solution)/shard_map/reduce_x/ppermute | solution.py:32
  126.4 2.5 %convolution_convert_fusion = bf16[256,768]{1,0:T(8,128)(2,1)S(1)} fusion(bf16[768,1536]{1,0:T(8,128)(2,1)} %collective-permute-done.20, bf16[256,384]{1,0:T(8,128)(2,1)S(1)} %collective-permute-done.45, bf16[256,384]{1,0:T(8,128)(2,1)S(1)} %collective-permute-done.44, bf16[256,384]{1,0:T(8,128)(2,1)S(1)} %collective-permute-done.43, ...), kind=kOutput, calls=%fused_computation.15 | convolution fusion | flops 607322112 | bytes 3538944 | tf_op jit(solution)/shard_map/dot_general | solution.py:25
  134.9 2.3 %collective-permute-start.32 = (bf16[64,1536]{1,0:T(8,128)(2,1)S(1)}, bf16[64,1536]{1,0:T(8,128)(2,1)S(1)}, u32[]{:S(2)}, u32[]{:S(2)}) collective-permute-start(bf16[64,1536]{1,0:T(8,128)(2,1)S(1)} %add_convert_fusion.2), channel_id=1, source_target_pairs={{0,32},{32,64},{64,96},{96,0},{1,33},{33,65},{65,97},{97,1},{2,34}... | collective-permute-start | bytes 589832 | tf_op jit(solution)/shard_map/gather_y/ppermute | solution.py:32
  137.2 2.0 %collective-permute-start.31 = (bf16[64,1536]{1,0:T(8,128)(2,1)S(1)}, bf16[64,1536]{1,0:T(8,128)(2,1)S(1)}, u32[]{:S(2)}, u32[]{:S(2)}) collective-permute-start(bf16[64,1536]{1,0:T(8,128)(2,1)S(1)} %add_convert_fusion.2), channel_id=1, source_target_pairs={{0,64},{32,96},{64,0},{96,32},{1,65},{33,97},{65,1},{97,33},{2,66}... | collective-permute-start | bytes 589832 | tf_op jit(solution)/shard_map/gather_y/ppermute | solution.py:32
  140.4 3.0 %collective-permute-start.30 = (bf16[64,1536]{1,0:T(8,128)(2,1)S(1)}, bf16[64,1536]{1,0:T(8,128)(2,1)S(1)}, u32[]{:S(2)}, u32[]{:S(2)}) collective-permute-start(bf16[64,1536]{1,0:T(8,128)(2,1)S(1)} %add_convert_fusion.2), channel_id=1, source_target_pairs={{0,96},{32,0},{64,32},{96,64},{1,97},{33,1},{65,33},{97,65},{2,98}... | collective-permute-start | bytes 589832 | tf_op jit(solution)/shard_map/gather_y/ppermute | solution.py:32
  143.6 2.7 %collective-permute-start.50 = (bf16[64,1536]{1,0:T(8,128)(2,1)S(1)}, bf16[64,1536]{1,0:T(8,128)(2,1)S(1)}, u32[]{:S(2)}, u32[]{:S(2)}) collective-permute-start(bf16[64,1536]{1,0:T(8,128)(2,1)S(1)} %add_convert_fusion), channel_id=1, source_target_pairs={{0,64},{32,96},{64,0},{96,32},{1,65},{33,97},{65,1},{97,33},{2,66}... | collective-permute-start | bytes 589832 | tf_op jit(solution)/shard_map/gather_y/ppermute | solution.py:32
  146.3 10.7 %collective-permute-start.33 = (bf16[256,1536]{1,0:T(8,128)(2,1)S(1)}, bf16[256,1536]{1,0:T(8,128)(2,1)S(1)}, u32[]{:S(2)}, u32[]{:S(2)}) collective-permute-start(bf16[256,1536]{1,0:T(8,128)(2,1)S(1)} %pad_maximum_fusion.9), channel_id=1, source_target_pairs={{0,8},{8,0},{1,9},{9,1},{2,10},{10,2},{3,11},{11,3},{4,12},{12,4},... | collective-permute-start | bytes 2359304 | tf_op jit(solution)/shard_map/ppermute | solution.py:36
  157.3 4.0 %collective-permute-start.52 = (bf16[256,1536]{1,0:T(8,128)(2,1)S(1)}, bf16[256,1536]{1,0:T(8,128)(2,1)S(1)}, u32[]{:S(2)}, u32[]{:S(2)}) collective-permute-start(bf16[256,1536]{1,0:T(8,128)(2,1)S(1)} %pad_maximum_fusion.12), channel_id=1, source_target_pairs={{0,8},{8,0},{1,9},{9,1},{2,10},{10,2},{3,11},{11,3},{4,12},{12,4},... | collective-permute-start | bytes 2359304 | tf_op jit(solution)/shard_map/ppermute | solution.py:36
  167.5 2.2 %collective-permute-start.55 = (bf16[256,768]{1,0:T(8,128)(2,1)S(1)}, bf16[256,768]{1,0:T(8,128)(2,1)S(1)}, u32[]{:S(2)}, u32[]{:S(2)}) collective-permute-start(bf16[256,768]{1,0:T(8,128)(2,1)S(1)} %get-tuple-element.39), channel_id=1, source_target_pairs={{0,17},{16,0},{1,16},{17,1},{2,19},{18,2},{3,18},{19,3},{4,21},{20... | collective-permute-start | bytes 1179656 | tf_op jit(solution)/shard_map/reduce_x/ppermute | solution.py:32
  171.3 6.3 %collective-permute-done.53 = bf16[256,768]{1,0:T(8,128)(2,1)S(1)} collective-permute-done((bf16[256,768]{1,0:T(8,128)(2,1)S(1)}, bf16[256,768]{1,0:T(8,128)(2,1)S(1)}, u32[]{:S(2)}, u32[]{:S(2)}) %collective-permute-start.53) | collective-permute-done | bytes 393248 | tf_op jit(solution)/shard_map/reduce_x/ppermute | solution.py:32
  177.6 9.1 %collective-permute-done.54 = bf16[256,768]{1,0:T(8,128)(2,1)S(1)} collective-permute-done((bf16[256,768]{1,0:T(8,128)(2,1)S(1)}, bf16[256,768]{1,0:T(8,128)(2,1)S(1)}, u32[]{:S(2)}, u32[]{:S(2)}) %collective-permute-start.54) | collective-permute-done | bytes 393248 | tf_op jit(solution)/shard_map/reduce_x/ppermute | solution.py:32
  (176 shorter events, 69.6 us)
Async XLA Ops:
  0.7 16.8 %collective-permute-start.1 = (bf16[768,384]{1,0:T(8,128)(2,1)}, bf16[768,384]{1,0:T(8,128)(2,1)}, u32[]{:S(2)}, u32[]{:S(2)}) collective-permute-start(bf16[768,384]{1,0:T(8,128)(2,1)} %param.11), channel_id=1, source_target_pairs={{0,0},{1,8},{2,2},{3,10},{4,4},{5,12},{6,6},{7,14},{8,16},{9,24},{... | collective-permute-start | bytes 1769480 | tf_op jit(solution)/shard_map/ppermute | solution.py:44
  6.4 11.0 %collective-permute-start = (bf16[256,256]{0,1:T(8,128)(2,1)S(1)}, bf16[256,256]{0,1:T(8,128)(2,1)S(1)}, u32[]{:S(2)}, u32[]{:S(2)}) collective-permute-start(bf16[256,256]{0,1:T(8,128)(2,1)S(1)} %bitcast.13), channel_id=1, source_target_pairs={{0,16},{16,0},{1,17},{17,1},{2,18},{18,2},{3,19},{19,3},{4,20},{20... | collective-permute-start | bytes 393224 | tf_op jit(solution)/shard_map/ppermute | solution.py:36
  19.2 15.7 %collective-permute-start.3 = (bf16[256,768]{1,0:T(8,128)(2,1)S(1)}, bf16[256,768]{1,0:T(8,128)(2,1)S(1)}, u32[]{:S(2)}, u32[]{:S(2)}) collective-permute-start(bf16[256,768]{1,0:T(8,128)(2,1)S(1)} %convert_element_type.139), channel_id=1, source_target_pairs={{0,16},{16,1},{1,17},{17,0},{2,18},{18,3},{3,19},{19,2},{4,20},{20... | collective-permute-start | bytes 1179656 | tf_op jit(solution)/shard_map/gather_x/ppermute | solution.py:32
  19.3 15.6 %collective-permute-start.2 = (bf16[256,768]{1,0:T(8,128)(2,1)S(1)}, bf16[256,768]{1,0:T(8,128)(2,1)}, u32[]{:S(2)}, u32[]{:S(2)}) collective-permute-start(bf16[256,768]{1,0:T(8,128)(2,1)S(1)} %convert_element_type.139), channel_id=1, source_target_pairs={{0,17},{16,0},{1,16},{17,1},{2,19},{18,2},{3,18},{19,3},{4,21},{20... | collective-permute-start | bytes 1179656 | tf_op jit(solution)/shard_map/gather_x/ppermute | solution.py:32
  22.0 16.9 %collective-permute-start.8 = (bf16[768,384]{1,0:T(8,128)(2,1)}, bf16[768,384]{1,0:T(8,128)(2,1)}, u32[]{:S(2)}, u32[]{:S(2)}) collective-permute-start(bf16[768,384]{1,0:T(8,128)(2,1)} %collective-permute-done.1), channel_id=1, source_target_pairs={{0,32},{32,64},{64,96},{96,0},{1,33},{33,65},{65,97},{97,1},{2,34}... | collective-permute-start | bytes 1769480 | tf_op jit(solution)/shard_map/gather_y/ppermute | solution.py:32
  23.2 15.6 %collective-permute-start.7 = (bf16[768,384]{1,0:T(8,128)(2,1)}, bf16[768,384]{1,0:T(8,128)(2,1)}, u32[]{:S(2)}, u32[]{:S(2)}) collective-permute-start(bf16[768,384]{1,0:T(8,128)(2,1)} %collective-permute-done.1), channel_id=1, source_target_pairs={{0,96},{32,0},{64,32},{96,64},{1,97},{33,1},{65,33},{97,65},{2,98}... | collective-permute-start | bytes 1769480 | tf_op jit(solution)/shard_map/gather_y/ppermute | solution.py:32
  36.6 11.2 %collective-permute-start.10 = (bf16[256,768]{1,0:T(8,128)(2,1)S(1)}, bf16[256,768]{1,0:T(8,128)(2,1)S(1)}, u32[]{:S(2)}, u32[]{:S(2)}) collective-permute-start(bf16[256,768]{1,0:T(8,128)(2,1)S(1)} %convert_element_type.139), channel_id=1, source_target_pairs={{0,1},{16,17},{1,0},{17,16},{2,3},{18,19},{3,2},{19,18},{4,5},{20,... | collective-permute-start | bytes 1179656 | tf_op jit(solution)/shard_map/gather_x/ppermute | solution.py:32
  38.8 31.8 %collective-permute-start.9 = (bf16[768,384]{1,0:T(8,128)(2,1)}, bf16[768,384]{1,0:T(8,128)(2,1)S(1)}, u32[]{:S(2)}, u32[]{:S(2)}) collective-permute-start(bf16[768,384]{1,0:T(8,128)(2,1)} %collective-permute-done.1), channel_id=1, source_target_pairs={{0,64},{32,96},{64,0},{96,32},{1,65},{33,97},{65,1},{97,33},{2,66}... | collective-permute-start | bytes 1769480 | tf_op jit(solution)/shard_map/gather_y/ppermute | solution.py:32
  50.5 20.2 %collective-permute-start.11 = (f32[512,384]{1,0:T(8,128)S(1)}, f32[512,384]{1,0:T(8,128)}, u32[]{:S(2)}, u32[]{:S(2)}) collective-permute-start(f32[512,384]{1,0:T(8,128)S(1)} %get-tuple-element.26), channel_id=1, source_target_pairs={{0,16},{16,0},{1,17},{17,1},{2,18},{18,2},{3,19},{19,3},{4,20},{20... | collective-permute-start | bytes 2359304 | tf_op jit(solution)/shard_map/ppermute | solution.py:36
  58.5 12.0 %collective-permute-start.15 = (bf16[64,1536]{1,0:T(8,128)(2,1)S(1)}, bf16[64,1536]{1,0:T(8,128)(2,1)S(1)}, u32[]{:S(2)}, u32[]{:S(2)}) collective-permute-start(bf16[64,1536]{1,0:T(8,128)(2,1)S(1)} %get-tuple-element.85), channel_id=1, source_target_pairs={{0,32},{32,64},{64,96},{96,0},{1,33},{33,65},{65,97},{97,1},{2,34}... | collective-permute-start | bytes 589832 | tf_op jit(solution)/shard_map/reduce_y/ppermute | solution.py:32
  62.6 11.0 %collective-permute-start.34 = (bf16[64,1536]{1,0:T(8,128)(2,1)}, bf16[64,1536]{1,0:T(8,128)(2,1)}, u32[]{:S(2)}, u32[]{:S(2)}) collective-permute-start(bf16[64,1536]{1,0:T(8,128)(2,1)} %get-tuple-element.80), channel_id=1, source_target_pairs={{0,64},{32,96},{64,0},{96,32},{1,65},{33,97},{65,1},{97,33},{2,66}... | collective-permute-start | bytes 589832 | tf_op jit(solution)/shard_map/reduce_y/ppermute | solution.py:32
  72.6 13.1 %collective-permute-start.20 = (bf16[768,1536]{1,0:T(8,128)(2,1)S(1)}, bf16[768,1536]{1,0:T(8,128)(2,1)}, u32[]{:S(2)}, u32[]{:S(2)}) collective-permute-start(bf16[768,1536]{1,0:T(8,128)(2,1)S(1)} %pad_maximum_fusion), channel_id=1, source_target_pairs={{0,8},{8,0},{1,9},{9,1},{2,10},{10,2},{3,11},{11,3},{4,12},{12,4},... | collective-permute-start | bytes 7077896 | tf_op jit(solution)/shard_map/ppermute | solution.py:36
  73.6 11.3 %collective-permute-start.19 = (bf16[64,1536]{1,0:T(8,128)(2,1)S(1)}, bf16[64,1536]{1,0:T(8,128)(2,1)S(1)}, u32[]{:S(2)}, u32[]{:S(2)}) collective-permute-start(bf16[64,1536]{1,0:T(8,128)(2,1)S(1)} %add_convert_fusion.3), channel_id=1, source_target_pairs={{0,16},{16,1},{1,17},{17,0},{2,18},{18,3},{3,19},{19,2},{4,20},{20... | collective-permute-start | bytes 589832 | tf_op jit(solution)/shard_map/gather_x/ppermute | solution.py:32
  73.6 11.3 %collective-permute-start.18 = (bf16[64,1536]{1,0:T(8,128)(2,1)S(1)}, bf16[64,1536]{1,0:T(8,128)(2,1)S(1)}, u32[]{:S(2)}, u32[]{:S(2)}) collective-permute-start(bf16[64,1536]{1,0:T(8,128)(2,1)S(1)} %add_convert_fusion.3), channel_id=1, source_target_pairs={{0,1},{16,17},{1,0},{17,16},{2,3},{18,19},{3,2},{19,18},{4,5},{20,... | collective-permute-start | bytes 589832 | tf_op jit(solution)/shard_map/gather_x/ppermute | solution.py:32
  75.7 10.0 %collective-permute-start.17 = (bf16[64,1536]{1,0:T(8,128)(2,1)S(1)}, bf16[64,1536]{1,0:T(8,128)(2,1)S(1)}, u32[]{:S(2)}, u32[]{:S(2)}) collective-permute-start(bf16[64,1536]{1,0:T(8,128)(2,1)S(1)} %add_convert_fusion.3), channel_id=1, source_target_pairs={{0,17},{16,0},{1,16},{17,1},{2,19},{18,2},{3,18},{19,3},{4,21},{20... | collective-permute-start | bytes 589832 | tf_op jit(solution)/shard_map/gather_x/ppermute | solution.py:32
  78.7 15.8 %collective-permute-start.39 = (bf16[64,1536]{1,0:T(8,128)(2,1)S(1)}, bf16[64,1536]{1,0:T(8,128)(2,1)S(1)}, u32[]{:S(2)}, u32[]{:S(2)}) collective-permute-start(bf16[64,1536]{1,0:T(8,128)(2,1)S(1)} %add_convert_fusion.1), channel_id=1, source_target_pairs={{0,16},{16,1},{1,17},{17,0},{2,18},{18,3},{3,19},{19,2},{4,20},{20... | collective-permute-start | bytes 589832 | tf_op jit(solution)/shard_map/gather_x/ppermute | solution.py:32
  89.9 13.6 %collective-permute-start.21 = (bf16[256,384]{1,0:T(8,128)(2,1)S(1)}, bf16[256,384]{1,0:T(8,128)(2,1)S(1)}, u32[]{:S(2)}, u32[]{:S(2)}) collective-permute-start(bf16[256,384]{1,0:T(8,128)(2,1)S(1)} %get-tuple-element.71), channel_id=1, source_target_pairs={{0,4},{2,6},{4,0},{6,2},{1,5},{3,7},{5,1},{7,3},{8,12},{10,14},{12... | collective-permute-start | bytes 589832 | tf_op jit(solution)/shard_map/reduce_z/ppermute | solution.py:32
  91.5 11.9 %collective-permute-start.23 = (bf16[256,384]{1,0:T(8,128)(2,1)S(1)}, bf16[256,384]{1,0:T(8,128)(2,1)S(1)}, u32[]{:S(2)}, u32[]{:S(2)}) collective-permute-start(bf16[256,384]{1,0:T(8,128)(2,1)S(1)} %get-tuple-element.72), channel_id=1, source_target_pairs={{0,6},{2,0},{4,2},{6,4},{1,7},{3,1},{5,3},{7,5},{8,14},{10,8},{12,... | collective-permute-start | bytes 589832 | tf_op jit(solution)/shard_map/reduce_z/ppermute | solution.py:32
  103.9 12.6 %collective-permute-start.26 = (bf16[256,384]{1,0:T(8,128)(2,1)S(1)}, bf16[256,384]{1,0:T(8,128)(2,1)S(1)}, u32[]{:S(2)}, u32[]{:S(2)}) collective-permute-start(bf16[256,384]{1,0:T(8,128)(2,1)S(1)} %get-tuple-element.55), channel_id=1, source_target_pairs={{0,2},{2,4},{4,6},{6,0},{1,3},{3,5},{5,7},{7,1},{8,10},{10,12},{12... | collective-permute-start | bytes 589832 | tf_op jit(solution)/shard_map/gather_z/ppermute | solution.py:32
  104.0 14.2 %collective-permute-start.25 = (bf16[256,384]{1,0:T(8,128)(2,1)S(1)}, bf16[256,384]{1,0:T(8,128)(2,1)S(1)}, u32[]{:S(2)}, u32[]{:S(2)}) collective-permute-start(bf16[256,384]{1,0:T(8,128)(2,1)S(1)} %get-tuple-element.55), channel_id=1, source_target_pairs={{0,4},{2,6},{4,0},{6,2},{1,5},{3,7},{5,1},{7,3},{8,12},{10,14},{12... | collective-permute-start | bytes 589832 | tf_op jit(solution)/shard_map/gather_z/ppermute | solution.py:32
  107.8 10.4 %collective-permute-start.24 = (bf16[256,384]{1,0:T(8,128)(2,1)S(1)}, bf16[256,384]{1,0:T(8,128)(2,1)S(1)}, u32[]{:S(2)}, u32[]{:S(2)}) collective-permute-start(bf16[256,384]{1,0:T(8,128)(2,1)S(1)} %get-tuple-element.55), channel_id=1, source_target_pairs={{0,6},{2,0},{4,2},{6,4},{1,7},{3,1},{5,3},{7,5},{8,14},{10,8},{12,... | collective-permute-start | bytes 589832 | tf_op jit(solution)/shard_map/gather_z/ppermute | solution.py:32
  111.5 14.8 %collective-permute-start.45 = (bf16[256,384]{1,0:T(8,128)(2,1)S(1)}, bf16[256,384]{1,0:T(8,128)(2,1)S(1)}, u32[]{:S(2)}, u32[]{:S(2)}) collective-permute-start(bf16[256,384]{1,0:T(8,128)(2,1)S(1)} %get-tuple-element.57), channel_id=1, source_target_pairs={{0,2},{2,4},{4,6},{6,0},{1,3},{3,5},{5,7},{7,1},{8,10},{10,12},{12... | collective-permute-start | bytes 589832 | tf_op jit(solution)/shard_map/gather_z/ppermute | solution.py:32
  111.6 14.8 %collective-permute-start.44 = (bf16[256,384]{1,0:T(8,128)(2,1)S(1)}, bf16[256,384]{1,0:T(8,128)(2,1)S(1)}, u32[]{:S(2)}, u32[]{:S(2)}) collective-permute-start(bf16[256,384]{1,0:T(8,128)(2,1)S(1)} %get-tuple-element.57), channel_id=1, source_target_pairs={{0,4},{2,6},{4,0},{6,2},{1,5},{3,7},{5,1},{7,3},{8,12},{10,14},{12... | collective-permute-start | bytes 589832 | tf_op jit(solution)/shard_map/gather_z/ppermute | solution.py:32
  133.4 10.0 %collective-permute-start.48 = (bf16[64,1536]{1,0:T(8,128)(2,1)S(1)}, bf16[64,1536]{1,0:T(8,128)(2,1)S(1)}, u32[]{:S(2)}, u32[]{:S(2)}) collective-permute-start(bf16[64,1536]{1,0:T(8,128)(2,1)S(1)} %get-tuple-element.75), channel_id=1, source_target_pairs={{0,17},{16,0},{1,16},{17,1},{2,19},{18,2},{3,18},{19,3},{4,21},{20... | collective-permute-start | bytes 589832 | tf_op jit(solution)/shard_map/reduce_x/ppermute | solution.py:32
  134.9 11.4 %collective-permute-start.32 = (bf16[64,1536]{1,0:T(8,128)(2,1)S(1)}, bf16[64,1536]{1,0:T(8,128)(2,1)S(1)}, u32[]{:S(2)}, u32[]{:S(2)}) collective-permute-start(bf16[64,1536]{1,0:T(8,128)(2,1)S(1)} %add_convert_fusion.2), channel_id=1, source_target_pairs={{0,32},{32,64},{64,96},{96,0},{1,33},{33,65},{65,97},{97,1},{2,34}... | collective-permute-start | bytes 589832 | tf_op jit(solution)/shard_map/gather_y/ppermute | solution.py:32
  143.5 13.7 %collective-permute-start.51 = (bf16[64,1536]{1,0:T(8,128)(2,1)S(1)}, bf16[64,1536]{1,0:T(8,128)(2,1)S(1)}, u32[]{:S(2)}, u32[]{:S(2)}) collective-permute-start(bf16[64,1536]{1,0:T(8,128)(2,1)S(1)} %add_convert_fusion), channel_id=1, source_target_pairs={{0,32},{32,64},{64,96},{96,0},{1,33},{33,65},{65,97},{97,1},{2,34}... | collective-permute-start | bytes 589832 | tf_op jit(solution)/shard_map/gather_y/ppermute | solution.py:32
  143.6 13.6 %collective-permute-start.50 = (bf16[64,1536]{1,0:T(8,128)(2,1)S(1)}, bf16[64,1536]{1,0:T(8,128)(2,1)S(1)}, u32[]{:S(2)}, u32[]{:S(2)}) collective-permute-start(bf16[64,1536]{1,0:T(8,128)(2,1)S(1)} %add_convert_fusion), channel_id=1, source_target_pairs={{0,64},{32,96},{64,0},{96,32},{1,65},{33,97},{65,1},{97,33},{2,66}... | collective-permute-start | bytes 589832 | tf_op jit(solution)/shard_map/gather_y/ppermute | solution.py:32
  146.2 11.0 %collective-permute-start.49 = (bf16[64,1536]{1,0:T(8,128)(2,1)S(1)}, bf16[64,1536]{1,0:T(8,128)(2,1)S(1)}, u32[]{:S(2)}, u32[]{:S(2)}) collective-permute-start(bf16[64,1536]{1,0:T(8,128)(2,1)S(1)} %add_convert_fusion), channel_id=1, source_target_pairs={{0,96},{32,0},{64,32},{96,64},{1,97},{33,1},{65,33},{97,65},{2,98}... | collective-permute-start | bytes 589832 | tf_op jit(solution)/shard_map/gather_y/ppermute | solution.py:32
  146.3 15.2 %collective-permute-start.33 = (bf16[256,1536]{1,0:T(8,128)(2,1)S(1)}, bf16[256,1536]{1,0:T(8,128)(2,1)S(1)}, u32[]{:S(2)}, u32[]{:S(2)}) collective-permute-start(bf16[256,1536]{1,0:T(8,128)(2,1)S(1)} %pad_maximum_fusion.9), channel_id=1, source_target_pairs={{0,8},{8,0},{1,9},{9,1},{2,10},{10,2},{3,11},{11,3},{4,12},{12,4},... | collective-permute-start | bytes 2359304 | tf_op jit(solution)/shard_map/ppermute | solution.py:36
  165.7 12.0 %collective-permute-start.53 = (bf16[256,768]{1,0:T(8,128)(2,1)S(1)}, bf16[256,768]{1,0:T(8,128)(2,1)S(1)}, u32[]{:S(2)}, u32[]{:S(2)}) collective-permute-start(bf16[256,768]{1,0:T(8,128)(2,1)S(1)} %get-tuple-element.37), channel_id=1, source_target_pairs={{0,1},{16,17},{1,0},{17,16},{2,3},{18,19},{3,2},{19,18},{4,5},{20,... | collective-permute-start | bytes 1179656 | tf_op jit(solution)/shard_map/reduce_x/ppermute | solution.py:32
  167.1 19.6 %collective-permute-start.54 = (bf16[256,768]{1,0:T(8,128)(2,1)S(1)}, bf16[256,768]{1,0:T(8,128)(2,1)S(1)}, u32[]{:S(2)}, u32[]{:S(2)}) collective-permute-start(bf16[256,768]{1,0:T(8,128)(2,1)S(1)} %get-tuple-element.38), channel_id=1, source_target_pairs={{0,16},{16,1},{1,17},{17,0},{2,18},{18,3},{3,19},{19,2},{4,20},{20... | collective-permute-start | bytes 1179656 | tf_op jit(solution)/shard_map/reduce_x/ppermute | solution.py:32
  167.5 19.2 %collective-permute-start.55 = (bf16[256,768]{1,0:T(8,128)(2,1)S(1)}, bf16[256,768]{1,0:T(8,128)(2,1)S(1)}, u32[]{:S(2)}, u32[]{:S(2)}) collective-permute-start(bf16[256,768]{1,0:T(8,128)(2,1)S(1)} %get-tuple-element.39), channel_id=1, source_target_pairs={{0,17},{16,0},{1,16},{17,1},{2,19},{18,2},{3,18},{19,3},{4,21},{20... | collective-permute-start | bytes 1179656 | tf_op jit(solution)/shard_map/reduce_x/ppermute | solution.py:32
  (36 other events, 287.8 us)

commit v5 on v4

--- a/solution.py
+++ b/solution.py
@@ -122,7 +122,6 @@
         (grad_low, grad_near, left_part, left_near)
     )
     grad_far, left_far = far(grad_low, "x"), far(left_part, "z")
-    right_far = far(after(right_part, right_near), "y")
     pair = jnp.concatenate([exp_avg, exp_avg_sq], axis=0)
     entering = swap(after(columns_of(pair, 1 - xl), grad_far), "xl")
 
@@ -175,6 +174,8 @@
         now = slice(h * 4 * ROWS, (h + 1) * 4 * ROWS)
         part = dot(left_own[:, now], grad_own, 0, 0) + dot(left_swapped[:, now], grad_other, 0, 0)
         part = part.astype(low)
+        if h == 0:
+            right_far = far(after(right_part, (right_near, part)), "y")
         parts = [part[d * ROWS : (d + 1) * ROWS] for d in range(4)]
         left_lows.append(reduce(parts, "y").astype(low))
     right_far, entering = after((right_far, entering), left_lows[0])

time: 189 us -> 196 us (1.037)
  waiting for transfers between devices: 61.7 us -> 80.6 us
  starting transfers between devices: 90.2 us -> 83.8 us
  other arithmetic: 13.6 us -> 8.03 us
    ppermute x48, waiting for transfers between devices: 49.7 us -> 69.7 us  [shift(): lax.ppermute(value, names, [(place[i], place[(i + by) % 4]) for i in rang...]
    ppermute x48, starting transfers between devices: 65.6 us -> 56.9 us  [shift(): lax.ppermute(value, names, [(place[i], place[(i + by) % 4]) for i in rang...]
    select_n x12, other arithmetic: 7.85 us -> 2.24 us  [pick(): return lax.select(jnp.broadcast_to(test, first.shape), first, second)]
    ppermute x8, starting transfers between devices: 19.9 us -> 22.2 us  [swap(): return lax.ppermute(value, axis, [(0, 1), (1, 0)])]
  transfers between devices with their start and end apart: 57 -> 57, of which waited for: 25 -> 23; matrix products, arithmetic and copies ran while one was open for 17% -> 14% of each run, Pallas kernels for 0% -> 0%
where the time goes in v5:
time: 196 us
  starting transfers between devices  83.8 us (43%)
  waiting for transfers between devices  80.6 us (41%)
  matrix products  17.8 us (9%)
  other arithmetic  8.03 us (4%)
  local copies, waits for them, and re-layouts  4.2 us (2%)
    ppermute x48, waiting for transfers between devices, shift(): lax.ppermute(value, names, [(place[i], place[(i + by) % 4]) for i in rang...  69.7 us
    ppermute x48, starting transfers between devices, shift(): lax.ppermute(value, names, [(place[i], place[(i + by) % 4]) for i in rang...  56.9 us
    ppermute x8, starting transfers between devices, swap(): return lax.ppermute(value, axis, [(0, 1), (1, 0)])  22.2 us
    dot_general x16, matrix products, dot(): lax.dot_general(left, right, (((left_dim,), (right_dim,)), ((), ())), pre...  17.8 us
    ppermute x8, waiting for transfers between devices, swap(): return lax.ppermute(value, axis, [(0, 1), (1, 0)])  10.9 us
    ppermute x1, starting transfers between devices, move(): return lax.ppermute(value, AXES, pairs)  4.64 us
  transfers between devices with their start and end apart: 57, of which 23 were waited for; matrix products, arithmetic and copies ran while one was open for 14% of the time, Pallas kernels for 0%

profile of v5, /device:TPU:1, one launch (start us, length us, event | category | flops | bytes accessed | tf_op | source)
XLA Modules:
  0.0 195.8 jit_solution(17331191292923666737)
XLA Ops:
  0.7 4.6 %collective-permute-start.1 = (bf16[768,384]{1,0:T(8,128)(2,1)}, bf16[768,384]{1,0:T(8,128)(2,1)S(1)}, u32[]{:S(2)}, u32[]{:S(2)}) collective-permute-start(bf16[768,384]{1,0:T(8,128)(2,1)} %param.11), channel_id=1, source_target_pairs={{0,0},{1,8},{2,2},{3,10},{4,4},{5,12},{6,6},{7,14},{8,16},{9,24},{... | collective-permute-start | bytes 1769480 | tf_op jit(solution)/shard_map/ppermute | solution.py:44
  6.4 1.9 collective-permute-start
  8.5 8.9 %collective-permute-done = bf16[256,256]{0,1:T(8,128)(2,1)S(1)} collective-permute-done((bf16[256,256]{0,1:T(8,128)(2,1)S(1)}, bf16[256,256]{0,1:T(8,128)(2,1)S(1)}, u32[]{:S(2)}, u32[]{:S(2)}) %collective-permute-start) | collective-permute-done | bytes 131104 | tf_op jit(solution)/shard_map/ppermute | solution.py:36
  17.5 2.7 %collective-permute-start.2 = (bf16[256,768]{1,0:T(8,128)(2,1)S(1)}, bf16[256,768]{1,0:T(8,128)(2,1)S(1)}, u32[]{:S(2)}, u32[]{:S(2)}) collective-permute-start(bf16[256,768]{1,0:T(8,128)(2,1)S(1)} %convert_element_type.139), channel_id=1, source_target_pairs={{0,17},{16,0},{1,16},{17,1},{2,19},{18,2},{3,18},{19,3},{4,21},{20... | collective-permute-start | bytes 1179656 | tf_op jit(solution)/shard_map/gather_x/ppermute | solution.py:32
  22.0 2.2 %collective-permute-start.4 = (bf16[512,256]{0,1:T(8,128)(2,1)S(1)}, bf16[512,256]{0,1:T(8,128)(2,1)S(1)}, u32[]{:S(2)}, u32[]{:S(2)}) collective-permute-start(bf16[512,256]{0,1:T(8,128)(2,1)S(1)} %pad_maximum_fusion.14), channel_id=1, source_target_pairs={{0,6},{2,0},{4,2},{6,4},{1,7},{3,1},{5,3},{7,5},{8,14},{10,8},{12,... | collective-permute-start | bytes 786440 | tf_op jit(solution)/shard_map/gather_z/ppermute | solution.py:32
  26.4 3.9 %collective-permute-done.5 = bf16[512,256]{0,1:T(8,128)(2,1)S(1)} collective-permute-done((bf16[512,256]{0,1:T(8,128)(2,1)S(1)}, bf16[512,256]{0,1:T(8,128)(2,1)S(1)}, u32[]{:S(2)}, u32[]{:S(2)}) %collective-permute-start.5) | collective-permute-done | bytes 262176 | tf_op jit(solution)/shard_map/gather_z/ppermute | solution.py:32
  30.3 2.5 %collective-permute-start.7 = (bf16[768,384]{1,0:T(8,128)(2,1)S(1)}, bf16[768,384]{1,0:T(8,128)(2,1)S(1)}, u32[]{:S(2)}, u32[]{:S(2)}) collective-permute-start(bf16[768,384]{1,0:T(8,128)(2,1)S(1)} %collective-permute-done.1), channel_id=1, source_target_pairs={{0,96},{32,0},{64,32},{96,64},{1,97},{33,1},{65,33},{97,65},{2,98}... | collective-permute-start | bytes 1769480 | tf_op jit(solution)/shard_map/gather_y/ppermute | solution.py:32
  32.8 1.9 collective-permute-start.6
  34.8 7.1 %collective-permute-done.6 = bf16[512,256]{0,1:T(8,128)(2,1)S(1)} collective-permute-done((bf16[512,256]{0,1:T(8,128)(2,1)S(1)}, bf16[512,256]{0,1:T(8,128)(2,1)S(1)}, u32[]{:S(2)}, u32[]{:S(2)}) %collective-permute-start.6) | collective-permute-done | bytes 262176 | tf_op jit(solution)/shard_map/gather_z/ppermute | solution.py:32
  42.1 4.1 %collective-permute-done.9 = bf16[256,768]{1,0:T(8,128)(2,1)S(1)} collective-permute-done((bf16[256,768]{1,0:T(8,128)(2,1)S(1)}, bf16[256,768]{1,0:T(8,128)(2,1)S(1)}, u32[]{:S(2)}, u32[]{:S(2)}) %collective-permute-start.9) | collective-permute-done | bytes 393248 | tf_op jit(solution)/shard_map/gather_x/ppermute | solution.py:32
  63.8 3.7 %collective-permute-start.36 = (bf16[64,1536]{1,0:T(8,128)(2,1)}, bf16[64,1536]{1,0:T(8,128)(2,1)}, u32[]{:S(2)}, u32[]{:S(2)}) collective-permute-start(bf16[64,1536]{1,0:T(8,128)(2,1)} %get-tuple-element.81), channel_id=1, source_target_pairs={{0,96},{32,0},{64,32},{96,64},{1,97},{33,1},{65,33},{97,65},{2,98}... | collective-permute-start | bytes 589832 | tf_op jit(solution)/shard_map/reduce_y/ppermute | solution.py:32
  68.5 8.8 %collective-permute-done.12 = bf16[768,384]{1,0:T(8,128)(2,1)S(1)} collective-permute-done((bf16[768,384]{1,0:T(8,128)(2,1)S(1)}, bf16[768,384]{1,0:T(8,128)(2,1)S(1)}, u32[]{:S(2)}, u32[]{:S(2)}) %collective-permute-start.12) | collective-permute-done | bytes 589856 | tf_op jit(solution)/shard_map/gather_y/ppermute | solution.py:32
  77.8 2.1 %collective-permute-start.20 = (bf16[768,1536]{1,0:T(8,128)(2,1)S(1)}, bf16[768,1536]{1,0:T(8,128)(2,1)}, u32[]{:S(2)}, u32[]{:S(2)}) collective-permute-start(bf16[768,1536]{1,0:T(8,128)(2,1)S(1)} %pad_maximum_fusion), channel_id=1, source_target_pairs={{0,8},{8,0},{1,9},{9,1},{2,10},{10,2},{3,11},{11,3},{4,12},{12,4},... | collective-permute-start | bytes 7077896 | tf_op jit(solution)/shard_map/ppermute | solution.py:36
  81.9 3.1 %collective-permute-done.36 = bf16[64,1536]{1,0:T(8,128)(2,1)} collective-permute-done((bf16[64,1536]{1,0:T(8,128)(2,1)}, bf16[64,1536]{1,0:T(8,128)(2,1)}, u32[]{:S(2)}, u32[]{:S(2)}) %collective-permute-start.36) | collective-permute-done | bytes 196640 | tf_op jit(solution)/shard_map/reduce_y/ppermute | solution.py:32
  88.3 3.2 %collective-permute-done.19 = bf16[64,1536]{1,0:T(8,128)(2,1)S(1)} collective-permute-done((bf16[64,1536]{1,0:T(8,128)(2,1)S(1)}, bf16[64,1536]{1,0:T(8,128)(2,1)S(1)}, u32[]{:S(2)}, u32[]{:S(2)}) %collective-permute-start.19) | collective-permute-done | bytes 196640 | tf_op jit(solution)/shard_map/gather_x/ppermute | solution.py:32
  92.3 2.4 %fusion.29 = f32[256,1536]{1,0:T(8,128)S(1)} fusion(bf16[768,1536]{1,0:T(8,128)(2,1)} %collective-permute-done.20, bf16[256,1536]{1,0:T(8,128)(2,1)S(1)} %pad_maximum_fusion.7), kind=kOutput, calls=%fused_computation.81 | convolution fusion | flops 603979776 | bytes 4325376 | tf_op jit(solution)/shard_map/dot_general | solution.py:25
  97.4 2.9 %collective-permute-start.23 = (bf16[256,384]{1,0:T(8,128)(2,1)S(1)}, bf16[256,384]{1,0:T(8,128)(2,1)S(1)}, u32[]{:S(2)}, u32[]{:S(2)}) collective-permute-start(bf16[256,384]{1,0:T(8,128)(2,1)S(1)} %get-tuple-element.72), channel_id=1, source_target_pairs={{0,6},{2,0},{4,2},{6,4},{1,7},{3,1},{5,3},{7,5},{8,14},{10,8},{12,... | collective-permute-start | bytes 589832 | tf_op jit(solution)/shard_map/reduce_z/ppermute | solution.py:32
  101.8 2.4 %fusion.26 = f32[256,1536]{1,0:T(8,128)S(1)} fusion(bf16[768,1536]{1,0:T(8,128)(2,1)} %collective-permute-done.20, bf16[256,1536]{1,0:T(8,128)(2,1)S(1)} %pad_maximum_fusion.10), kind=kOutput, calls=%fused_computation.78 | convolution fusion | flops 603979776 | bytes 4325376 | tf_op jit(solution)/shard_map/dot_general | solution.py:25
  109.0 3.4 %collective-permute-start.25 = (bf16[256,384]{1,0:T(8,128)(2,1)S(1)}, bf16[256,384]{1,0:T(8,128)(2,1)S(1)}, u32[]{:S(2)}, u32[]{:S(2)}) collective-permute-start(bf16[256,384]{1,0:T(8,128)(2,1)S(1)} %get-tuple-element.55), channel_id=1, source_target_pairs={{0,4},{2,6},{4,0},{6,2},{1,5},{3,7},{5,1},{7,3},{8,12},{10,14},{12... | collective-permute-start | bytes 589832 | tf_op jit(solution)/shard_map/gather_z/ppermute | solution.py:32
  112.6 5.7 %collective-permute-done.41 = bf16[256,384]{1,0:T(8,128)(2,1)S(1)} collective-permute-done((bf16[256,384]{1,0:T(8,128)(2,1)S(1)}, bf16[256,384]{1,0:T(8,128)(2,1)S(1)}, u32[]{:S(2)}, u32[]{:S(2)}) %collective-permute-start.41) | collective-permute-done | bytes 196640 | tf_op jit(solution)/shard_map/reduce_z/ppermute | solution.py:32
  119.0 5.6 %collective-permute-done.26 = bf16[256,384]{1,0:T(8,128)(2,1)S(1)} collective-permute-done((bf16[256,384]{1,0:T(8,128)(2,1)S(1)}, bf16[256,384]{1,0:T(8,128)(2,1)S(1)}, u32[]{:S(2)}, u32[]{:S(2)}) %collective-permute-start.26) | collective-permute-done | bytes 196640 | tf_op jit(solution)/shard_map/gather_z/ppermute | solution.py:32
  124.6 2.5 %convolution_convert_fusion.2 = bf16[256,768]{1,0:T(8,128)(2,1)S(1)} fusion(bf16[768,1536]{1,0:T(8,128)(2,1)} %collective-permute-done.20, bf16[256,384]{1,0:T(8,128)(2,1)S(1)} %collective-permute-done.26, bf16[256,384]{1,0:T(8,128)(2,1)S(1)} %collective-permute-done.25, bf16[256,384]{1,0:T(8,128)(2,1)S(1)} %collective-permute-done.24, ...), kind=kOutput, calls=%fused_computation.17 | convolution fusion | flops 607322112 | bytes 3538944 | tf_op jit(solution)/shard_map/dot_general | solution.py:25
  128.1 3.9 %collective-permute-start.29 = (bf16[64,1536]{1,0:T(8,128)(2,1)S(1)}, bf16[64,1536]{1,0:T(8,128)(2,1)S(1)}, u32[]{:S(2)}, u32[]{:S(2)}) collective-permute-start(bf16[64,1536]{1,0:T(8,128)(2,1)S(1)} %get-tuple-element.69), channel_id=1, source_target_pairs={{0,17},{16,0},{1,16},{17,1},{2,19},{18,2},{3,18},{19,3},{4,21},{20... | collective-permute-start | bytes 589832 | tf_op jit(solution)/shard_map/reduce_x/ppermute | solution.py:32
  134.0 2.5 %convolution_convert_fusion = bf16[256,768]{1,0:T(8,128)(2,1)S(1)} fusion(bf16[768,1536]{1,0:T(8,128)(2,1)} %collective-permute-done.20, bf16[256,384]{1,0:T(8,128)(2,1)S(1)} %collective-permute-done.45, bf16[256,384]{1,0:T(8,128)(2,1)S(1)} %collective-permute-done.44, bf16[256,384]{1,0:T(8,128)(2,1)S(1)} %collective-permute-done.43, ...), kind=kOutput, calls=%fused_computation.15 | convolution fusion | flops 607322112 | bytes 3538944 | tf_op jit(solution)/shard_map/dot_general | solution.py:25
  137.4 3.6 %collective-permute-done.28 = bf16[64,1536]{1,0:T(8,128)(2,1)S(1)} collective-permute-done((bf16[64,1536]{1,0:T(8,128)(2,1)S(1)}, bf16[64,1536]{1,0:T(8,128)(2,1)S(1)}, u32[]{:S(2)}, u32[]{:S(2)}) %collective-permute-start.28) | collective-permute-done | bytes 196640 | tf_op jit(solution)/shard_map/reduce_x/ppermute | solution.py:32
  143.4 2.7 %collective-permute-start.31 = (bf16[64,1536]{1,0:T(8,128)(2,1)S(1)}, bf16[64,1536]{1,0:T(8,128)(2,1)S(1)}, u32[]{:S(2)}, u32[]{:S(2)}) collective-permute-start(bf16[64,1536]{1,0:T(8,128)(2,1)S(1)} %add_convert_fusion.2), channel_id=1, source_target_pairs={{0,64},{32,96},{64,0},{96,32},{1,65},{33,97},{65,1},{97,33},{2,66}... | collective-permute-start | bytes 589832 | tf_op jit(solution)/shard_map/gather_y/ppermute | solution.py:32
  149.7 2.6 %collective-permute-start.50 = (bf16[64,1536]{1,0:T(8,128)(2,1)S(1)}, bf16[64,1536]{1,0:T(8,128)(2,1)S(1)}, u32[]{:S(2)}, u32[]{:S(2)}) collective-permute-start(bf16[64,1536]{1,0:T(8,128)(2,1)S(1)} %add_convert_fusion), channel_id=1, source_target_pairs={{0,64},{32,96},{64,0},{96,32},{1,65},{33,97},{65,1},{97,33},{2,66}... | collective-permute-start | bytes 589832 | tf_op jit(solution)/shard_map/gather_y/ppermute | solution.py:32
  153.7 11.1 %collective-permute-start.33 = (bf16[256,1536]{1,0:T(8,128)(2,1)S(1)}, bf16[256,1536]{1,0:T(8,128)(2,1)S(1)}, u32[]{:S(2)}, u32[]{:S(2)}) collective-permute-start(bf16[256,1536]{1,0:T(8,128)(2,1)S(1)} %pad_maximum_fusion.9), channel_id=1, source_target_pairs={{0,8},{8,0},{1,9},{9,1},{2,10},{10,2},{3,11},{11,3},{4,12},{12,4},... | collective-permute-start | bytes 2359304 | tf_op jit(solution)/shard_map/ppermute | solution.py:36
  165.0 3.6 %collective-permute-start.52 = (bf16[256,1536]{1,0:T(8,128)(2,1)S(1)}, bf16[256,1536]{1,0:T(8,128)(2,1)S(1)}, u32[]{:S(2)}, u32[]{:S(2)}) collective-permute-start(bf16[256,1536]{1,0:T(8,128)(2,1)S(1)} %pad_maximum_fusion.12), channel_id=1, source_target_pairs={{0,8},{8,0},{1,9},{9,1},{2,10},{10,2},{3,11},{11,3},{4,12},{12,4},... | collective-permute-start | bytes 2359304 | tf_op jit(solution)/shard_map/ppermute | solution.py:36
  175.8 2.2 %collective-permute-start.55 = (bf16[256,768]{1,0:T(8,128)(2,1)S(1)}, bf16[256,768]{1,0:T(8,128)(2,1)S(1)}, u32[]{:S(2)}, u32[]{:S(2)}) collective-permute-start(bf16[256,768]{1,0:T(8,128)(2,1)S(1)} %get-tuple-element.39), channel_id=1, source_target_pairs={{0,17},{16,0},{1,16},{17,1},{2,19},{18,2},{3,18},{19,3},{4,21},{20... | collective-permute-start | bytes 1179656 | tf_op jit(solution)/shard_map/reduce_x/ppermute | solution.py:32
  179.6 6.0 %collective-permute-done.53 = bf16[256,768]{1,0:T(8,128)(2,1)S(1)} collective-permute-done((bf16[256,768]{1,0:T(8,128)(2,1)S(1)}, bf16[256,768]{1,0:T(8,128)(2,1)S(1)}, u32[]{:S(2)}, u32[]{:S(2)}) %collective-permute-start.53) | collective-permute-done | bytes 393248 | tf_op jit(solution)/shard_map/reduce_x/ppermute | solution.py:32
  185.5 9.0 %collective-permute-done.54 = bf16[256,768]{1,0:T(8,128)(2,1)S(1)} collective-permute-done((bf16[256,768]{1,0:T(8,128)(2,1)S(1)}, bf16[256,768]{1,0:T(8,128)(2,1)S(1)}, u32[]{:S(2)}, u32[]{:S(2)}) %collective-permute-start.54) | collective-permute-done | bytes 393248 | tf_op jit(solution)/shard_map/reduce_x/ppermute | solution.py:32
  (180 shorter events, 61.6 us)
Async XLA Ops:
  0.7 16.8 %collective-permute-start.1 = (bf16[768,384]{1,0:T(8,128)(2,1)}, bf16[768,384]{1,0:T(8,128)(2,1)S(1)}, u32[]{:S(2)}, u32[]{:S(2)}) collective-permute-start(bf16[768,384]{1,0:T(8,128)(2,1)} %param.11), channel_id=1, source_target_pairs={{0,0},{1,8},{2,2},{3,10},{4,4},{5,12},{6,6},{7,14},{8,16},{9,24},{... | collective-permute-start | bytes 1769480 | tf_op jit(solution)/shard_map/ppermute | solution.py:44
  6.4 11.0 %collective-permute-start = (bf16[256,256]{0,1:T(8,128)(2,1)S(1)}, bf16[256,256]{0,1:T(8,128)(2,1)S(1)}, u32[]{:S(2)}, u32[]{:S(2)}) collective-permute-start(bf16[256,256]{0,1:T(8,128)(2,1)S(1)} %bitcast.13), channel_id=1, source_target_pairs={{0,16},{16,0},{1,17},{17,1},{2,18},{18,2},{3,19},{19,3},{4,20},{20... | collective-permute-start | bytes 393224 | tf_op jit(solution)/shard_map/ppermute | solution.py:36
  17.4 15.3 %collective-permute-start.3 = (bf16[256,768]{1,0:T(8,128)(2,1)S(1)}, bf16[256,768]{1,0:T(8,128)(2,1)S(1)}, u32[]{:S(2)}, u32[]{:S(2)}) collective-permute-start(bf16[256,768]{1,0:T(8,128)(2,1)S(1)} %convert_element_type.139), channel_id=1, source_target_pairs={{0,16},{16,1},{1,17},{17,0},{2,18},{18,3},{3,19},{19,2},{4,20},{20... | collective-permute-start | bytes 1179656 | tf_op jit(solution)/shard_map/gather_x/ppermute | solution.py:32
  17.5 15.3 %collective-permute-start.2 = (bf16[256,768]{1,0:T(8,128)(2,1)S(1)}, bf16[256,768]{1,0:T(8,128)(2,1)S(1)}, u32[]{:S(2)}, u32[]{:S(2)}) collective-permute-start(bf16[256,768]{1,0:T(8,128)(2,1)S(1)} %convert_element_type.139), channel_id=1, source_target_pairs={{0,17},{16,0},{1,16},{17,1},{2,19},{18,2},{3,18},{19,3},{4,21},{20... | collective-permute-start | bytes 1179656 | tf_op jit(solution)/shard_map/gather_x/ppermute | solution.py:32
  22.0 10.8 %collective-permute-start.4 = (bf16[512,256]{0,1:T(8,128)(2,1)S(1)}, bf16[512,256]{0,1:T(8,128)(2,1)S(1)}, u32[]{:S(2)}, u32[]{:S(2)}) collective-permute-start(bf16[512,256]{0,1:T(8,128)(2,1)S(1)} %pad_maximum_fusion.14), channel_id=1, source_target_pairs={{0,6},{2,0},{4,2},{6,4},{1,7},{3,1},{5,3},{7,5},{8,14},{10,8},{12,... | collective-permute-start | bytes 786440 | tf_op jit(solution)/shard_map/gather_z/ppermute | solution.py:32
  25.1 27.5 %collective-permute-start.8 = (bf16[768,384]{1,0:T(8,128)(2,1)S(1)}, bf16[768,384]{1,0:T(8,128)(2,1)S(1)}, u32[]{:S(2)}, u32[]{:S(2)}) collective-permute-start(bf16[768,384]{1,0:T(8,128)(2,1)S(1)} %collective-permute-done.1), channel_id=1, source_target_pairs={{0,32},{32,64},{64,96},{96,0},{1,33},{33,65},{65,97},{97,1},{2,34}... | collective-permute-start | bytes 1769480 | tf_op jit(solution)/shard_map/gather_y/ppermute | solution.py:32
  30.3 22.4 %collective-permute-start.7 = (bf16[768,384]{1,0:T(8,128)(2,1)S(1)}, bf16[768,384]{1,0:T(8,128)(2,1)S(1)}, u32[]{:S(2)}, u32[]{:S(2)}) collective-permute-start(bf16[768,384]{1,0:T(8,128)(2,1)S(1)} %collective-permute-done.1), channel_id=1, source_target_pairs={{0,96},{32,0},{64,32},{96,64},{1,97},{33,1},{65,33},{97,65},{2,98}... | collective-permute-start | bytes 1769480 | tf_op jit(solution)/shard_map/gather_y/ppermute | solution.py:32
  34.7 11.4 %collective-permute-start.9 = (bf16[256,768]{1,0:T(8,128)(2,1)S(1)}, bf16[256,768]{1,0:T(8,128)(2,1)S(1)}, u32[]{:S(2)}, u32[]{:S(2)}) collective-permute-start(bf16[256,768]{1,0:T(8,128)(2,1)S(1)} %convert_element_type.139), channel_id=1, source_target_pairs={{0,1},{16,17},{1,0},{17,16},{2,3},{18,19},{3,2},{19,18},{4,5},{20,... | collective-permute-start | bytes 1179656 | tf_op jit(solution)/shard_map/gather_x/ppermute | solution.py:32
  48.5 19.1 %collective-permute-start.13 = (f32[512,384]{1,0:T(8,128)S(1)}, f32[512,384]{1,0:T(8,128)S(1)}, u32[]{:S(2)}, u32[]{:S(2)}) collective-permute-start(f32[512,384]{1,0:T(8,128)S(1)} %get-tuple-element.28), channel_id=1, source_target_pairs={{0,16},{16,0},{1,17},{17,1},{2,18},{18,2},{3,19},{19,3},{4,20},{20... | collective-permute-start | bytes 2359304 | tf_op jit(solution)/shard_map/ppermute | solution.py:36
  55.3 12.2 %collective-permute-start.15 = (bf16[64,1536]{1,0:T(8,128)(2,1)S(1)}, bf16[64,1536]{1,0:T(8,128)(2,1)S(1)}, u32[]{:S(2)}, u32[]{:S(2)}) collective-permute-start(bf16[64,1536]{1,0:T(8,128)(2,1)S(1)} %get-tuple-element.85), channel_id=1, source_target_pairs={{0,32},{32,64},{64,96},{96,0},{1,33},{33,65},{65,97},{97,1},{2,34}... | collective-permute-start | bytes 589832 | tf_op jit(solution)/shard_map/reduce_y/ppermute | solution.py:32
  56.0 21.3 %collective-permute-start.12 = (bf16[768,384]{1,0:T(8,128)(2,1)S(1)}, bf16[768,384]{1,0:T(8,128)(2,1)S(1)}, u32[]{:S(2)}, u32[]{:S(2)}) collective-permute-start(bf16[768,384]{1,0:T(8,128)(2,1)S(1)} %collective-permute-done.1), channel_id=1, source_target_pairs={{0,64},{32,96},{64,0},{96,32},{1,65},{33,97},{65,1},{97,33},{2,66}... | collective-permute-start | bytes 1769480 | tf_op jit(solution)/shard_map/gather_y/ppermute | solution.py:32
  60.4 21.2 %collective-permute-start.34 = (bf16[64,1536]{1,0:T(8,128)(2,1)}, bf16[64,1536]{1,0:T(8,128)(2,1)}, u32[]{:S(2)}, u32[]{:S(2)}) collective-permute-start(bf16[64,1536]{1,0:T(8,128)(2,1)} %get-tuple-element.80), channel_id=1, source_target_pairs={{0,64},{32,96},{64,0},{96,32},{1,65},{33,97},{65,1},{97,33},{2,66}... | collective-permute-start | bytes 589832 | tf_op jit(solution)/shard_map/reduce_y/ppermute | solution.py:32
  63.8 21.2 %collective-permute-start.36 = (bf16[64,1536]{1,0:T(8,128)(2,1)}, bf16[64,1536]{1,0:T(8,128)(2,1)}, u32[]{:S(2)}, u32[]{:S(2)}) collective-permute-start(bf16[64,1536]{1,0:T(8,128)(2,1)} %get-tuple-element.81), channel_id=1, source_target_pairs={{0,96},{32,0},{64,32},{96,64},{1,97},{33,1},{65,33},{97,65},{2,98}... | collective-permute-start | bytes 589832 | tf_op jit(solution)/shard_map/reduce_y/ppermute | solution.py:32
  67.5 19.2 %collective-permute-start.35 = (bf16[64,1536]{1,0:T(8,128)(2,1)S(1)}, bf16[64,1536]{1,0:T(8,128)(2,1)}, u32[]{:S(2)}, u32[]{:S(2)}) collective-permute-start(bf16[64,1536]{1,0:T(8,128)(2,1)S(1)} %get-tuple-element.82), channel_id=1, source_target_pairs={{0,32},{32,64},{64,96},{96,0},{1,33},{33,65},{65,97},{97,1},{2,34}... | collective-permute-start | bytes 589832 | tf_op jit(solution)/shard_map/reduce_y/ppermute | solution.py:32
  77.8 14.5 %collective-permute-start.20 = (bf16[768,1536]{1,0:T(8,128)(2,1)S(1)}, bf16[768,1536]{1,0:T(8,128)(2,1)}, u32[]{:S(2)}, u32[]{:S(2)}) collective-permute-start(bf16[768,1536]{1,0:T(8,128)(2,1)S(1)} %pad_maximum_fusion), channel_id=1, source_target_pairs={{0,8},{8,0},{1,9},{9,1},{2,10},{10,2},{3,11},{11,3},{4,12},{12,4},... | collective-permute-start | bytes 7077896 | tf_op jit(solution)/shard_map/ppermute | solution.py:36
  80.0 11.5 %collective-permute-start.19 = (bf16[64,1536]{1,0:T(8,128)(2,1)S(1)}, bf16[64,1536]{1,0:T(8,128)(2,1)S(1)}, u32[]{:S(2)}, u32[]{:S(2)}) collective-permute-start(bf16[64,1536]{1,0:T(8,128)(2,1)S(1)} %add_convert_fusion.3), channel_id=1, source_target_pairs={{0,16},{16,1},{1,17},{17,0},{2,18},{18,3},{3,19},{19,2},{4,20},{20... | collective-permute-start | bytes 589832 | tf_op jit(solution)/shard_map/gather_x/ppermute | solution.py:32
  88.0 12.3 %collective-permute-start.39 = (bf16[64,1536]{1,0:T(8,128)(2,1)S(1)}, bf16[64,1536]{1,0:T(8,128)(2,1)S(1)}, u32[]{:S(2)}, u32[]{:S(2)}) collective-permute-start(bf16[64,1536]{1,0:T(8,128)(2,1)S(1)} %add_convert_fusion.1), channel_id=1, source_target_pairs={{0,16},{16,1},{1,17},{17,0},{2,18},{18,3},{3,19},{19,2},{4,20},{20... | collective-permute-start | bytes 589832 | tf_op jit(solution)/shard_map/gather_x/ppermute | solution.py:32
  97.1 10.9 %collective-permute-start.21 = (bf16[256,384]{1,0:T(8,128)(2,1)S(1)}, bf16[256,384]{1,0:T(8,128)(2,1)S(1)}, u32[]{:S(2)}, u32[]{:S(2)}) collective-permute-start(bf16[256,384]{1,0:T(8,128)(2,1)S(1)} %get-tuple-element.71), channel_id=1, source_target_pairs={{0,4},{2,6},{4,0},{6,2},{1,5},{3,7},{5,1},{7,3},{8,12},{10,14},{12... | collective-permute-start | bytes 589832 | tf_op jit(solution)/shard_map/reduce_z/ppermute | solution.py:32
  97.4 10.6 %collective-permute-start.23 = (bf16[256,384]{1,0:T(8,128)(2,1)S(1)}, bf16[256,384]{1,0:T(8,128)(2,1)S(1)}, u32[]{:S(2)}, u32[]{:S(2)}) collective-permute-start(bf16[256,384]{1,0:T(8,128)(2,1)S(1)} %get-tuple-element.72), channel_id=1, source_target_pairs={{0,6},{2,0},{4,2},{6,4},{1,7},{3,1},{5,3},{7,5},{8,14},{10,8},{12,... | collective-permute-start | bytes 589832 | tf_op jit(solution)/shard_map/reduce_z/ppermute | solution.py:32
  108.5 16.1 %collective-permute-start.26 = (bf16[256,384]{1,0:T(8,128)(2,1)S(1)}, bf16[256,384]{1,0:T(8,128)(2,1)S(1)}, u32[]{:S(2)}, u32[]{:S(2)}) collective-permute-start(bf16[256,384]{1,0:T(8,128)(2,1)S(1)} %get-tuple-element.55), channel_id=1, source_target_pairs={{0,2},{2,4},{4,6},{6,0},{1,3},{3,5},{5,7},{7,1},{8,10},{10,12},{12... | collective-permute-start | bytes 589832 | tf_op jit(solution)/shard_map/gather_z/ppermute | solution.py:32
  109.0 15.6 %collective-permute-start.25 = (bf16[256,384]{1,0:T(8,128)(2,1)S(1)}, bf16[256,384]{1,0:T(8,128)(2,1)S(1)}, u32[]{:S(2)}, u32[]{:S(2)}) collective-permute-start(bf16[256,384]{1,0:T(8,128)(2,1)S(1)} %get-tuple-element.55), channel_id=1, source_target_pairs={{0,4},{2,6},{4,0},{6,2},{1,5},{3,7},{5,1},{7,3},{8,12},{10,14},{12... | collective-permute-start | bytes 589832 | tf_op jit(solution)/shard_map/gather_z/ppermute | solution.py:32
  112.3 12.2 %collective-permute-start.24 = (bf16[256,384]{1,0:T(8,128)(2,1)S(1)}, bf16[256,384]{1,0:T(8,128)(2,1)S(1)}, u32[]{:S(2)}, u32[]{:S(2)}) collective-permute-start(bf16[256,384]{1,0:T(8,128)(2,1)S(1)} %get-tuple-element.55), channel_id=1, source_target_pairs={{0,6},{2,0},{4,2},{6,4},{1,7},{3,1},{5,3},{7,5},{8,14},{10,8},{12,... | collective-permute-start | bytes 589832 | tf_op jit(solution)/shard_map/gather_z/ppermute | solution.py:32
  118.6 14.4 %collective-permute-start.45 = (bf16[256,384]{1,0:T(8,128)(2,1)S(1)}, bf16[256,384]{1,0:T(8,128)(2,1)S(1)}, u32[]{:S(2)}, u32[]{:S(2)}) collective-permute-start(bf16[256,384]{1,0:T(8,128)(2,1)S(1)} %get-tuple-element.57), channel_id=1, source_target_pairs={{0,2},{2,4},{4,6},{6,0},{1,3},{3,5},{5,7},{7,1},{8,10},{10,12},{12... | collective-permute-start | bytes 589832 | tf_op jit(solution)/shard_map/gather_z/ppermute | solution.py:32
  118.7 15.3 %collective-permute-start.44 = (bf16[256,384]{1,0:T(8,128)(2,1)S(1)}, bf16[256,384]{1,0:T(8,128)(2,1)S(1)}, u32[]{:S(2)}, u32[]{:S(2)}) collective-permute-start(bf16[256,384]{1,0:T(8,128)(2,1)S(1)} %get-tuple-element.57), channel_id=1, source_target_pairs={{0,4},{2,6},{4,0},{6,2},{1,5},{3,7},{5,1},{7,3},{8,12},{10,14},{12... | collective-permute-start | bytes 589832 | tf_op jit(solution)/shard_map/gather_z/ppermute | solution.py:32
  143.4 10.3 %collective-permute-start.31 = (bf16[64,1536]{1,0:T(8,128)(2,1)S(1)}, bf16[64,1536]{1,0:T(8,128)(2,1)S(1)}, u32[]{:S(2)}, u32[]{:S(2)}) collective-permute-start(bf16[64,1536]{1,0:T(8,128)(2,1)S(1)} %add_convert_fusion.2), channel_id=1, source_target_pairs={{0,64},{32,96},{64,0},{96,32},{1,65},{33,97},{65,1},{97,33},{2,66}... | collective-permute-start | bytes 589832 | tf_op jit(solution)/shard_map/gather_y/ppermute | solution.py:32
  149.4 15.4 %collective-permute-start.51 = (bf16[64,1536]{1,0:T(8,128)(2,1)S(1)}, bf16[64,1536]{1,0:T(8,128)(2,1)S(1)}, u32[]{:S(2)}, u32[]{:S(2)}) collective-permute-start(bf16[64,1536]{1,0:T(8,128)(2,1)S(1)} %add_convert_fusion), channel_id=1, source_target_pairs={{0,32},{32,64},{64,96},{96,0},{1,33},{33,65},{65,97},{97,1},{2,34}... | collective-permute-start | bytes 589832 | tf_op jit(solution)/shard_map/gather_y/ppermute | solution.py:32
  149.7 15.2 %collective-permute-start.50 = (bf16[64,1536]{1,0:T(8,128)(2,1)S(1)}, bf16[64,1536]{1,0:T(8,128)(2,1)S(1)}, u32[]{:S(2)}, u32[]{:S(2)}) collective-permute-start(bf16[64,1536]{1,0:T(8,128)(2,1)S(1)} %add_convert_fusion), channel_id=1, source_target_pairs={{0,64},{32,96},{64,0},{96,32},{1,65},{33,97},{65,1},{97,33},{2,66}... | collective-permute-start | bytes 589832 | tf_op jit(solution)/shard_map/gather_y/ppermute | solution.py:32
  152.3 12.6 %collective-permute-start.49 = (bf16[64,1536]{1,0:T(8,128)(2,1)S(1)}, bf16[64,1536]{1,0:T(8,128)(2,1)S(1)}, u32[]{:S(2)}, u32[]{:S(2)}) collective-permute-start(bf16[64,1536]{1,0:T(8,128)(2,1)S(1)} %add_convert_fusion), channel_id=1, source_target_pairs={{0,96},{32,0},{64,32},{96,64},{1,97},{33,1},{65,33},{97,65},{2,98}... | collective-permute-start | bytes 589832 | tf_op jit(solution)/shard_map/gather_y/ppermute | solution.py:32
  153.7 16.7 %collective-permute-start.33 = (bf16[256,1536]{1,0:T(8,128)(2,1)S(1)}, bf16[256,1536]{1,0:T(8,128)(2,1)S(1)}, u32[]{:S(2)}, u32[]{:S(2)}) collective-permute-start(bf16[256,1536]{1,0:T(8,128)(2,1)S(1)} %pad_maximum_fusion.9), channel_id=1, source_target_pairs={{0,8},{8,0},{1,9},{9,1},{2,10},{10,2},{3,11},{11,3},{4,12},{12,4},... | collective-permute-start | bytes 2359304 | tf_op jit(solution)/shard_map/ppermute | solution.py:36
  173.5 12.0 %collective-permute-start.53 = (bf16[256,768]{1,0:T(8,128)(2,1)S(1)}, bf16[256,768]{1,0:T(8,128)(2,1)S(1)}, u32[]{:S(2)}, u32[]{:S(2)}) collective-permute-start(bf16[256,768]{1,0:T(8,128)(2,1)S(1)} %get-tuple-element.37), channel_id=1, source_target_pairs={{0,1},{16,17},{1,0},{17,16},{2,3},{18,19},{3,2},{19,18},{4,5},{20,... | collective-permute-start | bytes 1179656 | tf_op jit(solution)/shard_map/reduce_x/ppermute | solution.py:32
  175.4 19.2 %collective-permute-start.54 = (bf16[256,768]{1,0:T(8,128)(2,1)S(1)}, bf16[256,768]{1,0:T(8,128)(2,1)S(1)}, u32[]{:S(2)}, u32[]{:S(2)}) collective-permute-start(bf16[256,768]{1,0:T(8,128)(2,1)S(1)} %get-tuple-element.38), channel_id=1, source_target_pairs={{0,16},{16,1},{1,17},{17,0},{2,18},{18,3},{3,19},{19,2},{4,20},{20... | collective-permute-start | bytes 1179656 | tf_op jit(solution)/shard_map/reduce_x/ppermute | solution.py:32
  175.8 18.7 %collective-permute-start.55 = (bf16[256,768]{1,0:T(8,128)(2,1)S(1)}, bf16[256,768]{1,0:T(8,128)(2,1)S(1)}, u32[]{:S(2)}, u32[]{:S(2)}) collective-permute-start(bf16[256,768]{1,0:T(8,128)(2,1)S(1)} %get-tuple-element.39), channel_id=1, source_target_pairs={{0,17},{16,0},{1,16},{17,1},{2,19},{18,2},{3,18},{19,3},{4,21},{20... | collective-permute-start | bytes 1179656 | tf_op jit(solution)/shard_map/reduce_x/ppermute | solution.py:32
  (38 other events, 288.3 us)
